TPU v7x, 512 devices: a whole 4x4x16 slice. The times are simulated.
512 devices in a mesh: gx: 16 (over z_hi, x, core), gy: 32 (over z_lo, y).
Axes of the slice: x: 4, y: 4, z: 16 (z_hi: 2, z_lo: 8; z = z_hi * 8 + z_lo), core: 2. Of those that a mesh axis runs over, the one named last changes fastest.
Arguments:
- p_now: float32 [18, 2048, 2048], P(None, 'gy', 'gx'), may hold values from -2 to 2
- p_prev: float32 [18, 2048, 2048], P(None, 'gy', 'gx'), may hold values from -2 to 2
- phase: int32 [18, 2048, 2048], P(None, 'gy', 'gx'), may hold values 0 or 1
- div_star: float32 [16, 2048, 2048], P(None, 'gy', 'gx'), may hold values from -6 to 6
Outputs:
- spectrum: float32 [2, 16, 32, 64, 16, 128], P(None, None, 'gy', None, 'gx')
Inputs may be any that keep to these rules, and one draw needn't show every extreme that they name: `phase`: 0 marks gas, 1 liquid.
All inputs are finite; a program needn't handle non-finite values. No bound on the sum of `phase` on one device may be relied on, other than what follows from the above.
Results may differ from a plain program's by a relative error of at most 0.000098.
Values sent between devices are 32-bit elements; how exact they have to be, the bound alone decides.
No kernel may reach another device: no remote copies, remote signals or barrier semaphores. Data moves between devices by JAX's collectives and lax.ppermute only.
A program may use at most 64 MiB of HBM per device.

v0:
```python
import math

import jax
import jax.numpy as jnp
import numpy as np
from jax import lax
from jax.sharding import PartitionSpec as P

NX = 2048
NY = 2048


RHO_GAS = 1.0
RHO_LIQUID = 8.0
SOURCE = 1.0


def with_halo(cells, sides, width):
    for axis, dim in sides:
        count = lax.axis_size(axis)
        head = lax.slice_in_dim(cells, 0, width, axis=dim)
        tail = lax.slice_in_dim(cells, cells.shape[dim] - width, cells.shape[dim], axis=dim)
        cells = jnp.concatenate(
            [
                lax.ppermute(tail, axis, [(i, (i + 1) % count) for i in range(count)]),
                cells,
                lax.ppermute(head, axis, [((i + 1) % count, i) for i in range(count)]),
            ],
            axis=dim,
        )
    return cells


def static_reversal(count):
    digits = count.bit_length() - 1
    table = []
    for counter in range(count):
        total = 0
        for place in range(digits):
            total = total * 2 + (counter >> place) % 2
        table.append(total)
    return np.array(table, dtype=np.int32)


def coefficient(first, second):
    return 1.0 - RHO_GAS / (0.5 * (first + second))


def phase_table(rows, cols, length):
    product = (
        jnp.arange(rows, dtype=jnp.int32)[:, None]
        * jnp.arange(cols, dtype=jnp.int32)[None, :]
        % length
    )
    angle = product.astype(jnp.float32) * (2.0 * math.pi / length)
    return (jnp.cos(angle), -jnp.sin(angle))


def complex_product(form, real, imag, cosine, sine):
    real_cos = jnp.einsum(form, real, cosine, precision=lax.Precision.HIGHEST)
    real_sin = jnp.einsum(form, real, sine, precision=lax.Precision.HIGHEST)
    if imag is None:
        return (real_cos, real_sin)
    imag_cos = jnp.einsum(form, imag, cosine, precision=lax.Precision.HIGHEST)
    imag_sin = jnp.einsum(form, imag, sine, precision=lax.Precision.HIGHEST)
    return (real_cos - imag_sin, real_sin + imag_cos)


def gathered_x(piece):
    planes, rows, total = piece.shape
    groups = lax.axis_size("gx")
    local = total // groups
    shaped = piece.reshape(planes, rows, groups, local)
    cos_group, sin_group = phase_table(groups, groups, groups)
    real, imag = complex_product("prgl,gk->prkl", shaped, None, cos_group, sin_group)
    cos_twist, sin_twist = phase_table(groups, local, total)
    real, imag = (real * cos_twist - imag * sin_twist, real * sin_twist + imag * cos_twist)
    cos_local, sin_local = phase_table(local, local, local)
    real, imag = complex_product("prkl,lm->prkm", real, imag, cos_local, sin_local)
    order = static_reversal(groups)
    real = jnp.take(real, order, axis=2).reshape(planes, rows, total)
    imag = jnp.take(imag, order, axis=2).reshape(planes, rows, total)
    real = jnp.transpose(real, (0, 2, 1))
    imag = jnp.transpose(imag, (0, 2, 1))
    return (
        lax.all_to_all(real, "gx", split_axis=1, concat_axis=2, tiled=True),
        lax.all_to_all(imag, "gx", split_axis=1, concat_axis=2, tiled=True),
    )


def gathered_y(pieces):
    real, imag = pieces
    outer, rows, total = real.shape
    groups = lax.axis_size("gy")
    local = total // groups
    real = real.reshape(outer, rows, groups, local)
    imag = imag.reshape(outer, rows, groups, local)
    cos_group, sin_group = phase_table(groups, groups, groups)
    real, imag = complex_product("argl,gk->arkl", real, imag, cos_group, sin_group)
    cos_twist, sin_twist = phase_table(groups, local, total)
    real, imag = (real * cos_twist - imag * sin_twist, real * sin_twist + imag * cos_twist)
    cos_local, sin_local = phase_table(local, local, local)
    real, imag = complex_product("arkl,lm->arkm", real, imag, cos_local, sin_local)
    order = static_reversal(groups)
    real = jnp.take(real, order, axis=2).reshape(outer, rows, total)
    imag = jnp.take(imag, order, axis=2).reshape(outer, rows, total)
    return (
        lax.all_to_all(real, "gy", split_axis=2, concat_axis=1, tiled=True),
        lax.all_to_all(imag, "gy", split_axis=2, concat_axis=1, tiled=True),
    )


def body(p_now, p_prev, phase, div_star):
    extrapolated = 2.0 * p_now - p_prev
    density = jnp.where(phase == 1, RHO_LIQUID, RHO_GAS).astype(jnp.float32)
    stacked = jnp.stack([extrapolated[1:-1], density[1:-1]])
    padded = with_halo(stacked, (("gx", 3), ("gy", 2)), 1)
    field_x = padded[0, :, 1:-1, :]
    weight_x = padded[1, :, 1:-1, :]
    flux_x = coefficient(weight_x[:, :, :-1], weight_x[:, :, 1:]) * (
        field_x[:, :, 1:] - field_x[:, :, :-1]
    )
    term_x = flux_x[:, :, 1:] - flux_x[:, :, :-1]
    field_y = padded[0, :, :, 1:-1]
    weight_y = padded[1, :, :, 1:-1]
    flux_y = coefficient(weight_y[:, :-1, :], weight_y[:, 1:, :]) * (
        field_y[:, 1:, :] - field_y[:, :-1, :]
    )
    term_y = flux_y[:, 1:, :] - flux_y[:, :-1, :]
    flux_z = coefficient(density[:-1], density[1:]) * (extrapolated[1:] - extrapolated[:-1])
    term_z = flux_z[1:] - flux_z[:-1]
    rhs = term_x + term_y + term_z + SOURCE * div_star
    planes, rows, cols = rhs.shape
    real, imag = gathered_x(lax.all_to_all(rhs, "gx", split_axis=1, concat_axis=2, tiled=True))
    real = real.reshape(1, planes * cols, rows)
    imag = imag.reshape(1, planes * cols, rows)
    real, imag = gathered_y(
        (
            lax.all_to_all(real, "gy", split_axis=1, concat_axis=2, tiled=True),
            lax.all_to_all(imag, "gy", split_axis=1, concat_axis=2, tiled=True),
        )
    )
    real = jnp.transpose(real.reshape(planes, cols, rows), (0, 2, 1))
    imag = jnp.transpose(imag.reshape(planes, cols, rows), (0, 2, 1))
    factor = 1.0 / math.sqrt(NX * NY)
    result = jnp.stack([real * factor, imag * factor])
    return result.reshape(2, planes, 1, rows, 1, cols)


def solution(mesh):
    return jax.shard_map(
        body,
        mesh=mesh,
        in_specs=(
            P(None, "gy", "gx"),
            P(None, "gy", "gx"),
            P(None, "gy", "gx"),
            P(None, "gy", "gx"),
        ),
        out_specs=P(None, None, "gy", None, "gx", None),
        check_vma=False,
    )
```

profile of v0, /device:TPU:2, one launch (start us, length us, event | category | flops | bytes accessed | tf_op | source)
XLA Modules:
  0.0 353.3 jit_solution(6375103268782560044)
XLA Ops:
  0.0 2.5 copy_subtract_fusion
  13.6 5.2 %collective-permute-done = f32[2,16,64,1]{2,1,3,0:T(8,128)S(1)} collective-permute-done((f32[2,16,64,1]{2,1,3,0:T(8,128)S(1)}, f32[2,16,64,1]{2,1,3,0:T(8,128)S(1)}, u32[]{:S(2)}, u32[]{:S(2)}) %collective-permute-start) | collective-permute-done | bytes 8224 | tf_op jit(solution)/shard_map/ppermute | solution.py:25
  20.4 11.3 %collective-permute-start.3 = (f32[2,16,1,130]{3,1,2,0:T(8,128)S(1)}, f32[2,16,1,130]{3,1,2,0:T(8,128)S(1)}, u32[]{:S(2)}, u32[]{:S(2)}) collective-permute-start(f32[2,16,1,130]{3,1,2,0:T(8,128)S(1)} %get-tuple-element.10), channel_id=1, source_target_pairs={{1,0},{2,1},{3,2},{4,3},{5,4},{6,5},{7,6},{8,7},{9,8},{10,9},{11,1... | collective-permute-start | bytes 49928 | tf_op jit(solution)/shard_map/ppermute | solution.py:27
  34.5 11.8 %collective-permute-done.2 = f32[2,16,1,130]{3,1,2,0:T(8,128)S(1)} collective-permute-done((f32[2,16,1,130]{3,1,2,0:T(8,128)S(1)}, f32[2,16,1,130]{3,1,2,0:T(8,128)S(1)}, u32[]{:S(2)}, u32[]{:S(2)}) %collective-permute-start.2) | collective-permute-done | bytes 16672 | tf_op jit(solution)/shard_map/ppermute | solution.py:25
  49.2 25.4 %all-to-all-start = ((f32[16,64,128]{2,0,1:T(8,128)}), f32[16,64,128]{2,0,1:T(8,128)S(1)}, u32[]{:S(2)}, u32[]{:S(2)}) async-start(f32[16,64,128]{2,0,1:T(8,128)} %fusion.33), calls=%async_computation | async-start | bytes 1048576 | tf_op jit(solution)/shard_map/all_to_all | solution.py:134
  74.6 18.8 %all-to-all-done = f32[16,64,128]{2,0,1:T(8,128)S(1)} async-done(((f32[16,64,128]{2,0,1:T(8,128)}), f32[16,64,128]{2,0,1:T(8,128)S(1)}, u32[]{:S(2)}, u32[]{:S(2)}) %all-to-all-start) | async-done | bytes 524320 | tf_op jit(solution)/shard_map/all_to_all | solution.py:134
  97.9 3.1 copy.62
  100.9 5.4 %reshape.232 = f32[16,1,8192]{2,1,0:T(1,128)} reshape(f32[2048,4,16]{2,1,0:T(4,128)} %bitcast.184) | data formatting | bytes 1048576
  106.4 14.8 %all-to-all-start.1 = ((f32[16,1,8192]{2,1,0:T(1,128)}), f32[16,1,8192]{2,1,0:T(1,128)S(1)}, u32[]{:S(2)}, u32[]{:S(2)}) async-start(f32[16,1,8192]{2,1,0:T(1,128)} %reshape.232), calls=%async_computation.1 | async-start | bytes 1048576 | tf_op jit(solution)/shard_map/all_to_all | solution.py:86
  123.8 3.1 copy.70
  126.9 5.4 %reshape.236 = f32[16,1,8192]{2,1,0:T(1,128)} reshape(f32[2048,4,16]{2,1,0:T(4,128)} %bitcast.185) | data formatting | bytes 1048576
  132.3 8.3 %all-to-all-done.1 = f32[16,1,8192]{2,1,0:T(1,128)S(1)} async-done(((f32[16,1,8192]{2,1,0:T(1,128)}), f32[16,1,8192]{2,1,0:T(1,128)S(1)}, u32[]{:S(2)}, u32[]{:S(2)}) %all-to-all-start.1) | async-done | bytes 524320 | tf_op jit(solution)/shard_map/all_to_all | solution.py:86
  140.6 15.6 %all-to-all-start.3 = ((f32[16,1,8192]{2,1,0:T(1,128)}), f32[16,1,8192]{2,1,0:T(1,128)S(1)}, u32[]{:S(2)}, u32[]{:S(2)}) async-start(f32[16,1,8192]{2,1,0:T(1,128)} %reshape.236), calls=%async_computation.3 | async-start | bytes 1048576 | tf_op jit(solution)/shard_map/all_to_all | solution.py:87
  158.7 4.3 %reshape.233 = f32[2048,4,16]{2,1,0:T(4,128)} reshape(f32[16,8192]{1,0:T(8,128)S(1)} %reduce) | data formatting | bytes 1048576
  163.0 3.4 copy.92
  167.1 9.4 %reduce.1 = f32[2048,64]{1,0:T(8,128)S(1)} reduce(f32[2048,1,64]{2,1,0:T(1,128)S(1)} %bitcast.194, f32[]{:T(128)} %broadcast.307), dimensions={1}, to_apply=%bitcast.160.reduce_sub_computation | reduce | bytes 1048580
  177.9 4.1 %all-to-all-start.2 = ((f32[32,1,4096]{2,1,0:T(1,128)}), f32[32,1,4096]{2,1,0:T(1,128)S(1)}, u32[]{:S(2)}, u32[]{:S(2)}) async-start(f32[32,1,4096]{2,1,0:T(1,128)} %reshape.234), calls=%async_computation.2 | async-start | bytes 1048576 | tf_op jit(solution)/shard_map/all_to_all | solution.py:139
  183.9 4.3 %reshape.237 = f32[2048,4,16]{2,1,0:T(4,128)} reshape(f32[16,8192]{1,0:T(8,128)S(1)} %reduce.3) | data formatting | bytes 1048576
  188.2 3.4 copy.96
  192.3 9.4 %reduce.4 = f32[2048,64]{1,0:T(8,128)S(1)} reduce(f32[2048,1,64]{2,1,0:T(1,128)S(1)} %bitcast.195, f32[]{:T(128)} %broadcast.307), dimensions={1}, to_apply=%bitcast.164.reduce_sub_computation | reduce | bytes 1048580
  203.2 9.1 %all-to-all-done.2 = f32[32,1,4096]{2,1,0:T(1,128)S(1)} async-done(((f32[32,1,4096]{2,1,0:T(1,128)}), f32[32,1,4096]{2,1,0:T(1,128)S(1)}, u32[]{:S(2)}, u32[]{:S(2)}) %all-to-all-start.2) | async-done | bytes 524320 | tf_op jit(solution)/shard_map/all_to_all | solution.py:139
  212.2 6.2 %all-to-all-start.4 = ((f32[32,1,4096]{2,1,0:T(1,128)}), f32[32,1,4096]{2,1,0:T(1,128)S(1)}, u32[]{:S(2)}, u32[]{:S(2)}) async-start(f32[32,1,4096]{2,1,0:T(1,128)} %reshape.238), calls=%async_computation.4 | async-start | bytes 1048576 | tf_op jit(solution)/shard_map/all_to_all | solution.py:140
  223.4 2.6 fusion.8
  226.0 21.7 %all-to-all-done.4 = f32[32,1,4096]{2,1,0:T(1,128)S(1)} async-done(((f32[32,1,4096]{2,1,0:T(1,128)}), f32[32,1,4096]{2,1,0:T(1,128)S(1)}, u32[]{:S(2)}, u32[]{:S(2)}) %all-to-all-start.4) | async-done | bytes 524320 | tf_op jit(solution)/shard_map/all_to_all | solution.py:140
  260.0 2.5 copy.100
  262.5 10.4 %reduce.6 = f32[2048,64]{1,0:T(8,128)S(1)} reduce(f32[2048,1,64]{2,1,0:T(1,128)} %bitcast.198, f32[]{:T(128)} %broadcast.307), dimensions={1}, to_apply=%bitcast.166.reduce_sub_computation | reduce | bytes 1048580
  274.4 6.4 %all-to-all-start.6 = ((f32[32,1,4096]{2,1,0:T(1,128)}), f32[32,1,4096]{2,1,0:T(1,128)}, u32[]{:S(2)}, u32[]{:S(2)}) async-start(f32[32,1,4096]{2,1,0:T(1,128)} %reshape.240), calls=%async_computation.6 | async-start | bytes 1048576 | tf_op jit(solution)/shard_map/all_to_all | solution.py:109
  285.3 9.4 %reduce.8 = f32[2048,64]{1,0:T(8,128)S(1)} reduce(f32[2048,1,64]{2,1,0:T(1,128)S(1)} %bitcast.199, f32[]{:T(128)} %broadcast.307), dimensions={1}, to_apply=%bitcast.168.reduce_sub_computation | reduce | bytes 1048580
  296.1 14.1 %all-to-all-done.6 = f32[32,1,4096]{2,1,0:T(1,128)} async-done(((f32[32,1,4096]{2,1,0:T(1,128)}), f32[32,1,4096]{2,1,0:T(1,128)}, u32[]{:S(2)}, u32[]{:S(2)}) %all-to-all-start.6) | async-done | bytes 524320 | tf_op jit(solution)/shard_map/all_to_all | solution.py:109
  310.2 6.3 %all-to-all-start.5 = ((f32[32,1,4096]{2,1,0:T(1,128)}), f32[32,1,4096]{2,1,0:T(1,128)S(1)}, u32[]{:S(2)}, u32[]{:S(2)}) async-start(f32[32,1,4096]{2,1,0:T(1,128)} %reshape.242), calls=%async_computation.5 | async-start | bytes 1048576 | tf_op jit(solution)/shard_map/all_to_all | solution.py:108
  316.5 3.0 reduce.7
  322.6 23.4 %all-to-all-done.5 = f32[32,1,4096]{2,1,0:T(1,128)S(1)} async-done(((f32[32,1,4096]{2,1,0:T(1,128)}), f32[32,1,4096]{2,1,0:T(1,128)S(1)}, u32[]{:S(2)}, u32[]{:S(2)}) %all-to-all-start.5) | async-done | bytes 524320 | tf_op jit(solution)/shard_map/all_to_all | solution.py:108
  (83 shorter events, 68.7 us)
Async XLA Ops:
  6.0 7.1 %collective-permute-start.1 = (f32[2,16,64,1]{2,1,3,0:T(8,128)S(1)}, f32[2,16,64,1]{2,1,3,0:T(8,128)S(1)}, u32[]{:S(2)}, u32[]{:S(2)}) collective-permute-start(f32[2,16,64,1]{2,1,3,0:T(8,128)S(1)} %copy.55), channel_id=1, source_target_pairs={{32,0},{64,32},{96,64},{128,96},{160,128},{192,160},{224,192},{256... | collective-permute-start | bytes 24584 | tf_op jit(solution)/shard_map/ppermute | solution.py:27
  9.5 9.3 %collective-permute-start = (f32[2,16,64,1]{2,1,3,0:T(8,128)S(1)}, f32[2,16,64,1]{2,1,3,0:T(8,128)S(1)}, u32[]{:S(2)}, u32[]{:S(2)}) collective-permute-start(f32[2,16,64,1]{2,1,3,0:T(8,128)S(1)} %copy.54), channel_id=1, source_target_pairs={{0,32},{32,64},{64,96},{96,128},{128,160},{160,192},{192,224},{224... | collective-permute-start | bytes 24584 | tf_op jit(solution)/shard_map/ppermute | solution.py:25
  20.4 14.1 %collective-permute-start.3 = (f32[2,16,1,130]{3,1,2,0:T(8,128)S(1)}, f32[2,16,1,130]{3,1,2,0:T(8,128)S(1)}, u32[]{:S(2)}, u32[]{:S(2)}) collective-permute-start(f32[2,16,1,130]{3,1,2,0:T(8,128)S(1)} %get-tuple-element.10), channel_id=1, source_target_pairs={{1,0},{2,1},{3,2},{4,3},{5,4},{6,5},{7,6},{8,7},{9,8},{10,9},{11,1... | collective-permute-start | bytes 49928 | tf_op jit(solution)/shard_map/ppermute | solution.py:27
  31.7 14.5 %collective-permute-start.2 = (f32[2,16,1,130]{3,1,2,0:T(8,128)S(1)}, f32[2,16,1,130]{3,1,2,0:T(8,128)S(1)}, u32[]{:S(2)}, u32[]{:S(2)}) collective-permute-start(f32[2,16,1,130]{3,1,2,0:T(8,128)S(1)} %get-tuple-element.9), channel_id=1, source_target_pairs={{0,1},{1,2},{2,3},{3,4},{4,5},{5,6},{6,7},{7,8},{8,9},{9,10},{10,1... | collective-permute-start | bytes 49928 | tf_op jit(solution)/shard_map/ppermute | solution.py:25
  46.6 1.1 copy-start
  46.6 1.3 copy-start.2
  47.9 26.7 %copy-start.4 = (s32[16]{0:T(128)S(1)}, s32[16]{0:T(128)}, u32[]{:S(2)}) copy-start(s32[16]{0:T(128)} %constant.169) | copy-start | bytes 196
  49.2 44.3 %all-to-all-start = ((f32[16,64,128]{2,0,1:T(8,128)}), f32[16,64,128]{2,0,1:T(8,128)S(1)}, u32[]{:S(2)}, u32[]{:S(2)}) async-start(f32[16,64,128]{2,0,1:T(8,128)} %fusion.33), calls=%async_computation | async-start | bytes 1048576 | tf_op jit(solution)/shard_map/all_to_all | solution.py:134
  106.4 34.2 %all-to-all-start.1 = ((f32[16,1,8192]{2,1,0:T(1,128)}), f32[16,1,8192]{2,1,0:T(1,128)S(1)}, u32[]{:S(2)}, u32[]{:S(2)}) async-start(f32[16,1,8192]{2,1,0:T(1,128)} %reshape.232), calls=%async_computation.1 | async-start | bytes 1048576 | tf_op jit(solution)/shard_map/all_to_all | solution.py:86
  140.6 37.3 %all-to-all-start.3 = ((f32[16,1,8192]{2,1,0:T(1,128)}), f32[16,1,8192]{2,1,0:T(1,128)S(1)}, u32[]{:S(2)}, u32[]{:S(2)}) async-start(f32[16,1,8192]{2,1,0:T(1,128)} %reshape.236), calls=%async_computation.3 | async-start | bytes 1048576 | tf_op jit(solution)/shard_map/all_to_all | solution.py:87
  177.9 34.3 %all-to-all-start.2 = ((f32[32,1,4096]{2,1,0:T(1,128)}), f32[32,1,4096]{2,1,0:T(1,128)S(1)}, u32[]{:S(2)}, u32[]{:S(2)}) async-start(f32[32,1,4096]{2,1,0:T(1,128)} %reshape.234), calls=%async_computation.2 | async-start | bytes 1048576 | tf_op jit(solution)/shard_map/all_to_all | solution.py:139
  192.3 26.1 %copy-start.3 = (s32[32]{0:T(128)S(1)}, s32[32]{0:T(128)}, u32[]{:S(2)}) copy-start(s32[32]{0:T(128)} %constant.171) | copy-start | bytes 388
  212.2 35.4 %all-to-all-start.4 = ((f32[32,1,4096]{2,1,0:T(1,128)}), f32[32,1,4096]{2,1,0:T(1,128)S(1)}, u32[]{:S(2)}, u32[]{:S(2)}) async-start(f32[32,1,4096]{2,1,0:T(1,128)} %reshape.238), calls=%async_computation.4 | async-start | bytes 1048576 | tf_op jit(solution)/shard_map/all_to_all | solution.py:140
  250.9 1.6 copy-start.1
  274.4 35.8 %all-to-all-start.6 = ((f32[32,1,4096]{2,1,0:T(1,128)}), f32[32,1,4096]{2,1,0:T(1,128)}, u32[]{:S(2)}, u32[]{:S(2)}) async-start(f32[32,1,4096]{2,1,0:T(1,128)} %reshape.240), calls=%async_computation.6 | async-start | bytes 1048576 | tf_op jit(solution)/shard_map/all_to_all | solution.py:109
  310.2 35.7 %all-to-all-start.5 = ((f32[32,1,4096]{2,1,0:T(1,128)}), f32[32,1,4096]{2,1,0:T(1,128)S(1)}, u32[]{:S(2)}, u32[]{:S(2)}) async-start(f32[32,1,4096]{2,1,0:T(1,128)} %reshape.242), calls=%async_computation.5 | async-start | bytes 1048576 | tf_op jit(solution)/shard_map/all_to_all | solution.py:108
where the time goes:
time: 360 us; the launch traced here: 353 us
  waiting for transfers between devices  112 us (31%)
  starting transfers between devices  96.3 us (27%)
  other arithmetic  61.8 us (17%)
  local copies, waits for them, and re-layouts  61.8 us (17%)
  matrix products  20.3 us (6%)
    unnamed x4, other arithmetic  38.5 us
    unnamed x22, local copies, waits for them, and re-layouts  31.6 us
    all_to_all x1, starting transfers between devices, body(): lax.all_to_all(rhs, 'gx', split_axis=1, concat_axis=2, tiled=True)  25.4 us
    all_to_all x1, waiting for transfers between devices, gathered_y(): lax.all_to_all(real, 'gy', split_axis=2, concat_axis=1, tiled=True)  23.4 us
    all_to_all x1, waiting for transfers between devices, body(): lax.all_to_all(imag, 'gy', split_axis=1, concat_axis=2, tiled=True)  21.7 us
    all_to_all x1, waiting for transfers between devices, body(): lax.all_to_all(rhs, 'gx', split_axis=1, concat_axis=2, tiled=True)  18.8 us
    ppermute x2, waiting for transfers between devices, with_halo(): lax.ppermute(tail, axis, [(i, (i + 1) % count) for i in range(count)])  17 us
    all_to_all x1, starting transfers between devices, gathered_x(): lax.all_to_all(imag, 'gx', split_axis=1, concat_axis=2, tiled=True)  15.6 us
  transfers between devices with their start and end apart: 11, of which 8 were waited for; matrix products, arithmetic and copies ran while one was open for 25% of the time, Pallas kernels for 0%

commit v1 on v0

v1 whole, which is shorter than its diff:
```python
import math

import jax
import jax.numpy as jnp
import ml_dtypes
import numpy as np
from jax import lax
from jax.experimental import pallas as pl
from jax.experimental.pallas import tpu as pltpu
from jax.sharding import PartitionSpec as P

NX = 2048
NY = 2048
PLANES = 16
LY = 64
LX = 128
N_GX = 16
N_GY = 32
N_ALL = N_GX * N_GY
F32 = jnp.float32
BF16 = jnp.bfloat16

QUAD = 7.0 / 16.0 - 7.0 / 9.0
LIN = 7.0 / 9.0 - QUAD


def reversal(index, digits):
    total = 0
    for place in range(digits):
        total = total * 2 + ((index >> place) & 1)
    return total


def split(value):
    high = value.astype(BF16)
    return high, (value - high.astype(F32)).astype(BF16)


def dot3(left, right):
    left_high, left_low = left
    right_high, right_low = right
    return (
        jnp.dot(left_high, right_high, preferred_element_type=F32)
        + jnp.dot(left_high, right_low, preferred_element_type=F32)
        + jnp.dot(left_low, right_high, preferred_element_type=F32)
    )


def flux(liquid_a, liquid_b, field_a, field_b):
    count = liquid_a + liquid_b
    return count * (LIN + QUAD * count) * (field_b - field_a)


def edges_kernel(now_ref, prev_ref, phase_ref, x_low, x_high, y_low, y_high):
    lane = lax.broadcasted_iota(jnp.int32, (LY, LX), 1)
    low = jnp.zeros((LY, LX), F32)
    high = jnp.zeros((LY, LX), F32)
    for k in range(PLANES):
        field = 2.0 * now_ref[k + 1] - prev_ref[k + 1]
        liquid = phase_ref[k + 1].astype(F32)
        y_low[k : k + 1, :] = field[0:1]
        y_low[PLANES + k : PLANES + k + 1, :] = liquid[0:1]
        y_high[k : k + 1, :] = field[LY - 1 : LY]
        y_high[PLANES + k : PLANES + k + 1, :] = liquid[LY - 1 : LY]
        low = jnp.where(lane == k, jnp.broadcast_to(field[:, 0:1], (LY, LX)), low)
        low = jnp.where(lane == PLANES + k, jnp.broadcast_to(liquid[:, 0:1], (LY, LX)), low)
        high = jnp.where(lane == k, jnp.broadcast_to(field[:, LX - 1 : LX], (LY, LX)), high)
        high = jnp.where(
            lane == PLANES + k, jnp.broadcast_to(liquid[:, LX - 1 : LX], (LY, LX)), high
        )
    x_low[...] = low
    x_high[...] = high


def stencil_kernel(now_ref, prev_ref, phase_ref, div_ref, x_below, x_above, y_below, y_above, out):
    lane = lax.broadcasted_iota(jnp.int32, (LY, LX), 1)
    row = lax.broadcasted_iota(jnp.int32, (LY, LX), 0)

    def plane(k):
        return 2.0 * now_ref[k] - prev_ref[k], phase_ref[k].astype(F32)

    def wide(ref, k):
        return jnp.broadcast_to(ref[:, k : k + 1], (LY, LX))

    def tall(ref, k):
        return jnp.broadcast_to(ref[k : k + 1, :], (LY, LX))

    field_before, liquid_before = plane(0)
    field, liquid = plane(1)
    flux_z = flux(liquid_before, liquid, field_before, field)
    for k in range(PLANES):
        field_after, liquid_after = plane(k + 2)
        flux_z_upper = flux(liquid, liquid_after, field, field_after)
        total = div_ref[k] + (flux_z_upper - flux_z)
        right = jnp.where(lane == LX - 1, wide(x_above, k), pltpu.roll(field, LX - 1, 1))
        right_liquid = jnp.where(
            lane == LX - 1, wide(x_above, PLANES + k), pltpu.roll(liquid, LX - 1, 1)
        )
        upper = flux(liquid, right_liquid, field, right)
        entering = flux(wide(x_below, PLANES + k), liquid, wide(x_below, k), field)
        total = total + (upper - jnp.where(lane == 0, entering, pltpu.roll(upper, 1, 1)))
        above = jnp.where(row == LY - 1, tall(y_above, k), pltpu.roll(field, LY - 1, 0))
        above_liquid = jnp.where(
            row == LY - 1, tall(y_above, PLANES + k), pltpu.roll(liquid, LY - 1, 0)
        )
        upper = flux(liquid, above_liquid, field, above)
        entering = flux(tall(y_below, PLANES + k), liquid, tall(y_below, k), field)
        total = total + (upper - jnp.where(row == 0, entering, pltpu.roll(upper, 1, 0)))
        out[k] = total
        field, liquid, flux_z = field_after, liquid_after, flux_z_upper


def device_kernel(x_ref, high_ref, low_ref, out):
    both = jnp.concatenate(
        [x_ref[pl.ds(0, N_ALL, stride=2), :], x_ref[pl.ds(1, N_ALL, stride=2), :]], axis=1
    )
    right = split(both)
    for part in range(2):
        rows = pl.ds(part * N_ALL, N_ALL)
        result = dot3((high_ref[rows, :], low_ref[rows, :]), right)
        out[pl.ds(2 * part, N_ALL, stride=4), :] = result[:, :LX]
        out[pl.ds(2 * part + 1, N_ALL, stride=4), :] = result[:, LX:]


def local_kernel(x_ref, y_matrix_ref, x_matrix_ref, out):
    y_matrix = split(y_matrix_ref[...])
    x_matrix = split(x_matrix_ref[...])
    for k in range(PLANES):
        lines = dot3(y_matrix, split(x_ref[pl.ds(k * 2 * LY, 2 * LY), :]))
        lines = jnp.concatenate([lines[:LY], lines[LY:]], axis=1)
        modes = dot3(split(lines), x_matrix)
        out[0, k] = modes[:, :LX]
        out[1, k] = modes[:, LX:]


def device_tables():
    source = np.arange(N_ALL)
    rev_p = np.array([reversal(i, 4) for i in range(N_GX)])
    rev_q = np.array([reversal(i, 5) for i in range(N_GY)])
    kx = rev_p[source // N_GY][:, None]
    ky = rev_q[source % N_GY][:, None]
    turns = (2 * kx * (source // N_GY)[None] + ky * (source % N_GY)[None]) % N_GY
    angle = turns * (2.0 * math.pi / N_GY)
    table = np.concatenate([np.cos(angle), -np.sin(angle)])
    high = table.astype(ml_dtypes.bfloat16)
    return high, (table - high.astype(np.float64)).astype(ml_dtypes.bfloat16)


def cos_sin(place, mode, length):
    angle = ((place * mode) % length).astype(F32) * (2.0 * math.pi / length)
    return jnp.cos(angle), jnp.sin(angle)


def local_tables():
    rp = reversal(lax.axis_index("gx"), 4)
    rq = reversal(lax.axis_index("gy"), 5)
    line = lax.broadcasted_iota(jnp.int32, (2 * LY, 2 * LY), 0)
    col = lax.broadcasted_iota(jnp.int32, (2 * LY, 2 * LY), 1)
    cosine, sine = cos_sin((col >> 2) * 2 + (col & 1), 32 * (line % LY) + rq, NY)
    part_out, part_in = line // LY, (col >> 1) & 1
    sign = jnp.where(part_out < part_in, 1.0, -1.0)
    y_matrix = jnp.where(part_out == part_in, cosine, sign * sine) * (1.0 / math.sqrt(NX * NY))
    line = lax.broadcasted_iota(jnp.int32, (2 * LX, 2 * LX), 0)
    col = lax.broadcasted_iota(jnp.int32, (2 * LX, 2 * LX), 1)
    cosine, sine = cos_sin(line % LX, 16 * (col % LX) + rp, NX)
    part_in, part_out = line // LX, col // LX
    sign = jnp.where(part_out < part_in, 1.0, -1.0)
    x_matrix = jnp.where(part_out == part_in, cosine, sign * sine)
    return y_matrix, x_matrix


def call(kernel, outs, *args):
    return pl.pallas_call(
        kernel,
        out_shape=outs,
        compiler_params=pltpu.CompilerParams(vmem_limit_bytes=40 * 1024 * 1024),
    )(*args)


def shape(*dims):
    return jax.ShapeDtypeStruct(dims, F32)


def body(p_now, p_prev, phase, div_star):
    x_low, x_high, y_low, y_high = call(
        edges_kernel,
        (shape(LY, LX), shape(LY, LX), shape(2 * PLANES, LX), shape(2 * PLANES, LX)),
        p_now,
        p_prev,
        phase,
    )
    up_x = [(i, (i + 1) % N_GX) for i in range(N_GX)]
    up_y = [(i, (i + 1) % N_GY) for i in range(N_GY)]
    down_x = [(b, a) for a, b in up_x]
    down_y = [(b, a) for a, b in up_y]
    x_below = lax.ppermute(x_high, "gx", up_x)
    x_above = lax.ppermute(x_low, "gx", down_x)
    y_below = lax.ppermute(y_high, "gy", up_y)
    y_above = lax.ppermute(y_low, "gy", down_y)
    rhs = call(
        stencil_kernel,
        shape(PLANES, LY, LX),
        p_now,
        p_prev,
        phase,
        div_star,
        x_below,
        x_above,
        y_below,
        y_above,
    )
    everywhere = ("gx", "gy")
    chunks = lax.all_to_all(rhs.reshape(N_ALL, 2, LX), everywhere, 0, 0, tiled=True)
    high, low = device_tables()
    modes = call(
        device_kernel,
        shape(4 * N_ALL, LX),
        chunks.reshape(2 * N_ALL, LX),
        jnp.asarray(high),
        jnp.asarray(low),
    )
    back = lax.all_to_all(modes.reshape(N_ALL, 4, LX), everywhere, 0, 0, tiled=True)
    y_matrix, x_matrix = local_tables()
    result = call(
        local_kernel,
        shape(2, PLANES, LY, LX),
        back.reshape(4 * N_ALL, LX),
        y_matrix,
        x_matrix,
    )
    return result.reshape(2, PLANES, 1, LY, 1, LX)


def solution(mesh):
    spec = P(None, "gy", "gx")
    return jax.shard_map(
        body,
        mesh=mesh,
        in_specs=(spec, spec, spec, spec),
        out_specs=P(None, None, "gy", None, "gx", None),
        check_vma=False,
    )
```

time: 360 us -> 168 us (0.47); the launches traced: 353 us -> 167 us
  blocking collectives: 0 us -> 64.3 us
  starting transfers between devices: 96.3 us -> 32.8 us
  other arithmetic: 61.8 us -> 2.4 us
  local copies, waits for them, and re-layouts: 61.8 us -> 3.21 us
  waiting for transfers between devices: 112 us -> 56.8 us
  matrix products: 20.3 us -> 0 us
  Pallas kernels: 0 us -> 7.6 us
    all_to_all x7 -> x1, starting transfers between devices: 78.7 us -> 9.7 us  [body(): lax.all_to_all(modes.reshape(N_ALL, 4, LX), everywhere, 0, 0, tiled=True)]
    all_to_all x0 -> x1, blocking collectives: none -> 64.3 us  [body(): lax.all_to_all(rhs.reshape(N_ALL, 2, LX), everywhere, 0, 0, tiled=True)]
    all_to_all x7 -> x1, waiting for transfers between devices: 95.3 us -> 55.4 us  [body(): lax.all_to_all(modes.reshape(N_ALL, 4, LX), everywhere, 0, 0, tiled=True)]
    unnamed x4 -> x0, other arithmetic: 38.5 us -> none
    unnamed x22 -> x12, local copies, waits for them, and re-layouts: 31.6 us -> 3.21 us
    dot_general x14 -> x0, matrix products: 20.3 us -> none  [the longest x4 6.48 us: complex_product(): real_sin = jnp.einsum(form, real, sine, precision=lax.Precision.HIGHEST)]
    ppermute x4, waiting for transfers between devices: 17 us -> 1.42 us  [the longest x1 1.41 us: body(): y_above = lax.ppermute(y_low, 'gy', down_y)]
    all_to_all x6 -> x0, other arithmetic: 12.5 us -> none  [the longest x1 2.97 us: gathered_y(): lax.all_to_all(imag, 'gy', split_axis=2, concat_axis=1, tiled=True)]
  transfers between devices with their start and end apart: 11 -> 5, of which waited for: 8 -> 2; matrix products, arithmetic and copies ran while one was open for 25% -> 1% of each run, Pallas kernels for 0% -> 0%
where the time goes in v1:
time: 168 us; the launch traced here: 167 us
  blocking collectives  64.3 us (38%)
  waiting for transfers between devices  56.8 us (34%)
  starting transfers between devices  32.8 us (20%)
  Pallas kernels  7.6 us (5%)
  local copies, waits for them, and re-layouts  3.21 us (2%)
  other arithmetic  2.4 us (1%)
    all_to_all x1, blocking collectives, body(): lax.all_to_all(rhs.reshape(N_ALL, 2, LX), everywhere, 0, 0, tiled=True)  64.3 us
    all_to_all x1, waiting for transfers between devices, body(): lax.all_to_all(modes.reshape(N_ALL, 4, LX), everywhere, 0, 0, tiled=True)  55.4 us
    ppermute x1, starting transfers between devices, body(): y_above = lax.ppermute(y_low, 'gy', down_y)  14 us
    all_to_all x1, starting transfers between devices, body(): lax.all_to_all(modes.reshape(N_ALL, 4, LX), everywhere, 0, 0, tiled=True)  9.7 us
    pallas_call x4, Pallas kernels, call(): pl.pallas_call(kernel, out_shape=outs, compiler_params=pltpu.CompilerPara...  7.6 us
    ppermute x1, starting transfers between devices, body(): x_above = lax.ppermute(x_low, 'gx', down_x)  3.64 us
    ppermute x1, starting transfers between devices, body(): y_below = lax.ppermute(y_high, 'gy', up_y)  3.48 us
  transfers between devices with their start and end apart: 5, of which 2 were waited for; matrix products, arithmetic and copies ran while one was open for 1% of the time, Pallas kernels for 0%

profile of v1, /device:TPU:2, one launch (start us, length us, event | category | flops | bytes accessed | tf_op | source)
XLA Modules:
  0.0 167.2 jit_solution(17194383964362949735)
XLA Ops:
  0.0 0.0 copy-start
  0.0 1.1 copy-done
  1.1 0.0 copy-start.1
  1.1 1.1 copy-done.1
  2.1 0.0 copy-start.2
  2.1 1.1 copy-done.2
  3.2 0.0 copy-start.5
  3.2 0.7 shard_map.64
  3.9 1.9 %collective-permute-start = (f32[64,128]{1,0:T(8,128)S(1)}, f32[64,128]{1,0:T(8,128)S(1)}, u32[]{:S(2)}, u32[]{:S(2)}) collective-permute-start(f32[64,128]{1,0:T(8,128)S(1)} %get-tuple-element.9), channel_id=1, source_target_pairs={{0,32},{32,64},{64,96},{96,128},{128,160},{160,192},{192,224},{224... | collective-permute-start | bytes 98312 | tf_op jit(solution)/shard_map/ppermute | solution.py:196
  5.8 3.6 %collective-permute-start.1 = (f32[64,128]{1,0:T(8,128)S(1)}, f32[64,128]{1,0:T(8,128)S(1)}, u32[]{:S(2)}, u32[]{:S(2)}) collective-permute-start(f32[64,128]{1,0:T(8,128)S(1)} %get-tuple-element.10), channel_id=1, source_target_pairs={{32,0},{64,32},{96,64},{128,96},{160,128},{192,160},{224,192},{256... | collective-permute-start | bytes 98312 | tf_op jit(solution)/shard_map/ppermute | solution.py:197
  9.4 3.5 %collective-permute-start.2 = (f32[32,128]{1,0:T(8,128)S(1)}, f32[32,128]{1,0:T(8,128)S(1)}, u32[]{:S(2)}, u32[]{:S(2)}) collective-permute-start(f32[32,128]{1,0:T(8,128)S(1)} %get-tuple-element.11), channel_id=1, source_target_pairs={{0,1},{1,2},{2,3},{3,4},{4,5},{5,6},{6,7},{7,8},{8,9},{9,10},{10,1... | collective-permute-start | bytes 49160 | tf_op jit(solution)/shard_map/ppermute | solution.py:198
  12.9 14.0 %collective-permute-start.3 = (f32[32,128]{1,0:T(8,128)S(1)}, f32[32,128]{1,0:T(8,128)S(1)}, u32[]{:S(2)}, u32[]{:S(2)}) collective-permute-start(f32[32,128]{1,0:T(8,128)S(1)} %get-tuple-element.12), channel_id=1, source_target_pairs={{1,0},{2,1},{3,2},{4,3},{5,4},{6,5},{7,6},{8,7},{9,8},{10,9},{11,1... | collective-permute-start | bytes 49160 | tf_op jit(solution)/shard_map/ppermute | solution.py:199
  27.0 0.0 collective-permute-done.2.y_below
  27.0 1.4 collective-permute-done.3.y_above
  28.4 0.0 collective-permute-done.x_below
  28.4 0.0 collective-permute-done.1.x_above
  28.4 0.0 copy-done.5
  28.4 0.0 copy-start.4
  28.4 1.9 %shard_map.65 = f32[16,64,128]{2,1,0:T(8,128)S(1)} custom-call(f32[18,64,128]{2,1,0:T(8,128)S(1)} %copy-done, f32[18,64,128]{2,1,0:T(8,128)S(1)} %copy-done.1, s32[18,64,128]{2,1,0:T(8,128)S(1)} %copy-done.2, f32[16,64,128]{2,1,0:T(8,128)S(1)} %copy-done.5, f32[64,128]{1,0:T(8,128)S(1)} %collective-permute-done.x_below, ...), custom_call_target="tpu_custom_call" | custom-call | tf_op jit(solution)/shard_map/pallas_call | solution.py:173
  30.3 0.0 copy-start.3
  30.3 64.3 %all_to_all.10 = f32[512,2,128]{2,1,0:T(2,128)S(1)} all-to-all(f32[512,2,128]{2,1,0:T(2,128)S(1)} %bitcast.9), channel_id=1, replica_groups=mesh['gx'=16,'gy'=32] {'gx','gy'}, dimensions={0} | all-to-all | bytes 1048576 | tf_op jit(solution)/shard_map/all_to_all | solution.py:213
  94.6 0.0 copy-done.4
  94.6 0.0 copy-done.3
  94.6 2.0 %shard_map.66 = f32[2048,128]{1,0:T(8,128)} custom-call(f32[1024,128]{1,0:T(8,128)S(1)} %bitcast.8, bf16[1024,512]{1,0:T(8,128)(2,1)S(1)} %copy-done.3, bf16[1024,512]{1,0:T(8,128)(2,1)S(1)} %copy-done.4), custom_call_target="tpu_custom_call" | custom-call | tf_op jit(solution)/shard_map/pallas_call | solution.py:173
  96.6 9.7 %all-to-all-start.1 = ((f32[512,4,128]{2,1,0:T(4,128)}), f32[512,4,128]{2,1,0:T(4,128)S(1)}, u32[]{:S(2)}, u32[]{:S(2)}) async-start(f32[512,4,128]{2,1,0:T(4,128)} %bitcast.2), calls=%async_computation.1 | async-start | bytes 2097152 | tf_op jit(solution)/shard_map/all_to_all | solution.py:222
  106.4 0.4 select_multiply_fusion.y_matrix_ref
  106.8 2.0 %multiply_select_fusion.x_matrix_ref = f32[256,256]{1,0:T(8,128)S(1)} fusion(s32[]{:T(128)S(6)} %add.82, s32[256]{0:T(256)S(1)} %get-tuple-element.22, s32[256]{0:T(256)S(1)} %get-tuple-element.25, s32[256]{0:T(256)S(1)} %get-tuple-element.21, s32[256]{0:T(256)S(1)} %get-tuple-element.26, pred[256]{0:T(512)(128)(4,1)S(1)} %get-tuple-element.23, ...), kind=kLoop, calls=%fused_computation.8 | loop fusion | flops 1638400 | bytes 266756 | tf_op jit(solution)/shard_map/jit(_where)/select_n | solution.py:168
  108.8 55.4 %all-to-all-done.1 = f32[512,4,128]{2,1,0:T(4,128)S(1)} async-done(((f32[512,4,128]{2,1,0:T(4,128)}), f32[512,4,128]{2,1,0:T(4,128)S(1)}, u32[]{:S(2)}, u32[]{:S(2)}) %all-to-all-start.1) | async-done | bytes 1048608 | tf_op jit(solution)/shard_map/all_to_all | solution.py:222
  164.1 3.1 %shard_map.67 = f32[2,16,64,128]{3,2,1,0:T(8,128)} custom-call(f32[2048,128]{1,0:T(8,128)S(1)} %bitcast.7, f32[128,128]{1,0:T(8,128)S(1)} %select_multiply_fusion.y_matrix_ref, f32[256,256]{1,0:T(8,128)S(1)} %multiply_select_fusion.x_matrix_ref), custom_call_target="tpu_custom_call" | custom-call | tf_op jit(solution)/shard_map/pallas_call | solution.py:173
  (7 shorter events, 0.0 us)
Async XLA Ops:
  0.0 1.1 copy-start
  1.1 1.1 copy-start.1
  2.1 1.1 copy-start.2
  3.2 25.2 %copy-start.5 = (f32[16,64,128]{2,1,0:T(8,128)S(1)}, f32[16,64,128]{2,1,0:T(8,128)}, u32[]{:S(2)}) copy-start(f32[16,64,128]{2,1,0:T(8,128)} %div_ref.1) | copy-start | bytes 1572868
  3.9 24.5 %collective-permute-start = (f32[64,128]{1,0:T(8,128)S(1)}, f32[64,128]{1,0:T(8,128)S(1)}, u32[]{:S(2)}, u32[]{:S(2)}) collective-permute-start(f32[64,128]{1,0:T(8,128)S(1)} %get-tuple-element.9), channel_id=1, source_target_pairs={{0,32},{32,64},{64,96},{96,128},{128,160},{160,192},{192,224},{224... | collective-permute-start | bytes 98312 | tf_op jit(solution)/shard_map/ppermute | solution.py:196
  5.8 22.6 %collective-permute-start.1 = (f32[64,128]{1,0:T(8,128)S(1)}, f32[64,128]{1,0:T(8,128)S(1)}, u32[]{:S(2)}, u32[]{:S(2)}) collective-permute-start(f32[64,128]{1,0:T(8,128)S(1)} %get-tuple-element.10), channel_id=1, source_target_pairs={{32,0},{64,32},{96,64},{128,96},{160,128},{192,160},{224,192},{256... | collective-permute-start | bytes 98312 | tf_op jit(solution)/shard_map/ppermute | solution.py:197
  9.4 17.5 %collective-permute-start.2 = (f32[32,128]{1,0:T(8,128)S(1)}, f32[32,128]{1,0:T(8,128)S(1)}, u32[]{:S(2)}, u32[]{:S(2)}) collective-permute-start(f32[32,128]{1,0:T(8,128)S(1)} %get-tuple-element.11), channel_id=1, source_target_pairs={{0,1},{1,2},{2,3},{3,4},{4,5},{5,6},{6,7},{7,8},{8,9},{9,10},{10,1... | collective-permute-start | bytes 49160 | tf_op jit(solution)/shard_map/ppermute | solution.py:198
  12.9 15.5 %collective-permute-start.3 = (f32[32,128]{1,0:T(8,128)S(1)}, f32[32,128]{1,0:T(8,128)S(1)}, u32[]{:S(2)}, u32[]{:S(2)}) collective-permute-start(f32[32,128]{1,0:T(8,128)S(1)} %get-tuple-element.12), channel_id=1, source_target_pairs={{1,0},{2,1},{3,2},{4,3},{5,4},{6,5},{7,6},{8,7},{9,8},{10,9},{11,1... | collective-permute-start | bytes 49160 | tf_op jit(solution)/shard_map/ppermute | solution.py:199
  28.4 66.2 %copy-start.4 = (bf16[1024,512]{1,0:T(8,128)(2,1)S(1)}, bf16[1024,512]{1,0:T(8,128)(2,1)}, u32[]{:S(2)}) copy-start(bf16[1024,512]{1,0:T(8,128)(2,1)} %constant.130.clone.low_ref) | copy-start | bytes 3145732
  30.3 64.3 %copy-start.3 = (bf16[1024,512]{1,0:T(8,128)(2,1)S(1)}, bf16[1024,512]{1,0:T(8,128)(2,1)}, u32[]{:S(2)}) copy-start(bf16[1024,512]{1,0:T(8,128)(2,1)} %constant.129.clone.high_ref) | copy-start | bytes 3145732
  96.6 67.5 %all-to-all-start.1 = ((f32[512,4,128]{2,1,0:T(4,128)}), f32[512,4,128]{2,1,0:T(4,128)S(1)}, u32[]{:S(2)}, u32[]{:S(2)}) async-start(f32[512,4,128]{2,1,0:T(4,128)} %bitcast.2), calls=%async_computation.1 | async-start | bytes 2097152 | tf_op jit(solution)/shard_map/all_to_all | solution.py:222

commit v2 on v1

v2 whole, which is shorter than its diff:
```python
import math

import jax
import jax.numpy as jnp
import ml_dtypes
import numpy as np
from jax import lax
from jax.experimental import pallas as pl
from jax.experimental.pallas import tpu as pltpu
from jax.sharding import PartitionSpec as P

NX = 2048
NY = 2048
PLANES = 16
LY = 64
LX = 128
N_GX = 16
N_GY = 32
N_ALL = N_GX * N_GY
F32 = jnp.float32
BF16 = jnp.bfloat16

QUAD = 7.0 / 16.0 - 7.0 / 9.0
LIN = 7.0 / 9.0 - QUAD

PIECES = 8
PIECE = LX // PIECES
SHIFT = 8
PER_PLANE = N_ALL // PLANES
WIDE = PER_PLANE - PIECES


def reversal(index, digits):
    total = 0
    for place in range(digits):
        total = total * 2 + ((index >> place) & 1)
    return total


def split(value):
    high = value.astype(BF16)
    return high, (value - high.astype(F32)).astype(BF16)


def dot3(left, right):
    left_high, left_low = left
    right_high, right_low = right
    return (
        jnp.dot(left_high, right_high, preferred_element_type=F32)
        + jnp.dot(left_high, right_low, preferred_element_type=F32)
        + jnp.dot(left_low, right_high, preferred_element_type=F32)
    )


def flux(liquid_a, liquid_b, field_a, field_b):
    count = liquid_a + liquid_b
    return count * (LIN + QUAD * count) * (field_b - field_a)


def roll(value, by, axis):
    by = by % value.shape[axis]
    return pltpu.roll(value, by, axis) if by else value


def lanes_of(rows):
    return lax.broadcasted_iota(jnp.int32, (rows, LX), 1)


def rows_of(rows):
    return lax.broadcasted_iota(jnp.int32, (rows, LX), 0)


def exchange_pieces(value):
    offset = (lanes_of(PIECES) // PIECE - rows_of(PIECES)) & (PIECES - 1)
    total = value
    for d in range(1, PIECES):
        total = jnp.where(offset == d, roll(roll(value, -d, 0), PIECE * d, 1), total)
    return total


def stencil_kernel(now_ref, prev_ref, phase_ref, div_ref, out):
    lane = lanes_of(LY)
    row = rows_of(LY)
    edge_lane = (lane == 0) | (lane == LX - 1)
    sub = rows_of(PIECES)
    first_half = lanes_of(PIECES) % PIECE < PIECE // 2

    def plane(k):
        return 2.0 * now_ref[k] - prev_ref[k], phase_ref[k].astype(F32)

    field_before, liquid_before = plane(0)
    field, liquid = plane(1)
    flux_z = flux(liquid_before, liquid, field_before, field)
    for k in range(PLANES):
        field_after, liquid_after = plane(k + 2)
        flux_z_upper = flux(liquid, liquid_after, field, field_after)
        total = div_ref[k] + (flux_z_upper - flux_z)
        upper = flux(liquid, roll(liquid, -1, 1), field, roll(field, -1, 1))
        upper = jnp.where(lane == LX - 1, 0.0, upper)
        total = total + (upper - roll(upper, 1, 1))
        upper = flux(liquid, roll(liquid, -1, 0), field, roll(field, -1, 0))
        upper = jnp.where(row == LY - 1, 0.0, upper)
        total = total + (upper - roll(upper, 1, 0))
        total = roll(total, SHIFT, 1)
        faces = jnp.where(edge_lane, field, 0.0) + roll(jnp.where(edge_lane, liquid, 0.0), 2, 1)
        faces = roll(faces, SHIFT, 1)
        lines = [field[0:1], liquid[0:1], field[LY - 1 : LY], liquid[LY - 1 : LY]]
        pairs = jnp.zeros((PIECES, LX), F32)
        for f, line in enumerate(lines):
            pairs = jnp.where(sub // 2 == f, jnp.broadcast_to(line, (PIECES, LX)), pairs)
        pairs = jnp.where(sub % 2 == 0, roll(pairs, SHIFT, 1), pairs)
        pairs = roll(exchange_pieces(jnp.where(first_half, pairs, 0.0)), -1, 1)

        start = k * PER_PLANE * 3
        low, high = slice(0, PIECES), slice(LY - PIECES, LY)
        out[pl.ds(start, PIECES, stride=3), :] = exchange_pieces(total[low])
        out[pl.ds(start + 1, PIECES, stride=3), :] = exchange_pieces(total[high])
        out[pl.ds(start + 2, PIECES, stride=3), :] = (
            exchange_pieces(faces[low] + roll(faces[high], 4, 1)) + pairs
        )
        start += PIECES * 3
        low, high = slice(PIECES, PIECES + WIDE), slice(PIECES + WIDE, PIECES + 2 * WIDE)
        out[pl.ds(start, WIDE, stride=3), :] = total[low]
        out[pl.ds(start + 1, WIDE, stride=3), :] = total[high]
        out[pl.ds(start + 2, WIDE, stride=3), :] = faces[low] + roll(faces[high], 4, 1)
        field, liquid, flux_z = field_after, liquid_after, flux_z_upper


def device_kernel(x_ref, high_ref, low_ref, out, cells):
    lane = lanes_of(N_GY)
    place = lane % PIECE
    row = rows_of(N_GY)
    x_face = place == 7
    y_first = (lane == LX - 1) | (lane < 7)
    y_second = (lane >= 15) & (lane < 23)

    def group(g, r):
        return x_ref[pl.ds((g % N_GX) * N_GY * 3 + r, N_GY, stride=3), :]

    def x_flux(here, there, t):
        through = flux(
            roll(here, -2 - 4 * t, 1),
            roll(there, -3 - 4 * t, 1),
            roll(here, -4 * t, 1),
            roll(there, -1 - 4 * t, 1),
        )
        return jnp.where(x_face, through, 0.0)

    last = group(N_GX - 1, 2)
    here = group(0, 2)
    entering = [x_flux(last, here, t) for t in range(2)]
    for g in range(N_GX):
        there = group(g + 1, 2)
        first, second = group(g, 0), group(g, 1)
        leaving = [x_flux(here, there, t) for t in range(2)]
        first = first + (leaving[0] - roll(entering[0], 1, 1))
        second = second + (leaving[1] - roll(entering[1], 1, 1))
        after = roll(here, -1, 0)
        through = flux(roll(here, -96, 1), roll(after, -32, 1), roll(here, -64, 1), after)
        through_first = jnp.where(y_first, through, 0.0)
        through_second = jnp.where(y_second, through, 0.0)
        before = roll(through_first, 1, 1) + roll(through_second, -7, 1)
        first = first - roll(before, 1, 0)
        second = second + roll(before, LX - PIECE, 1)
        cells[pl.ds(g * N_GY, N_GY), :LX] = first
        cells[pl.ds(g * N_GY, N_GY), LX:] = second
        here, entering = there, leaving

    right = split(cells[...])
    for part in range(2):
        rows = pl.ds(part * N_ALL, N_ALL)
        result = dot3((high_ref[rows, :], low_ref[rows, :]), right)
        out[pl.ds(2 * part, N_ALL, stride=4), :] = result[:, :LX]
        out[pl.ds(2 * part + 1, N_ALL, stride=4), :] = result[:, LX:]


def local_kernel(x_ref, y_matrix_ref, x_matrix_ref, out):
    y_matrix = split(y_matrix_ref[...])
    x_matrix = split(x_matrix_ref[...])
    for k in range(PLANES):
        start = k * 2 * LY
        lines = [
            exchange_pieces(x_ref[pl.ds(start + kind, PIECES, stride=4), :]) for kind in range(4)
        ]
        lines.append(x_ref[pl.ds(start + 4 * PIECES, 4 * WIDE), :])
        lines = dot3(y_matrix, split(jnp.concatenate(lines, axis=0)))
        lines = jnp.concatenate([lines[:LY], lines[LY:]], axis=1)
        modes = dot3(split(lines), x_matrix)
        out[0, k] = modes[:, :LX]
        out[1, k] = modes[:, LX:]


def device_tables():
    source = np.arange(N_ALL)
    rev_p = np.array([reversal(i, 4) for i in range(N_GX)])
    rev_q = np.array([reversal(i, 5) for i in range(N_GY)])
    kx = rev_p[source // N_GY][:, None]
    ky = rev_q[source % N_GY][:, None]
    turns = (2 * kx * (source // N_GY)[None] + ky * (source % N_GY)[None]) % N_GY
    angle = turns * (2.0 * math.pi / N_GY)
    table = np.concatenate([np.cos(angle), -np.sin(angle)])
    high = table.astype(ml_dtypes.bfloat16)
    return high, (table - high.astype(np.float64)).astype(ml_dtypes.bfloat16)


def cos_sin(place, mode, length):
    angle = ((place * mode) % length).astype(F32) * (2.0 * math.pi / length)
    return jnp.cos(angle), jnp.sin(angle)


def local_tables():
    rp = reversal(lax.axis_index("gx"), 4)
    rq = reversal(lax.axis_index("gy"), 5)
    line = lax.broadcasted_iota(jnp.int32, (2 * LY, 2 * LY), 0)
    col = lax.broadcasted_iota(jnp.int32, (2 * LY, 2 * LY), 1)
    rest = col - 4 * PIECES
    in_piece = rest < 0
    part_in = jnp.where(in_piece, col >> 4, rest >> 1) & 1
    place = jnp.where(
        in_piece,
        (col & 7) + (LY - PIECES) * ((col >> 3) & 1),
        PIECES + (rest >> 2) + WIDE * (rest & 1),
    )
    cosine, sine = cos_sin(place, 32 * (line % LY) + rq, NY)
    part_out = line // LY
    sign = jnp.where(part_out < part_in, 1.0, -1.0)
    y_matrix = jnp.where(part_out == part_in, cosine, sign * sine) * (1.0 / math.sqrt(NX * NY))
    line = lax.broadcasted_iota(jnp.int32, (2 * LX, 2 * LX), 0)
    col = lax.broadcasted_iota(jnp.int32, (2 * LX, 2 * LX), 1)
    cosine, sine = cos_sin((line + LX - SHIFT) % LX, 16 * (col % LX) + rp, NX)
    part_in, part_out = line // LX, col // LX
    sign = jnp.where(part_out < part_in, 1.0, -1.0)
    x_matrix = jnp.where(part_out == part_in, cosine, sign * sine)
    return y_matrix, x_matrix


def call(kernel, outs, *args, scratch=()):
    return pl.pallas_call(
        kernel,
        out_shape=outs,
        scratch_shapes=scratch,
        compiler_params=pltpu.CompilerParams(vmem_limit_bytes=40 * 1024 * 1024),
    )(*args)


def shape(*dims):
    return jax.ShapeDtypeStruct(dims, F32)


def body(p_now, p_prev, phase, div_star):
    chunks = call(stencil_kernel, shape(3 * N_ALL, LX), p_now, p_prev, phase, div_star)
    everywhere = ("gx", "gy")
    chunks = lax.all_to_all(chunks.reshape(N_ALL, 1, 3 * LX), everywhere, 0, 0, tiled=True)
    high, low = device_tables()
    modes = call(
        device_kernel,
        shape(4 * N_ALL, LX),
        chunks.reshape(3 * N_ALL, LX),
        jnp.asarray(high),
        jnp.asarray(low),
        scratch=[pltpu.VMEM((N_ALL, 2 * LX), F32)],
    )
    back = lax.all_to_all(modes.reshape(N_ALL, 4, LX), everywhere, 0, 0, tiled=True)
    y_matrix, x_matrix = local_tables()
    result = call(
        local_kernel,
        shape(2, PLANES, LY, LX),
        back.reshape(4 * N_ALL, LX),
        y_matrix,
        x_matrix,
    )
    return result.reshape(2, PLANES, 1, LY, 1, LX)


def solution(mesh):
    spec = P(None, "gy", "gx")
    return jax.shard_map(
        body,
        mesh=mesh,
        in_specs=(spec, spec, spec, spec),
        out_specs=P(None, None, "gy", None, "gx", None),
        check_vma=False,
    )
```

time: 168 us -> 154 us (0.917)
  starting transfers between devices: 32.8 us -> 9.66 us
  blocking collectives: 64.3 us -> 69.8 us
  Pallas kernels: 7.6 us -> 11.9 us
    ppermute x4 -> x0, starting transfers between devices: 23.1 us -> none  [the longest x1 14 us: body(): y_above = lax.ppermute(y_low, 'gy', down_y)]
    all_to_all x1, blocking collectives: 64.3 us -> 69.8 us  [body(): lax.all_to_all(chunks.reshape(N_ALL, 1, 3 * LX), everywhere, 0, 0, tiled=...]
    pallas_call x4 -> x3, Pallas kernels: 7.6 us -> 11.9 us  [call(): pl.pallas_call(kernel, out_shape=outs, scratch_shapes=scratch, compiler_p...]
  transfers between devices with their start and end apart: 5 -> 1, of which waited for: 2 -> 1; matrix products, arithmetic and copies ran while one was open for 1% -> 2% of each run, Pallas kernels for 0% -> 0%
where the time goes in v2:
time: 154 us; the launch traced here: 153 us
  blocking collectives  69.8 us (45%)
  waiting for transfers between devices  55.3 us (36%)
  Pallas kernels  11.9 us (8%)
  starting transfers between devices  9.66 us (6%)
  local copies, waits for them, and re-layouts  4.24 us (3%)
  other arithmetic  2.43 us (2%)
    all_to_all x1, blocking collectives, body(): lax.all_to_all(chunks.reshape(N_ALL, 1, 3 * LX), everywhere, 0, 0, tiled=...  69.8 us
    all_to_all x1, waiting for transfers between devices, body(): lax.all_to_all(modes.reshape(N_ALL, 4, LX), everywhere, 0, 0, tiled=True)  55.3 us
    pallas_call x3, Pallas kernels, call(): pl.pallas_call(kernel, out_shape=outs, scratch_shapes=scratch, compiler_p...  11.9 us
    all_to_all x1, starting transfers between devices, body(): lax.all_to_all(modes.reshape(N_ALL, 4, LX), everywhere, 0, 0, tiled=True)  9.66 us
    unnamed x12, local copies, waits for them, and re-layouts  4.24 us
  transfers between devices with their start and end apart: 1, of which 1 were waited for; matrix products, arithmetic and copies ran while one was open for 2% of the time, Pallas kernels for 0%

profile of v2, /device:TPU:2, one launch (start us, length us, event | category | flops | bytes accessed | tf_op | source)
XLA Modules:
  0.0 153.4 jit_solution(17388430574860784843)
XLA Ops:
  0.0 0.0 copy-start.2
  0.0 1.1 copy-done.2
  1.1 0.0 copy-start.3
  1.1 1.1 copy-done.3
  2.1 0.0 copy-start.4
  2.1 1.1 copy-done.4
  3.2 0.0 copy-start.5
  3.2 1.0 copy-done.5
  4.2 0.0 copy-start.1
  4.2 5.8 %shard_map.64 = f32[1536,128]{1,0:T(8,128)S(1)} custom-call(f32[18,64,128]{2,1,0:T(8,128)S(1)} %copy-done.2, f32[18,64,128]{2,1,0:T(8,128)S(1)} %copy-done.3, s32[18,64,128]{2,1,0:T(8,128)S(1)} %copy-done.4, f32[16,64,128]{2,1,0:T(8,128)S(1)} %copy-done.5), custom_call_target="tpu_custom_call" | custom-call | tf_op jit(solution)/shard_map/pallas_call | solution.py:238
  10.0 0.0 copy-start
  10.0 69.8 %all_to_all.10 = f32[512,1,384]{2,1,0:T(1,128)S(1)} all-to-all(f32[512,1,384]{2,1,0:T(1,128)S(1)} %bitcast.8), channel_id=1, replica_groups=mesh['gx'=16,'gy'=32] {'gx','gy'}, dimensions={0} | all-to-all | bytes 1572864 | tf_op jit(solution)/shard_map/all_to_all | solution.py:253
  79.8 0.0 copy-done.1
  79.8 0.0 copy-done
  79.8 2.9 %shard_map.65 = f32[2048,128]{1,0:T(8,128)} custom-call(f32[1536,128]{1,0:T(8,128)S(1)} %bitcast.9, bf16[1024,512]{1,0:T(8,128)(2,1)S(1)} %copy-done, bf16[1024,512]{1,0:T(8,128)(2,1)S(1)} %copy-done.1), custom_call_target="tpu_custom_call" | custom-call | tf_op jit(solution)/shard_map/pallas_call | solution.py:238
  82.7 9.7 %all-to-all-start.1 = ((f32[512,4,128]{2,1,0:T(4,128)}), f32[512,4,128]{2,1,0:T(4,128)S(1)}, u32[]{:S(2)}, u32[]{:S(2)}) async-start(f32[512,4,128]{2,1,0:T(4,128)} %bitcast.2), calls=%async_computation.1 | async-start | bytes 2097152 | tf_op jit(solution)/shard_map/all_to_all | solution.py:263
  92.5 0.4 select_multiply_fusion.y_matrix_ref
  92.9 2.0 %multiply_select_fusion.x_matrix_ref = f32[256,256]{1,0:T(8,128)S(1)} fusion(s32[]{:T(128)S(6)} %add.106, s32[256]{0:T(256)S(1)} %get-tuple-element.17, s32[256]{0:T(256)S(1)} %get-tuple-element.18, s32[256]{0:T(256)S(1)} %get-tuple-element.15, s32[256]{0:T(256)S(1)} %get-tuple-element.21, s32[256]{0:T(256)S(1)} %get-tuple-element.16, ...), kind=kLoop, calls=%fused_computation.8 | loop fusion | flops 1638400 | bytes 269060 | tf_op jit(solution)/shard_map/jit(_where)/select_n | solution.py:233
  94.9 55.3 %all-to-all-done.1 = f32[512,4,128]{2,1,0:T(4,128)S(1)} async-done(((f32[512,4,128]{2,1,0:T(4,128)}), f32[512,4,128]{2,1,0:T(4,128)S(1)}, u32[]{:S(2)}, u32[]{:S(2)}) %all-to-all-start.1) | async-done | bytes 1048608 | tf_op jit(solution)/shard_map/all_to_all | solution.py:263
  150.2 3.2 %shard_map.66 = f32[2,16,64,128]{3,2,1,0:T(8,128)} custom-call(f32[2048,128]{1,0:T(8,128)S(1)} %bitcast.7, f32[128,128]{1,0:T(8,128)S(1)} %select_multiply_fusion.y_matrix_ref, f32[256,256]{1,0:T(8,128)S(1)} %multiply_select_fusion.x_matrix_ref), custom_call_target="tpu_custom_call" | custom-call | tf_op jit(solution)/shard_map/pallas_call | solution.py:238
  (11 shorter events, 0.1 us)
Async XLA Ops:
  0.0 1.1 copy-start.2
  1.1 1.1 copy-start.3
  2.1 1.1 copy-start.4
  3.2 1.0 copy-start.5
  4.2 75.6 %copy-start.1 = (bf16[1024,512]{1,0:T(8,128)(2,1)S(1)}, bf16[1024,512]{1,0:T(8,128)(2,1)}, u32[]{:S(2)}) copy-start(bf16[1024,512]{1,0:T(8,128)(2,1)} %constant.149.clone.low_ref) | copy-start | bytes 3145732
  10.0 69.8 %copy-start = (bf16[1024,512]{1,0:T(8,128)(2,1)S(1)}, bf16[1024,512]{1,0:T(8,128)(2,1)}, u32[]{:S(2)}) copy-start(bf16[1024,512]{1,0:T(8,128)(2,1)} %constant.148.clone.high_ref) | copy-start | bytes 3145732
  82.7 67.5 %all-to-all-start.1 = ((f32[512,4,128]{2,1,0:T(4,128)}), f32[512,4,128]{2,1,0:T(4,128)S(1)}, u32[]{:S(2)}, u32[]{:S(2)}) async-start(f32[512,4,128]{2,1,0:T(4,128)} %bitcast.2), calls=%async_computation.1 | async-start | bytes 2097152 | tf_op jit(solution)/shard_map/all_to_all | solution.py:263

commit v3 on v2

v3 whole, which is shorter than its diff:
```python
import math

import jax
import jax.numpy as jnp
import ml_dtypes
import numpy as np
from jax import lax
from jax.experimental import pallas as pl
from jax.experimental.pallas import tpu as pltpu
from jax.sharding import PartitionSpec as P

NX = 2048
NY = 2048
PLANES = 16
LY = 64
LX = 128
N_GX = 16
N_GY = 32
N_ALL = N_GX * N_GY
F32 = jnp.float32
BF16 = jnp.bfloat16

QUAD = 7.0 / 16.0 - 7.0 / 9.0
LIN = 7.0 / 9.0 - QUAD

BLOCKS = 8
BLOCK = LX // BLOCKS
PER_PLANE = N_ALL // PLANES
WIDE = PER_PLANE - BLOCKS
HALF = LY // 2
GROUP = 4


def reversal(index, digits):
    total = 0
    for place in range(digits):
        total = total * 2 + ((index >> place) & 1)
    return total


def split(value):
    high = value.astype(BF16)
    return high, (value - high.astype(F32)).astype(BF16)


def dot3(left, right):
    left_high, left_low = left
    right_high, right_low = right
    return (
        jnp.dot(left_high, right_high, preferred_element_type=F32)
        + jnp.dot(left_high, right_low, preferred_element_type=F32)
        + jnp.dot(left_low, right_high, preferred_element_type=F32)
    )


def flux(liquid_a, liquid_b, field_a, field_b):
    count = liquid_a + liquid_b
    return count * (LIN + QUAD * count) * (field_b - field_a)


def roll(value, by, axis):
    by = by % value.shape[axis]
    return pltpu.roll(value, by, axis) if by else value


def lanes_of(rows):
    return lax.broadcasted_iota(jnp.int32, (rows, LX), 1)


def rows_of(rows):
    return lax.broadcasted_iota(jnp.int32, (rows, LX), 0)


def turn(value, block, sign, offset):
    value = roll(value, -offset, 0)
    for bit in (1, 2, 4):
        value = jnp.where((block & bit) != 0, roll(value, -sign * bit, 0), value)
    return value


def cell_block():
    return ((lanes_of(BLOCKS) + BLOCK // 2) // BLOCK) & (BLOCKS - 1)


def face_block(rows):
    lane = (lanes_of(rows) + LX - 1) & (LX - 1)
    return lane // BLOCK, lane % BLOCK < BLOCK // 2


def stencil_kernel(
    now_hbm,
    prev_hbm,
    phase_hbm,
    div_hbm,
    out_hbm,
    now_ref,
    prev_ref,
    phase_ref,
    div_ref,
    out,
    sems,
    out_sems,
):
    copies, sent = [], []
    for g in range(PLANES // GROUP):
        first = GROUP * g + 2 if g else 0
        planes = pl.ds(first, GROUP * (g + 1) + 2 - first)
        inner = pl.ds(GROUP * g, GROUP)
        copies.append(
            [
                pltpu.make_async_copy(source.at[part], target.at[part], sems.at[g, a])
                for a, (source, target, part) in enumerate(
                    (
                        (now_hbm, now_ref, planes),
                        (prev_hbm, prev_ref, planes),
                        (phase_hbm, phase_ref, planes),
                        (div_hbm, div_ref, inner),
                    )
                )
            ]
        )
        for copy in copies[-1]:
            copy.start()

    lane = lanes_of(LY)
    row = rows_of(LY)
    edge_lane = (lane == 0) | (lane == LX - 1)
    sub = rows_of(BLOCKS)
    block = cell_block()
    line_block, in_half = face_block(BLOCKS)

    def plane(k):
        return 2.0 * now_ref[k] - prev_ref[k], phase_ref[k].astype(F32)

    for k in range(PLANES):
        if k % GROUP == 0:
            for copy in copies[k // GROUP]:
                copy.wait()
        if k == 0:
            field_before, liquid_before = plane(0)
            field, liquid = plane(1)
            flux_z = flux(liquid_before, liquid, field_before, field)
        field_after, liquid_after = plane(k + 2)
        flux_z_upper = flux(liquid, liquid_after, field, field_after)
        total = div_ref[k] + (flux_z_upper - flux_z)
        upper = flux(liquid, roll(liquid, -1, 1), field, roll(field, -1, 1))
        upper = jnp.where(lane == LX - 1, 0.0, upper)
        total = total + (upper - roll(upper, 1, 1))
        upper = flux(liquid, roll(liquid, -1, 0), field, roll(field, -1, 0))
        upper = jnp.where(row == LY - 1, 0.0, upper)
        total = total + (upper - roll(upper, 1, 0))
        ends = jnp.where(edge_lane, field, 0.0)
        wet_ends = jnp.where(edge_lane, liquid, 0.0)
        first = ends[:HALF] + roll(wet_ends[:HALF], -2, 1)
        second = roll(ends[HALF:], -4, 1) + roll(wet_ends[HALF:], -6, 1)
        lines = jnp.broadcast_to(liquid[LY - 1 : LY], (BLOCKS, LX))
        for f, line in ((2, field[LY - 1 : LY]), (1, liquid[0:1]), (0, field[0:1])):
            lines = jnp.where(sub < 2 * f + 2, jnp.broadcast_to(line, (BLOCKS, LX)), lines)
        lines = roll(lines, 9, 1)
        for bit, by in ((1, 8), (2, 32), (4, 64)):
            lines = jnp.where((sub & bit) != 0, roll(lines, by, 1), lines)
        lines = turn(jnp.where(in_half, lines, 0.0), line_block, 1, 0)

        start = k * PER_PLANE * 3
        out[pl.ds(start, BLOCKS, stride=3), :] = turn(total[:BLOCKS], block, 1, 0)
        out[pl.ds(start + 1, BLOCKS, stride=3), :] = turn(total[LY - BLOCKS :], block, 1, 7)
        out[pl.ds(start + 2, BLOCKS, stride=3), :] = (
            first[:BLOCKS] + roll(second[WIDE:], 1, 0) + lines
        )
        start += BLOCKS * 3
        out[pl.ds(start, WIDE, stride=3), :] = total[BLOCKS:HALF]
        out[pl.ds(start + 1, WIDE, stride=3), :] = total[HALF : HALF + WIDE]
        out[pl.ds(start + 2, WIDE, stride=3), :] = first[BLOCKS:] + second[:WIDE]
        field, liquid, flux_z = field_after, liquid_after, flux_z_upper
        if k % GROUP == GROUP - 1:
            g = k // GROUP
            rows = pl.ds(g * GROUP * PER_PLANE * 3, GROUP * PER_PLANE * 3)
            sent.append(pltpu.make_async_copy(out.at[rows], out_hbm.at[rows], out_sems.at[g]))
            sent[-1].start()
    for copy in sent:
        copy.wait()


def device_kernel(x_ref, high_ref, low_ref, out, cells):
    last_lane = lanes_of(N_GY) == LX - 1
    own = (BLOCKS - lax.axis_index("gy") % BLOCKS) % BLOCKS
    line_block, in_half = face_block(N_GY)
    first_half = in_half & (line_block == own)
    second_half = in_half & (line_block == (own + 1) % BLOCKS)

    def group(g, r):
        return x_ref[pl.ds((g % N_GX) * N_GY * 3 + r, N_GY, stride=3), :]

    def x_flux(here, there, t):
        through = flux(
            roll(here, 2 + 4 * t, 1),
            roll(there, 1 + 4 * t, 1),
            roll(here, 4 * t, 1),
            roll(there, 4 * t - 1, 1),
        )
        return jnp.where(last_lane, through, 0.0)

    last = group(N_GX - 1, 2)
    here = group(0, 2)
    entering = [x_flux(last, here, t) for t in range(2)]
    for g in range(N_GX):
        there = group(g + 1, 2)
        first, second = group(g, 0), group(g, 1)
        leaving = [x_flux(here, there, t) for t in range(2)]
        first = first + (leaving[0] - roll(entering[0], 1, 1))
        second = second + (leaving[1] - roll(entering[1], 1, 1))
        after = roll(here, -1, 0)
        through = flux(roll(here, -96, 1), roll(after, -32, 1), roll(here, -64, 1), after)
        through = roll(jnp.where(first_half, through, 0.0), -9, 1) + roll(
            jnp.where(second_half, through, 0.0), -17, 1
        )
        cells[pl.ds(g * N_GY, N_GY), :LX] = first - roll(through, 1, 0)
        cells[pl.ds(g * N_GY, N_GY), LX:] = second + through
        here, entering = there, leaving

    right = split(cells[...])
    for part in range(2):
        rows = pl.ds(part * N_ALL, N_ALL)
        result = dot3((high_ref[rows, :], low_ref[rows, :]), right)
        out[pl.ds(2 * part, N_ALL, stride=4), :] = result[:, :LX]
        out[pl.ds(2 * part + 1, N_ALL, stride=4), :] = result[:, LX:]


def local_kernel(x_ref, y_matrix_ref, x_matrix_ref, out_hbm, out, sems):
    y_matrix = split(y_matrix_ref[...])
    x_matrix = split(x_matrix_ref[...])
    block = cell_block()
    copies = []
    for k in range(PLANES):
        start = k * 2 * LY
        lines = [
            turn(x_ref[pl.ds(start + kind, BLOCKS, stride=4), :], block, -1, kind & 1)
            for kind in range(4)
        ]
        lines.append(x_ref[pl.ds(start + 4 * BLOCKS, 4 * WIDE), :])
        lines = dot3(y_matrix, split(jnp.concatenate(lines, axis=0)))
        lines = jnp.concatenate([lines[:LY], lines[LY:]], axis=1)
        modes = dot3(split(lines), x_matrix)
        out[0, k] = modes[:, :LX]
        out[1, k] = modes[:, LX:]
        if k % GROUP == GROUP - 1:
            g = k // GROUP
            for part in range(2):
                planes = (part, pl.ds(g * GROUP, GROUP))
                copies.append(
                    pltpu.make_async_copy(
                        out.at[planes], out_hbm.at[planes], sems.at[g, part]
                    )
                )
                copies[-1].start()
    for copy in copies:
        copy.wait()


def device_tables():
    source = np.arange(N_ALL)
    rev_p = np.array([reversal(i, 4) for i in range(N_GX)])
    rev_q = np.array([reversal(i, 5) for i in range(N_GY)])
    kx = rev_p[source // N_GY][:, None]
    ky = rev_q[source % N_GY][:, None]
    turns = (2 * kx * (source // N_GY)[None] + ky * (source % N_GY)[None]) % N_GY
    angle = turns * (2.0 * math.pi / N_GY)
    table = np.concatenate([np.cos(angle), -np.sin(angle)])
    high = table.astype(ml_dtypes.bfloat16)
    return high, (table - high.astype(np.float64)).astype(ml_dtypes.bfloat16)


def cos_sin(place, mode, length):
    angle = ((place * mode) % length).astype(F32) * (2.0 * math.pi / length)
    return jnp.cos(angle), jnp.sin(angle)


def local_tables():
    rp = reversal(lax.axis_index("gx"), 4)
    rq = reversal(lax.axis_index("gy"), 5)
    line = lax.broadcasted_iota(jnp.int32, (2 * LY, 2 * LY), 0)
    col = lax.broadcasted_iota(jnp.int32, (2 * LY, 2 * LY), 1)
    rest = col - 4 * BLOCKS
    in_block = rest < 0
    part_in = jnp.where(in_block, col >> 4, rest >> 1) & 1
    place = jnp.where(
        in_block,
        (col & 7) + (LY - BLOCKS) * ((col >> 3) & 1),
        BLOCKS + (rest >> 2) + WIDE * (rest & 1),
    )
    cosine, sine = cos_sin(place, 32 * (line % LY) + rq, NY)
    part_out = line // LY
    sign = jnp.where(part_out < part_in, 1.0, -1.0)
    y_matrix = jnp.where(part_out == part_in, cosine, sign * sine) * (1.0 / math.sqrt(NX * NY))
    line = lax.broadcasted_iota(jnp.int32, (2 * LX, 2 * LX), 0)
    col = lax.broadcasted_iota(jnp.int32, (2 * LX, 2 * LX), 1)
    cosine, sine = cos_sin(line % LX, 16 * (col % LX) + rp, NX)
    part_in, part_out = line // LX, col // LX
    sign = jnp.where(part_out < part_in, 1.0, -1.0)
    x_matrix = jnp.where(part_out == part_in, cosine, sign * sine)
    return y_matrix, x_matrix


def call(kernel, outs, *args, scratch=(), in_hbm=False, out_hbm=False, mib=40):
    def spec(hbm):
        return pl.BlockSpec(memory_space=pltpu.HBM if hbm else pltpu.VMEM)

    return pl.pallas_call(
        kernel,
        out_shape=outs,
        in_specs=[spec(in_hbm)] * len(args),
        out_specs=spec(out_hbm),
        scratch_shapes=scratch,
        compiler_params=pltpu.CompilerParams(vmem_limit_bytes=mib * 1024 * 1024),
    )(*args)


def shape(*dims):
    return jax.ShapeDtypeStruct(dims, F32)


def body(p_now, p_prev, phase, div_star):
    padded = (PLANES + 2, LY, LX)
    chunks = call(
        stencil_kernel,
        shape(3 * N_ALL, LX),
        p_now,
        p_prev,
        phase,
        div_star,
        scratch=[
            pltpu.VMEM(padded, F32),
            pltpu.VMEM(padded, F32),
            pltpu.VMEM(padded, jnp.int32),
            pltpu.VMEM((PLANES, LY, LX), F32),
            pltpu.VMEM((3 * N_ALL, LX), F32),
            pltpu.SemaphoreType.DMA((PLANES // GROUP, 4)),
            pltpu.SemaphoreType.DMA((PLANES // GROUP,)),
        ],
        in_hbm=True,
        out_hbm=True,
        mib=60,
    )
    everywhere = ("gx", "gy")
    chunks = lax.all_to_all(chunks.reshape(N_ALL, 1, 3 * LX), everywhere, 0, 0, tiled=True)
    high, low = device_tables()
    modes = call(
        device_kernel,
        shape(4 * N_ALL, LX),
        chunks.reshape(3 * N_ALL, LX),
        jnp.asarray(high),
        jnp.asarray(low),
        scratch=[pltpu.VMEM((N_ALL, 2 * LX), F32)],
    )
    back = lax.all_to_all(modes.reshape(N_ALL, 4, LX), everywhere, 0, 0, tiled=True)
    y_matrix, x_matrix = local_tables()
    result = call(
        local_kernel,
        shape(2, PLANES, LY, LX),
        back.reshape(4 * N_ALL, LX),
        y_matrix,
        x_matrix,
        scratch=[
            pltpu.VMEM((2, PLANES, LY, LX), F32),
            pltpu.SemaphoreType.DMA((PLANES // GROUP, 2)),
        ],
        out_hbm=True,
    )
    return result.reshape(2, PLANES, 1, LY, 1, LX)


def solution(mesh):
    spec = P(None, "gy", "gx")
    return jax.shard_map(
        body,
        mesh=mesh,
        in_specs=(spec, spec, spec, spec),
        out_specs=P(None, None, "gy", None, "gx", None),
        check_vma=False,
    )
```

time: 154 us -> 147 us (0.955)
  local copies, waits for them, and re-layouts: 4.24 us -> 0.01 us
  Pallas kernels: 11.9 us -> 9.38 us
    unnamed x12 -> x4, local copies, waits for them, and re-layouts: 4.24 us -> 0.01 us
    pallas_call x3, Pallas kernels: 11.9 us -> 9.38 us  [call(): pl.pallas_call(kernel, out_shape=outs, in_specs=[spec(in_hbm)] * len(args...]
where the time goes in v3:
time: 147 us
  blocking collectives  70 us (48%)
  waiting for transfers between devices  55.3 us (38%)
  starting transfers between devices  9.66 us (7%)
  Pallas kernels  9.38 us (6%)
  other arithmetic  2.42 us (2%)
    all_to_all x1, blocking collectives, body(): lax.all_to_all(chunks.reshape(N_ALL, 1, 3 * LX), everywhere, 0, 0, tiled=...  70 us
    all_to_all x1, waiting for transfers between devices, body(): lax.all_to_all(modes.reshape(N_ALL, 4, LX), everywhere, 0, 0, tiled=True)  55.3 us
    all_to_all x1, starting transfers between devices, body(): lax.all_to_all(modes.reshape(N_ALL, 4, LX), everywhere, 0, 0, tiled=True)  9.66 us
    pallas_call x3, Pallas kernels, call(): pl.pallas_call(kernel, out_shape=outs, in_specs=[spec(in_hbm)] * len(args...  9.38 us
  transfers between devices with their start and end apart: 1, of which 1 were waited for; matrix products, arithmetic and copies ran while one was open for 2% of the time, Pallas kernels for 0%

profile of v3, /device:TPU:2, one launch (start us, length us, event | category | flops | bytes accessed | tf_op | source)
XLA Modules:
  0.0 146.9 jit_solution(3914676220998733786)
XLA Ops:
  0.0 0.0 copy-start.1
  0.0 3.6 %shard_map.64 = f32[1536,128]{1,0:T(8,128)} custom-call(f32[18,64,128]{2,1,0:T(8,128)} %now_hbm.1, f32[18,64,128]{2,1,0:T(8,128)} %prev_hbm.1, s32[18,64,128]{2,1,0:T(8,128)} %phase_hbm.1, f32[16,64,128]{2,1,0:T(8,128)} %div_hbm.1), custom_call_target="tpu_custom_call" | custom-call | tf_op jit(solution)/shard_map/pallas_call | solution.py:308
  3.6 0.0 copy-start
  3.6 70.0 %all_to_all.10 = f32[512,1,384]{2,1,0:T(1,128)S(1)} all-to-all(f32[512,1,384]{2,1,0:T(1,128)} %bitcast.9), channel_id=1, replica_groups=mesh['gx'=16,'gy'=32] {'gx','gy'}, dimensions={0} | all-to-all | bytes 1572864 | tf_op jit(solution)/shard_map/all_to_all | solution.py:345
  73.6 0.0 copy-done.1
  73.6 0.0 copy-done
  73.6 2.9 %shard_map.65 = f32[2048,128]{1,0:T(8,128)} custom-call(f32[1536,128]{1,0:T(8,128)S(1)} %bitcast.8, bf16[1024,512]{1,0:T(8,128)(2,1)S(1)} %copy-done, bf16[1024,512]{1,0:T(8,128)(2,1)S(1)} %copy-done.1), custom_call_target="tpu_custom_call" | custom-call | tf_op jit(solution)/shard_map/pallas_call | solution.py:308
  76.4 9.7 %all-to-all-start.1 = ((f32[512,4,128]{2,1,0:T(4,128)}), f32[512,4,128]{2,1,0:T(4,128)S(1)}, u32[]{:S(2)}, u32[]{:S(2)}) async-start(f32[512,4,128]{2,1,0:T(4,128)} %bitcast.2), calls=%async_computation.1 | async-start | bytes 2097152 | tf_op jit(solution)/shard_map/all_to_all | solution.py:355
  86.2 0.4 select_multiply_fusion.y_matrix_ref
  86.6 2.0 %multiply_select_fusion.x_matrix_ref = f32[256,256]{1,0:T(8,128)S(1)} fusion(s32[]{:T(128)S(6)} %add.98, s32[256]{0:T(256)S(1)} %get-tuple-element.16, s32[256]{0:T(256)S(1)} %get-tuple-element.19, s32[256]{0:T(256)S(1)} %get-tuple-element.15, s32[256]{0:T(256)S(1)} %get-tuple-element.20, pred[256]{0:T(512)(128)(4,1)S(1)} %get-tuple-element.17, ...), kind=kLoop, calls=%fused_computation.8 | loop fusion | flops 1638400 | bytes 266756 | tf_op jit(solution)/shard_map/jit(_where)/select_n | solution.py:300
  88.6 55.3 %all-to-all-done.1 = f32[512,4,128]{2,1,0:T(4,128)S(1)} async-done(((f32[512,4,128]{2,1,0:T(4,128)}), f32[512,4,128]{2,1,0:T(4,128)S(1)}, u32[]{:S(2)}, u32[]{:S(2)}) %all-to-all-start.1) | async-done | bytes 1048608 | tf_op jit(solution)/shard_map/all_to_all | solution.py:355
  143.9 2.9 %shard_map.66 = f32[2,16,64,128]{3,2,1,0:T(8,128)} custom-call(f32[2048,128]{1,0:T(8,128)S(1)} %bitcast.7, f32[128,128]{1,0:T(8,128)S(1)} %select_multiply_fusion.y_matrix_ref, f32[256,256]{1,0:T(8,128)S(1)} %multiply_select_fusion.x_matrix_ref), custom_call_target="tpu_custom_call" | custom-call | tf_op jit(solution)/shard_map/pallas_call | solution.py:308
  (9 shorter events, 0.1 us)
Async XLA Ops:
  0.0 73.6 %copy-start.1 = (bf16[1024,512]{1,0:T(8,128)(2,1)S(1)}, bf16[1024,512]{1,0:T(8,128)(2,1)}, u32[]{:S(2)}) copy-start(bf16[1024,512]{1,0:T(8,128)(2,1)} %constant.142.clone.low_ref) | copy-start | bytes 3145732
  3.6 70.0 %copy-start = (bf16[1024,512]{1,0:T(8,128)(2,1)S(1)}, bf16[1024,512]{1,0:T(8,128)(2,1)}, u32[]{:S(2)}) copy-start(bf16[1024,512]{1,0:T(8,128)(2,1)} %constant.141.clone.high_ref) | copy-start | bytes 3145732
  76.4 67.5 %all-to-all-start.1 = ((f32[512,4,128]{2,1,0:T(4,128)}), f32[512,4,128]{2,1,0:T(4,128)S(1)}, u32[]{:S(2)}, u32[]{:S(2)}) async-start(f32[512,4,128]{2,1,0:T(4,128)} %bitcast.2), calls=%async_computation.1 | async-start | bytes 2097152 | tf_op jit(solution)/shard_map/all_to_all | solution.py:355

commit v4 on v3

v4 whole, which is shorter than its diff:
```python
import functools
import math

import jax
import jax.numpy as jnp
import ml_dtypes
import numpy as np
from jax import lax
from jax.experimental import pallas as pl
from jax.experimental.pallas import tpu as pltpu
from jax.sharding import Mesh
from jax.sharding import PartitionSpec as P

NX = 2048
NY = 2048
PLANES = 16
LY = 64
LX = 128
N_GX = 16
N_GY = 32
N_ALL = N_GX * N_GY
N_CHIP = N_ALL // 2
F32 = jnp.float32
BF16 = jnp.bfloat16

CHIPS = ("zh", "x", "zl", "y")
EVERYWHERE = ("zh", "x", "c", "zl", "y")

QUAD = 7.0 / 16.0 - 7.0 / 9.0
LIN = 7.0 / 9.0 - QUAD

BLOCKS = 16
BLOCK = LX // BLOCKS
PER_PLANE = N_ALL // PLANES
WIDE = PER_PLANE - BLOCKS
HALF = LY // 2
SHARE = PLANES // 2
GROUP = 4
QUARTER = LX // 4


def reversal(index, digits):
    total = 0
    for place in range(digits):
        total = total * 2 + ((index >> place) & 1)
    return total


def split(value):
    high = value.astype(BF16)
    return high, (value - high.astype(F32)).astype(BF16)


def dot3(left, right):
    left_high, left_low = left
    right_high, right_low = right
    return (
        jnp.dot(left_high, right_high, preferred_element_type=F32)
        + jnp.dot(left_high, right_low, preferred_element_type=F32)
        + jnp.dot(left_low, right_high, preferred_element_type=F32)
    )


def weighted(count, difference):
    return count * (LIN + QUAD * count) * difference


def flux(liquid_a, liquid_b, field_a, field_b):
    return weighted(liquid_a + liquid_b, field_b - field_a)


def roll(value, by, axis):
    if isinstance(by, int):
        by = by % value.shape[axis]
        return pltpu.roll(value, by, axis) if by else value
    return pltpu.roll(value, by & (value.shape[axis] - 1), axis)


def lanes_of(rows):
    return lax.broadcasted_iota(jnp.int32, (rows, LX), 1)


def rows_of(rows):
    return lax.broadcasted_iota(jnp.int32, (rows, LX), 0)


def within(lane, start, count):
    return ((lane - start) & (LX - 1)) < count


def turn(value, block, sign, offset):
    value = roll(value, -offset, 0)
    for bit in (1, 2, 4, 8):
        value = jnp.where((block & bit) != 0, roll(value, -sign * bit, 0), value)
    return value


def cell_block():
    return ((lanes_of(BLOCKS) + BLOCK // 2) // BLOCK) & (BLOCKS - 1)


def stencil_kernel(
    give,
    now_hbm,
    prev_hbm,
    phase_hbm,
    div_hbm,
    *refs,
):
    if give:
        out_hbm, now_ref, prev_ref, phase_ref, div_ref, out, sems, out_sems = refs
    else:
        (
            other_hbm, out_hbm, now_ref, prev_ref, phase_ref, div_ref, out, sems, out_sems,
            other, other_sem,
        ) = refs
    core = lax.axis_index("c")
    base = SHARE * (1 - core if give else core)
    copies, sent = [], []
    for g in range(SHARE // GROUP):
        first = GROUP * g + 2 if g else 0
        count = GROUP * (g + 1) + 2 - first
        copies.append(
            [
                pltpu.make_async_copy(
                    source.at[pl.ds(base + start, size)],
                    target.at[pl.ds(start, size)],
                    sems.at[g, a],
                )
                for a, (source, target, start, size) in enumerate(
                    (
                        (now_hbm, now_ref, first, count),
                        (prev_hbm, prev_ref, first, count),
                        (phase_hbm, phase_ref, first, count),
                        (div_hbm, div_ref, GROUP * g, GROUP),
                    )
                )
            ]
        )
        for copy in copies[-1]:
            copy.start()
    if not give:
        other_copy = pltpu.make_async_copy(other_hbm, other, other_sem.at[0])
        other_copy.start()

    lane = lanes_of(LY)
    row = rows_of(LY)
    sub = rows_of(8)
    block = cell_block()
    lane_in = lanes_of(PER_PLANE)
    slots = [(1 - core) * 16, (1 - core) * 16, core * 16, core * 16]
    x_lanes = [
        [within(lane_in, QUARTER * q + slots[q] + 8 + 2 * t, 2) for t in range(2)] for q in range(4)
    ]
    owner = rows_of(BLOCKS) * BLOCK
    y_lanes = [within(lanes_of(BLOCKS), QUARTER * f + 16 * core + owner, BLOCK) for f in range(4)]

    def plane(k):
        return 2.0 * now_ref[k] - prev_ref[k], phase_ref[k].astype(F32)

    for k in range(SHARE):
        if k % GROUP == 0:
            for copy in copies[k // GROUP]:
                copy.wait()
        if k == 0:
            field_before, liquid_before = plane(0)
            field, liquid = plane(1)
            flux_z = flux(liquid_before, liquid, field_before, field)
        field_after, liquid_after = plane(k + 2)
        flux_z_upper = flux(liquid, liquid_after, field, field_after)
        total = div_ref[k] + (flux_z_upper - flux_z)
        upper = flux(liquid, roll(liquid, -1, 1), field, roll(field, -1, 1))
        upper = jnp.where(lane == LX - 1, 0.0, upper)
        total = total + (upper - roll(upper, 1, 1))
        upper = flux(liquid, roll(liquid, -1, 0), field, roll(field, -1, 0))
        upper = jnp.where(row == LY - 1, 0.0, upper)
        total = total + (upper - roll(upper, 1, 0))
        faces = jnp.zeros((PER_PLANE, LX), F32)
        for q, column in enumerate(
            (field[:, 0:1], liquid[:, 0:1], field[:, LX - 1 : LX], liquid[:, LX - 1 : LX])
        ):
            column = jnp.broadcast_to(column, (LY, LX))
            faces = jnp.where(x_lanes[q][0], column[:HALF], faces)
            second = jnp.concatenate(
                [roll(column[HALF + WIDE :], 1, 0), column[HALF : HALF + WIDE]], axis=0
            )
            faces = jnp.where(x_lanes[q][1], second, faces)
        faces = pltpu.roll(faces, 0, 1, stride=BLOCK, stride_axis=0)
        lines = jnp.broadcast_to(liquid[LY - 1 : LY], (8, LX))
        for f, line in ((2, field[LY - 1 : LY]), (1, liquid[0:1]), (0, field[0:1])):
            lines = jnp.where(sub <= f, jnp.broadcast_to(line, (8, LX)), lines)
        lines = roll(lines, BLOCK // 2 + 16 * core, 1)
        for bit in (1, 2):
            lines = jnp.where((sub & bit) != 0, roll(lines, QUARTER * bit, 1), lines)
        y_faces = faces[:BLOCKS]
        for f in range(4):
            y_faces = jnp.where(
                y_lanes[f], jnp.broadcast_to(lines[f : f + 1], (BLOCKS, LX)), y_faces
            )

        rows = (
            jnp.concatenate([turn(total[:BLOCKS], block, -1, 0), total[BLOCKS:HALF]], axis=0),
            jnp.concatenate(
                [turn(total[HALF + WIDE :], block, -1, 15), total[HALF : HALF + WIDE]], axis=0
            ),
            jnp.concatenate([y_faces, faces[BLOCKS:]], axis=0),
        )
        if give:
            for r in range(3):
                out[pl.ds(k * PER_PLANE * 3 + r, PER_PLANE, stride=3), :] = rows[r]
        else:
            if k == 0:
                other_copy.wait()
            start = k * PER_PLANE * 3
            theirs = [other[pl.ds(start + r, PER_PLANE, stride=3), :] for r in range(3)]
            start = k * PER_PLANE * 5
            for r in range(2):
                lower = jnp.where(core == 0, rows[r], theirs[r])
                upper = jnp.where(core == 0, theirs[r], rows[r])
                out[pl.ds(start + r, PER_PLANE, stride=5), :] = lower
                out[pl.ds(start + 2 + r, PER_PLANE, stride=5), :] = upper
            out[pl.ds(start + 4, PER_PLANE, stride=5), :] = rows[2] + theirs[2]
        field, liquid, flux_z = field_after, liquid_after, flux_z_upper
        if k % GROUP == GROUP - 1:
            g = k // GROUP
            size = GROUP * PER_PLANE * (3 if give else 5)
            part = pl.ds(g * size, size)
            sent.append(pltpu.make_async_copy(out.at[part], out_hbm.at[part], out_sems.at[g]))
            sent[-1].start()
    for copy in sent:
        copy.wait()


def device_kernel(x_ref, high_ref, low_ref, out, cells):
    lane = lanes_of(N_GY)
    in_y = (lane & 15) < BLOCK
    next_chip = (lane & 16) != 0
    at_last, at_first = lane == LX - 1, lane == 0
    own = (lax.axis_index("zl") * 4 + lax.axis_index("y")) % BLOCKS * BLOCK
    groups = N_GX // 2

    def rows(g, r):
        return x_ref[pl.ds((g % groups) * N_GY * 5 + r, N_GY, stride=5), :]

    def aligned(g):
        return roll(rows(g, 4), LX - own, 1)

    def face_flux(here, there):
        lower = jnp.where(in_y, roll(here, -1, 0), jnp.where(next_chip, there, here))
        upper = roll(here, -2 * QUARTER, 1)
        return weighted(roll(upper + lower, -QUARTER, 1), lower - upper)

    def x_parts(through, c):
        return [roll(through, LX - 1 - (16 * c + 8 + 2 * t), 1) for t in range(2)]

    last, here = aligned(groups - 1), aligned(0)
    entering = x_parts(face_flux(last, here), 1)
    for g in range(groups):
        there = aligned(g + 1)
        through = face_flux(here, there)
        leaving = [x_parts(through, c) for c in range(2)]
        for c in range(2):
            along_y = jnp.where(within(lane, 16 * c, BLOCK), through, 0.0)
            along_y = roll(along_y, own + (LX - BLOCK // 2 - 16 * c), 1)
            before = leaving[0] if c else entering
            part = [
                rows(g, 2 * c + t)
                + jnp.where(at_last, leaving[c][t], 0.0)
                - jnp.where(at_first, before[t], 0.0)
                for t in range(2)
            ]
            place = pl.ds(c * N_CHIP + g * N_GY, N_GY)
            cells[place, :LX] = part[0] - roll(along_y, 1, 0)
            cells[place, LX:] = part[1] + along_y
        here, entering = there, leaving[1]

    right = split(cells[...])
    for part in range(2):
        table = pl.ds(part * N_ALL, N_ALL)
        result = dot3((high_ref[table, :], low_ref[table, :]), right)
        out[pl.ds(2 * part, N_ALL, stride=4), :] = result[:, :LX]
        out[pl.ds(2 * part + 1, N_ALL, stride=4), :] = result[:, LX:]


def local_kernel(x_ref, y_matrix_ref, x_matrix_ref, out_hbm, out, sems):
    y_matrix = split(y_matrix_ref[...])
    x_matrix = split(x_matrix_ref[...])
    block = cell_block()
    copies = []
    for k in range(PLANES):
        start = (2 * (k % SHARE) + k // SHARE) * 2 * LY
        lines = [
            turn(x_ref[pl.ds(start + kind, BLOCKS, stride=4), :], block, 1, kind & 1)
            for kind in range(4)
        ]
        lines.append(x_ref[pl.ds(start + 4 * BLOCKS, 4 * WIDE), :])
        lines = dot3(y_matrix, split(jnp.concatenate(lines, axis=0)))
        lines = jnp.concatenate([lines[:LY], lines[LY:]], axis=1)
        modes = dot3(split(lines), x_matrix)
        out[0, k] = modes[:, :LX]
        out[1, k] = modes[:, LX:]
        if k % GROUP == GROUP - 1:
            g = k // GROUP
            for part in range(2):
                planes = (part, pl.ds(g * GROUP, GROUP))
                copies.append(
                    pltpu.make_async_copy(out.at[planes], out_hbm.at[planes], sems.at[g, part])
                )
                copies[-1].start()
    for copy in copies:
        copy.wait()


def device_tables():
    dest = np.arange(N_ALL)
    rev_p = np.array([reversal(i, 4) for i in range(N_GX)])
    rev_q = np.array([reversal(i, 5) for i in range(N_GY)])
    kx = rev_p[dest // N_GY][:, None]
    ky = rev_q[dest % N_GY][:, None]
    source = np.arange(N_ALL)
    gx = (2 * (source % N_CHIP // N_GY) + source // N_CHIP)[None]
    gy = (source % N_GY)[None]
    angle = (2 * kx * gx + ky * gy) % N_GY * (2.0 * math.pi / N_GY)
    table = np.concatenate([np.cos(angle), -np.sin(angle)])
    high = table.astype(ml_dtypes.bfloat16)
    return high, (table - high.astype(np.float64)).astype(ml_dtypes.bfloat16)


def cos_sin(place, mode, length):
    angle = ((place * mode) % length).astype(F32) * (2.0 * math.pi / length)
    return jnp.cos(angle), jnp.sin(angle)


def local_tables():
    rp = reversal(lax.axis_index(("zh", "x", "c")), 4)
    rq = reversal(lax.axis_index(("zl", "y")), 5)
    line = lax.broadcasted_iota(jnp.int32, (2 * LY, 2 * LY), 0)
    col = lax.broadcasted_iota(jnp.int32, (2 * LY, 2 * LY), 1)
    rest = col - 4 * BLOCKS
    in_block = rest < 0
    part_in = jnp.where(in_block, col // (2 * BLOCKS), rest >> 1) & 1
    place = jnp.where(
        in_block,
        col % BLOCKS + (LY - BLOCKS) * (col // BLOCKS & 1),
        BLOCKS + (rest >> 2) + WIDE * (rest & 1),
    )
    cosine, sine = cos_sin(place, 32 * (line % LY) + rq, NY)
    part_out = line // LY
    sign = jnp.where(part_out < part_in, 1.0, -1.0)
    y_matrix = jnp.where(part_out == part_in, cosine, sign * sine) * (1.0 / math.sqrt(NX * NY))
    line = lax.broadcasted_iota(jnp.int32, (2 * LX, 2 * LX), 0)
    col = lax.broadcasted_iota(jnp.int32, (2 * LX, 2 * LX), 1)
    cosine, sine = cos_sin(line % LX, 16 * (col % LX) + rp, NX)
    part_in, part_out = line // LX, col // LX
    sign = jnp.where(part_out < part_in, 1.0, -1.0)
    x_matrix = jnp.where(part_out == part_in, cosine, sign * sine)
    return y_matrix, x_matrix


def call(kernel, outs, *args, scratch=(), in_hbm=False, out_hbm=False, mib=40):
    def spec(hbm):
        return pl.BlockSpec(memory_space=pltpu.HBM if hbm else pltpu.VMEM)

    in_specs = [spec(in_hbm)] * len(args)
    if in_hbm:
        in_specs[4:] = [pl.BlockSpec(memory_space=pl.ANY)] * len(in_specs[4:])

    return pl.pallas_call(
        kernel,
        out_shape=outs,
        in_specs=in_specs,
        out_specs=spec(out_hbm),
        scratch_shapes=scratch,
        compiler_params=pltpu.CompilerParams(vmem_limit_bytes=mib * 1024 * 1024),
    )(*args)


def shape(*dims):
    return jax.ShapeDtypeStruct(dims, F32)


def stencil(give, rows, *args):
    padded = (SHARE + 2, LY, LX)
    scratch = [
        pltpu.VMEM(padded, F32),
        pltpu.VMEM(padded, F32),
        pltpu.VMEM(padded, jnp.int32),
        pltpu.VMEM((SHARE, LY, LX), F32),
        pltpu.VMEM((rows * N_CHIP, LX), F32),
        pltpu.SemaphoreType.DMA((SHARE // GROUP, 4)),
        pltpu.SemaphoreType.DMA((SHARE // GROUP,)),
    ]
    if not give:
        scratch += [pltpu.VMEM((3 * N_CHIP, LX), F32), pltpu.SemaphoreType.DMA((1,))]
    return call(
        functools.partial(stencil_kernel, give),
        shape(rows * N_CHIP, LX),
        *args,
        scratch=scratch,
        in_hbm=True,
        out_hbm=True,
        mib=60,
    )


def body(*args):
    given = stencil(True, 3, *args)
    given = lax.ppermute(given, "c", [(0, 1), (1, 0)])
    chunks = stencil(False, 5, *args, given)
    chunks = lax.all_to_all(chunks.reshape(N_CHIP, 1, 5 * LX), CHIPS, 0, 0, tiled=True)
    high, low = device_tables()
    modes = call(
        device_kernel,
        shape(4 * N_ALL, LX),
        chunks.reshape(5 * N_CHIP, LX),
        jnp.asarray(high),
        jnp.asarray(low),
        scratch=[pltpu.VMEM((N_ALL, 2 * LX), F32)],
    )
    back = lax.all_to_all(modes.reshape(N_ALL, 4, LX), EVERYWHERE, 0, 0, tiled=True)
    y_matrix, x_matrix = local_tables()
    result = call(
        local_kernel,
        shape(2, PLANES, LY, LX),
        back.reshape(4 * N_ALL, LX),
        y_matrix,
        x_matrix,
        scratch=[
            pltpu.VMEM((2, PLANES, LY, LX), F32),
            pltpu.SemaphoreType.DMA((PLANES // GROUP, 2)),
        ],
        out_hbm=True,
    )
    return result.reshape(2, PLANES, 1, LY, 1, LX)


def solution(mesh):
    fine = Mesh(mesh.devices.reshape(2, 4, 2, 8, 4), EVERYWHERE)
    spec = P(None, ("zl", "y"), ("zh", "x", "c"))
    return jax.shard_map(
        body,
        mesh=fine,
        in_specs=(spec, spec, spec, spec),
        out_specs=P(None, None, ("zl", "y"), None, ("zh", "x", "c"), None),
        check_vma=False,
    )
```

time: 147 us -> 151 us (1.027)
  blocking collectives: 70 us -> 62.3 us
  starting transfers between devices: 9.66 us -> 14.6 us
  Pallas kernels: 9.38 us -> 13.2 us
  waiting for transfers between devices: 55.3 us -> 57.2 us
    all_to_all x1, blocking collectives: 70 us -> 62.3 us  [body(): lax.all_to_all(chunks.reshape(N_CHIP, 1, 5 * LX), CHIPS, 0, 0, tiled=True)]
    pallas_call x3 -> x4, Pallas kernels: 9.38 us -> 13.2 us  [call(): pl.pallas_call(kernel, out_shape=outs, in_specs=in_specs, out_specs=spec(...]
    all_to_all x1, starting transfers between devices: 9.66 us -> 12.7 us  [body(): lax.all_to_all(modes.reshape(N_ALL, 4, LX), EVERYWHERE, 0, 0, tiled=True)]
    ppermute x0 -> x1, starting transfers between devices: none -> 1.92 us  [body(): given = lax.ppermute(given, 'c', [(0, 1), (1, 0)])]
    ppermute x0 -> x1, waiting for transfers between devices: none -> 1.9 us  [body(): given = lax.ppermute(given, 'c', [(0, 1), (1, 0)])]
  transfers between devices with their start and end apart: 1 -> 2, of which waited for: 1 -> 2; matrix products, arithmetic and copies ran while one was open for 2% -> 2% of each run, Pallas kernels for 0% -> 0%
where the time goes in v4:
time: 151 us
  blocking collectives  62.3 us (41%)
  waiting for transfers between devices  57.2 us (38%)
  starting transfers between devices  14.6 us (10%)
  Pallas kernels  13.2 us (9%)
  other arithmetic  2.43 us (2%)
    all_to_all x1, blocking collectives, body(): lax.all_to_all(chunks.reshape(N_CHIP, 1, 5 * LX), CHIPS, 0, 0, tiled=True)  62.3 us
    all_to_all x1, waiting for transfers between devices, body(): lax.all_to_all(modes.reshape(N_ALL, 4, LX), EVERYWHERE, 0, 0, tiled=True)  55.3 us
    pallas_call x4, Pallas kernels, call(): pl.pallas_call(kernel, out_shape=outs, in_specs=in_specs, out_specs=spec(...  13.2 us
    all_to_all x1, starting transfers between devices, body(): lax.all_to_all(modes.reshape(N_ALL, 4, LX), EVERYWHERE, 0, 0, tiled=True)  12.7 us
  transfers between devices with their start and end apart: 2, of which 2 were waited for; matrix products, arithmetic and copies ran while one was open for 2% of the time, Pallas kernels for 0%

profile of v4, /device:TPU:2, one launch (start us, length us, event | category | flops | bytes accessed | tf_op | source)
XLA Modules:
  0.0 150.9 jit_solution(11108139600992694710)
XLA Ops:
  0.0 3.9 %shard_map.64 = f32[768,128]{1,0:T(8,128)} custom-call(f32[18,64,128]{2,1,0:T(8,128)} %now_hbm.3, f32[18,64,128]{2,1,0:T(8,128)} %prev_hbm.3, s32[18,64,128]{2,1,0:T(8,128)} %phase_hbm.3, f32[16,64,128]{2,1,0:T(8,128)} %div_hbm.3), custom_call_target="tpu_custom_call" | custom-call | tf_op jit(solution)/shard_map/pallas_call | solution.py:368
  3.9 1.9 %collective-permute-start = (f32[768,128]{1,0:T(8,128)}, f32[768,128]{1,0:T(8,128)S(1)}, u32[]{:S(2)}, u32[]{:S(2)}) collective-permute-start(f32[768,128]{1,0:T(8,128)} %shard_map.64), channel_id=1, source_target_pairs={{0,32},{32,0},{1,33},{33,1},{2,34},{34,2},{3,35},{35,3},{4,36},{36... | collective-permute-start | bytes 1179656 | tf_op jit(solution)/shard_map/ppermute | solution.py:408
  5.8 1.9 %collective-permute-done.refs_0_ = f32[768,128]{1,0:T(8,128)S(1)} collective-permute-done((f32[768,128]{1,0:T(8,128)}, f32[768,128]{1,0:T(8,128)S(1)}, u32[]{:S(2)}, u32[]{:S(2)}) %collective-permute-start) | collective-permute-done | bytes 393248 | tf_op jit(solution)/shard_map/ppermute | solution.py:408
  7.7 0.0 copy-start.2
  7.7 0.8 copy-done.2
  8.5 0.0 copy-start.1
  8.5 4.0 %shard_map.65 = f32[1280,128]{1,0:T(8,128)} custom-call(f32[18,64,128]{2,1,0:T(8,128)} %now_hbm.3, f32[18,64,128]{2,1,0:T(8,128)} %prev_hbm.3, s32[18,64,128]{2,1,0:T(8,128)} %phase_hbm.3, f32[16,64,128]{2,1,0:T(8,128)} %div_hbm.3, f32[768,128]{1,0:T(8,128)} %copy-done.2), custom_call_target="tpu_custom_call" | custom-call | tf_op jit(solution)/shard_map/pallas_call | solution.py:368
  12.5 0.0 copy-start
  12.5 62.3 %all_to_all.10 = f32[256,1,640]{2,1,0:T(1,128)S(1)} all-to-all(f32[256,1,640]{2,1,0:T(1,128)} %bitcast.9), channel_id=1, replica_groups=mesh['zh'=2,'x'=4,'c'=2,'zl'=8,'y'=4] {'zh','x','zl','y'}, dimensions={0} | all-to-all | bytes 1310720 | tf_op jit(solution)/shard_map/all_to_all | solution.py:410
  74.8 0.0 copy-done.1
  74.8 0.0 copy-done
  74.8 2.4 %shard_map.66 = f32[2048,128]{1,0:T(8,128)} custom-call(f32[1280,128]{1,0:T(8,128)S(1)} %bitcast.8, bf16[1024,512]{1,0:T(8,128)(2,1)S(1)} %copy-done, bf16[1024,512]{1,0:T(8,128)(2,1)S(1)} %copy-done.1), custom_call_target="tpu_custom_call" | custom-call | tf_op jit(solution)/shard_map/pallas_call | solution.py:368
  77.2 12.7 %all-to-all-start.1 = ((f32[512,4,128]{2,1,0:T(4,128)}), f32[512,4,128]{2,1,0:T(4,128)S(1)}, u32[]{:S(2)}, u32[]{:S(2)}) async-start(f32[512,4,128]{2,1,0:T(4,128)} %bitcast.2), calls=%async_computation.1 | async-start | bytes 2097152 | tf_op jit(solution)/shard_map/all_to_all | solution.py:420
  90.1 0.4 select_multiply_fusion.y_matrix_ref
  90.5 2.0 %multiply_select_fusion.x_matrix_ref = f32[256,256]{1,0:T(8,128)S(1)} fusion(s32[]{:T(128)S(6)} %add.115, s32[256]{0:T(256)S(1)} %get-tuple-element.24, s32[256]{0:T(256)S(1)} %get-tuple-element.27, s32[256]{0:T(256)S(1)} %get-tuple-element.23, s32[256]{0:T(256)S(1)} %get-tuple-element.28, pred[256]{0:T(512)(128)(4,1)S(1)} %get-tuple-element.25, ...), kind=kLoop, calls=%fused_computation.8 | loop fusion | flops 1638400 | bytes 266756 | tf_op jit(solution)/shard_map/jit(_where)/select_n | solution.py:356
  92.5 55.3 %all-to-all-done.1 = f32[512,4,128]{2,1,0:T(4,128)S(1)} async-done(((f32[512,4,128]{2,1,0:T(4,128)}), f32[512,4,128]{2,1,0:T(4,128)S(1)}, u32[]{:S(2)}, u32[]{:S(2)}) %all-to-all-start.1) | async-done | bytes 1048608 | tf_op jit(solution)/shard_map/all_to_all | solution.py:420
  147.7 2.9 %shard_map.67 = f32[2,16,64,128]{3,2,1,0:T(8,128)} custom-call(f32[2048,128]{1,0:T(8,128)S(1)} %bitcast.7, f32[128,128]{1,0:T(8,128)S(1)} %select_multiply_fusion.y_matrix_ref, f32[256,256]{1,0:T(8,128)S(1)} %multiply_select_fusion.x_matrix_ref), custom_call_target="tpu_custom_call" | custom-call | tf_op jit(solution)/shard_map/pallas_call | solution.py:368
  (12 shorter events, 0.1 us)
Async XLA Ops:
  3.9 3.8 %collective-permute-start = (f32[768,128]{1,0:T(8,128)}, f32[768,128]{1,0:T(8,128)S(1)}, u32[]{:S(2)}, u32[]{:S(2)}) collective-permute-start(f32[768,128]{1,0:T(8,128)} %shard_map.64), channel_id=1, source_target_pairs={{0,32},{32,0},{1,33},{33,1},{2,34},{34,2},{3,35},{35,3},{4,36},{36... | collective-permute-start | bytes 1179656 | tf_op jit(solution)/shard_map/ppermute | solution.py:408
  7.7 0.8 copy-start.2
  8.5 66.3 %copy-start.1 = (bf16[1024,512]{1,0:T(8,128)(2,1)S(1)}, bf16[1024,512]{1,0:T(8,128)(2,1)}, u32[]{:S(2)}) copy-start(bf16[1024,512]{1,0:T(8,128)(2,1)} %constant.187.clone.low_ref) | copy-start | bytes 3145732
  12.5 62.3 %copy-start = (bf16[1024,512]{1,0:T(8,128)(2,1)S(1)}, bf16[1024,512]{1,0:T(8,128)(2,1)}, u32[]{:S(2)}) copy-start(bf16[1024,512]{1,0:T(8,128)(2,1)} %constant.186.clone.high_ref) | copy-start | bytes 3145732
  77.2 70.5 %all-to-all-start.1 = ((f32[512,4,128]{2,1,0:T(4,128)}), f32[512,4,128]{2,1,0:T(4,128)S(1)}, u32[]{:S(2)}, u32[]{:S(2)}) async-start(f32[512,4,128]{2,1,0:T(4,128)} %bitcast.2), calls=%async_computation.1 | async-start | bytes 2097152 | tf_op jit(solution)/shard_map/all_to_all | solution.py:420

commit v5 on v3

--- a/solution.py
+++ b/solution.py
@@ -218,41 +218,56 @@
         cells[pl.ds(g * N_GY, N_GY), LX:] = second + through
         here, entering = there, leaving
 
-    right = split(cells[...])
+    right_high, right_low = split(cells[...])
+    result = dot3((high_ref[...], low_ref[...]), (right_high, right_low))
     for part in range(2):
-        rows = pl.ds(part * N_ALL, N_ALL)
-        result = dot3((high_ref[rows, :], low_ref[rows, :]), right)
-        out[pl.ds(2 * part, N_ALL, stride=4), :] = result[:, :LX]
-        out[pl.ds(2 * part + 1, N_ALL, stride=4), :] = result[:, LX:]
-
-
-def local_kernel(x_ref, y_matrix_ref, x_matrix_ref, out_hbm, out, sems):
+        rows = slice(part * N_ALL, (part + 1) * N_ALL)
+        out[pl.ds(2 * part, N_ALL, stride=4), :] = result[rows, :LX]
+        out[pl.ds(2 * part + 1, N_ALL, stride=4), :] = result[rows, LX:]
+
+
+def local_kernel(x_ref, y_matrix_ref, cos_ref, sin_ref, out_hbm, out, sems):
     y_matrix = split(y_matrix_ref[...])
-    x_matrix = split(x_matrix_ref[...])
+    x_matrix = split(
+        jnp.concatenate(
+            [
+                jnp.concatenate([cos_ref[...], -sin_ref[...]], axis=1),
+                jnp.concatenate([sin_ref[...], cos_ref[...]], axis=1),
+            ],
+            axis=0,
+        )
+    )
     block = cell_block()
     copies = []
-    for k in range(PLANES):
-        start = k * 2 * LY
-        lines = [
-            turn(x_ref[pl.ds(start + kind, BLOCKS, stride=4), :], block, -1, kind & 1)
-            for kind in range(4)
-        ]
-        lines.append(x_ref[pl.ds(start + 4 * BLOCKS, 4 * WIDE), :])
-        lines = dot3(y_matrix, split(jnp.concatenate(lines, axis=0)))
-        lines = jnp.concatenate([lines[:LY], lines[LY:]], axis=1)
+    for g in range(PLANES // GROUP):
+        group = []
+        for k in range(GROUP * g, GROUP * (g + 1)):
+            start = k * 2 * LY
+            lines = [
+                turn(x_ref[pl.ds(start + kind, BLOCKS, stride=4), :], block, -1, kind & 1)
+                for kind in range(4)
+            ]
+            lines.append(x_ref[pl.ds(start + 4 * BLOCKS, 4 * WIDE), :])
+            group.append(jnp.concatenate(lines, axis=0))
+        lines = dot3(y_matrix, split(jnp.concatenate(group, axis=1)))
+        lines = jnp.concatenate(
+            [
+                jnp.concatenate(
+                    [lines[:LY, k * LX : (k + 1) * LX], lines[LY:, k * LX : (k + 1) * LX]], axis=1
+                )
+                for k in range(GROUP)
+            ],
+            axis=0,
+        )
         modes = dot3(split(lines), x_matrix)
-        out[0, k] = modes[:, :LX]
-        out[1, k] = modes[:, LX:]
-        if k % GROUP == GROUP - 1:
-            g = k // GROUP
-            for part in range(2):
-                planes = (part, pl.ds(g * GROUP, GROUP))
-                copies.append(
-                    pltpu.make_async_copy(
-                        out.at[planes], out_hbm.at[planes], sems.at[g, part]
-                    )
-                )
-                copies[-1].start()
+        for part in range(2):
+            for k in range(GROUP):
+                out[part, GROUP * g + k] = modes[k * LY : (k + 1) * LY, part * LX : (part + 1) * LX]
+            planes = (part, pl.ds(g * GROUP, GROUP))
+            copies.append(
+                pltpu.make_async_copy(out.at[planes], out_hbm.at[planes], sems.at[g, part])
+            )
+            copies[-1].start()
     for copy in copies:
         copy.wait()
 
@@ -275,9 +290,7 @@
     return jnp.cos(angle), jnp.sin(angle)
 
 
-def local_tables():
-    rp = reversal(lax.axis_index("gx"), 4)
-    rq = reversal(lax.axis_index("gy"), 5)
+def local_tables(rp, rq):
     line = lax.broadcasted_iota(jnp.int32, (2 * LY, 2 * LY), 0)
     col = lax.broadcasted_iota(jnp.int32, (2 * LY, 2 * LY), 1)
     rest = col - 4 * BLOCKS
@@ -292,13 +305,9 @@
     part_out = line // LY
     sign = jnp.where(part_out < part_in, 1.0, -1.0)
     y_matrix = jnp.where(part_out == part_in, cosine, sign * sine) * (1.0 / math.sqrt(NX * NY))
-    line = lax.broadcasted_iota(jnp.int32, (2 * LX, 2 * LX), 0)
-    col = lax.broadcasted_iota(jnp.int32, (2 * LX, 2 * LX), 1)
-    cosine, sine = cos_sin(line % LX, 16 * (col % LX) + rp, NX)
-    part_in, part_out = line // LX, col // LX
-    sign = jnp.where(part_out < part_in, 1.0, -1.0)
-    x_matrix = jnp.where(part_out == part_in, cosine, sign * sine)
-    return y_matrix, x_matrix
+    line = lax.broadcasted_iota(jnp.int32, (LX, LX), 0)
+    col = lax.broadcasted_iota(jnp.int32, (LX, LX), 1)
+    return (y_matrix, *cos_sin(line, 16 * col + rp, NX))
 
 
 def call(kernel, outs, *args, scratch=(), in_hbm=False, out_hbm=False, mib=40):
@@ -342,7 +351,12 @@
         mib=60,
     )
     everywhere = ("gx", "gy")
+    chunks, rp, rq = lax.optimization_barrier(
+        (chunks, reversal(lax.axis_index("gx"), 4), reversal(lax.axis_index("gy"), 5))
+    )
+    tables = local_tables(rp, rq)
     chunks = lax.all_to_all(chunks.reshape(N_ALL, 1, 3 * LX), everywhere, 0, 0, tiled=True)
+    chunks, tables = lax.optimization_barrier((chunks, tables))
     high, low = device_tables()
     modes = call(
         device_kernel,
@@ -353,13 +367,11 @@
         scratch=[pltpu.VMEM((N_ALL, 2 * LX), F32)],
     )
     back = lax.all_to_all(modes.reshape(N_ALL, 4, LX), everywhere, 0, 0, tiled=True)
-    y_matrix, x_matrix = local_tables()
     result = call(
         local_kernel,
         shape(2, PLANES, LY, LX),
         back.reshape(4 * N_ALL, LX),
-        y_matrix,
-        x_matrix,
+        *tables,
         scratch=[
             pltpu.VMEM((2, PLANES, LY, LX), F32),
             pltpu.SemaphoreType.DMA((PLANES // GROUP, 2)),

time: 147 us -> 146 us (level)
  starting transfers between devices: 9.66 us -> 23.3 us
  waiting for transfers between devices: 55.3 us -> 45.8 us
  blocking collectives: 70 us -> 67.8 us
  Pallas kernels: 9.38 us -> 7.67 us
  other arithmetic: 2.42 us -> 0.72 us
    all_to_all x1, starting transfers between devices: 9.66 us -> 23.3 us  [body(): lax.all_to_all(chunks.reshape(N_ALL, 1, 3 * LX), everywhere, 0, 0, tiled=...]
    all_to_all x1, waiting for transfers between devices: 55.3 us -> 45.8 us  [body(): lax.all_to_all(chunks.reshape(N_ALL, 1, 3 * LX), everywhere, 0, 0, tiled=...]
    all_to_all x1, blocking collectives: 70 us -> 67.8 us  [body(): lax.all_to_all(modes.reshape(N_ALL, 4, LX), everywhere, 0, 0, tiled=True)]
    select_n x1 -> x0, other arithmetic: 1.97 us -> none  [local_tables(): x_matrix = jnp.where(part_out == part_in, cosine, sign * sine)]
    pallas_call x3, Pallas kernels: 9.38 us -> 7.67 us  [call(): pl.pallas_call(kernel, out_shape=outs, in_specs=[spec(in_hbm)] * len(args...]
  transfers between devices with their start and end apart: 1 -> 1, of which waited for: 1 -> 1; matrix products, arithmetic and copies ran while one was open for 2% -> 0% of each run, Pallas kernels for 0% -> 0%
where the time goes in v5:
time: 146 us; the launch traced here: 145 us
  blocking collectives  67.8 us (46%)
  waiting for transfers between devices  45.8 us (31%)
  starting transfers between devices  23.3 us (16%)
  Pallas kernels  7.67 us (5%)
    all_to_all x1, blocking collectives, body(): lax.all_to_all(modes.reshape(N_ALL, 4, LX), everywhere, 0, 0, tiled=True)  67.8 us
    all_to_all x1, waiting for transfers between devices, body(): lax.all_to_all(chunks.reshape(N_ALL, 1, 3 * LX), everywhere, 0, 0, tiled=...  45.8 us
    all_to_all x1, starting transfers between devices, body(): lax.all_to_all(chunks.reshape(N_ALL, 1, 3 * LX), everywhere, 0, 0, tiled=...  23.3 us
    pallas_call x3, Pallas kernels, call(): pl.pallas_call(kernel, out_shape=outs, in_specs=[spec(in_hbm)] * len(args...  7.67 us
  transfers between devices with their start and end apart: 1, of which 1 were waited for; matrix products, arithmetic and copies ran while one was open for 0% of the time, Pallas kernels for 0%

profile of v5, /device:TPU:2, one launch (start us, length us, event | category | flops | bytes accessed | tf_op | source)
XLA Modules:
  0.0 145.5 jit_solution(13447395803269323722)
XLA Ops:
  0.0 0.0 copy-start.1
  0.0 3.6 %shard_map.64 = f32[1536,128]{1,0:T(8,128)} custom-call(f32[18,64,128]{2,1,0:T(8,128)} %now_hbm.1, f32[18,64,128]{2,1,0:T(8,128)} %prev_hbm.1, s32[18,64,128]{2,1,0:T(8,128)} %phase_hbm.1, f32[16,64,128]{2,1,0:T(8,128)} %div_hbm.1), custom_call_target="tpu_custom_call" | custom-call | tf_op jit(solution)/shard_map/pallas_call | solution.py:317
  3.6 0.0 copy-start
  3.6 23.3 %all-to-all-start = ((f32[512,1,384]{2,1,0:T(1,128)}), f32[512,1,384]{2,1,0:T(1,128)S(1)}, u32[]{:S(2)}, u32[]{:S(2)}) async-start(f32[512,1,384]{2,1,0:T(1,128)} %bitcast.10), calls=%async_computation | async-start | bytes 1572864 | tf_op jit(solution)/shard_map/all_to_all | solution.py:358
  27.0 0.4 select_multiply_fusion.y_matrix_ref
  27.4 0.3 fusion.9
  27.7 45.8 %all-to-all-done = f32[512,1,384]{2,1,0:T(1,128)S(1)} async-done(((f32[512,1,384]{2,1,0:T(1,128)}), f32[512,1,384]{2,1,0:T(1,128)S(1)}, u32[]{:S(2)}, u32[]{:S(2)}) %all-to-all-start) | async-done | bytes 786464 | tf_op jit(solution)/shard_map/all_to_all | solution.py:358
  73.6 0.0 copy-done.1
  73.6 0.0 copy-done
  73.6 2.0 %shard_map.65 = f32[2048,128]{1,0:T(8,128)S(1)} custom-call(f32[1536,128]{1,0:T(8,128)S(1)} %bitcast.9, bf16[1024,512]{1,0:T(8,128)(2,1)S(1)} %copy-done.1, bf16[1024,512]{1,0:T(8,128)(2,1)S(1)} %copy-done), custom_call_target="tpu_custom_call" | custom-call | tf_op jit(solution)/shard_map/pallas_call | solution.py:317
  75.6 67.8 %all_to_all.10 = f32[512,4,128]{2,1,0:T(4,128)S(1)} all-to-all(f32[512,4,128]{2,1,0:T(4,128)S(1)} %bitcast.8), channel_id=1, replica_groups=mesh['gx'=16,'gy'=32] {'gx','gy'}, dimensions={0} | all-to-all | bytes 2097152 | tf_op jit(solution)/shard_map/all_to_all | solution.py:369
  143.4 2.1 %shard_map.66 = f32[2,16,64,128]{3,2,1,0:T(8,128)} custom-call(f32[2048,128]{1,0:T(8,128)S(1)} %bitcast.7, f32[128,128]{1,0:T(8,128)S(1)} %select_multiply_fusion.y_matrix_ref, f32[128,128]{1,0:T(8,128)S(1)} %get-tuple-element.17.cos_ref, f32[128,128]{1,0:T(8,128)S(1)} %get-tuple-element.18.sin_ref), custom_call_target="tpu_custom_call" | custom-call | tf_op jit(solution)/shard_map/pallas_call | solution.py:317
  (7 shorter events, 0.0 us)
Async XLA Ops:
  0.0 73.6 %copy-start.1 = (bf16[1024,512]{1,0:T(8,128)(2,1)S(1)}, bf16[1024,512]{1,0:T(8,128)(2,1)}, u32[]{:S(2)}) copy-start(bf16[1024,512]{1,0:T(8,128)(2,1)} %constant.97.clone.high_ref) | copy-start | bytes 3145732
  3.6 70.0 %copy-start = (bf16[1024,512]{1,0:T(8,128)(2,1)S(1)}, bf16[1024,512]{1,0:T(8,128)(2,1)}, u32[]{:S(2)}) copy-start(bf16[1024,512]{1,0:T(8,128)(2,1)} %constant.98.clone.low_ref) | copy-start | bytes 3145732
  3.6 70.0 %all-to-all-start = ((f32[512,1,384]{2,1,0:T(1,128)}), f32[512,1,384]{2,1,0:T(1,128)S(1)}, u32[]{:S(2)}, u32[]{:S(2)}) async-start(f32[512,1,384]{2,1,0:T(1,128)} %bitcast.10), calls=%async_computation | async-start | bytes 1572864 | tf_op jit(solution)/shard_map/all_to_all | solution.py:358

commit v6 on v5

--- a/solution.py
+++ b/solution.py
@@ -7,6 +7,7 @@
 from jax import lax
 from jax.experimental import pallas as pl
 from jax.experimental.pallas import tpu as pltpu
+from jax.sharding import Mesh
 from jax.sharding import PartitionSpec as P
 
 NX = 2048
@@ -17,18 +18,24 @@
 N_GX = 16
 N_GY = 32
 N_ALL = N_GX * N_GY
+N_CHIP = N_ALL // 2
 F32 = jnp.float32
 BF16 = jnp.bfloat16
 
+CHIPS = ("zh", "x", "zl", "y")
+EVERYWHERE = ("zh", "x", "c", "zl", "y")
+
 QUAD = 7.0 / 16.0 - 7.0 / 9.0
 LIN = 7.0 / 9.0 - QUAD
 
-BLOCKS = 8
+BLOCKS = 16
 BLOCK = LX // BLOCKS
-PER_PLANE = N_ALL // PLANES
-WIDE = PER_PLANE - BLOCKS
+WIDE = 16
 HALF = LY // 2
+TEAMS = PLANES
+ROWS = 5
 GROUP = 4
+QUARTER = LX // 4
 
 
 def reversal(index, digits):
@@ -53,14 +60,19 @@
     )
 
 
+def weighted(count, difference):
+    return count * (LIN + QUAD * count) * difference
+
+
 def flux(liquid_a, liquid_b, field_a, field_b):
-    count = liquid_a + liquid_b
-    return count * (LIN + QUAD * count) * (field_b - field_a)
+    return weighted(liquid_a + liquid_b, field_b - field_a)
 
 
 def roll(value, by, axis):
-    by = by % value.shape[axis]
-    return pltpu.roll(value, by, axis) if by else value
+    if isinstance(by, int):
+        by = by % value.shape[axis]
+        return pltpu.roll(value, by, axis) if by else value
+    return pltpu.roll(value, by & (value.shape[axis] - 1), axis)
 
 
 def lanes_of(rows):
@@ -71,20 +83,19 @@
     return lax.broadcasted_iota(jnp.int32, (rows, LX), 0)
 
 
+def within(lane, start, count):
+    return ((lane - start) & (LX - 1)) < count
+
+
 def turn(value, block, sign, offset):
     value = roll(value, -offset, 0)
-    for bit in (1, 2, 4):
+    for bit in (1, 2, 4, 8):
         value = jnp.where((block & bit) != 0, roll(value, -sign * bit, 0), value)
     return value
 
 
 def cell_block():
     return ((lanes_of(BLOCKS) + BLOCK // 2) // BLOCK) & (BLOCKS - 1)
-
-
-def face_block(rows):
-    lane = (lanes_of(rows) + LX - 1) & (LX - 1)
-    return lane // BLOCK, lane % BLOCK < BLOCK // 2
 
 
 def stencil_kernel(
@@ -124,10 +135,14 @@
 
     lane = lanes_of(LY)
     row = rows_of(LY)
-    edge_lane = (lane == 0) | (lane == LX - 1)
-    sub = rows_of(BLOCKS)
+    sub = rows_of(8)
     block = cell_block()
-    line_block, in_half = face_block(BLOCKS)
+    lane_in = lanes_of(TEAMS)
+    owner = rows_of(TEAMS) * BLOCK
+    x_lanes = [
+        [within(lane_in, QUARTER * q + 8 + 2 * t, 2) for t in range(4)] for q in range(4)
+    ]
+    y_lanes = [within(lane_in, QUARTER * f + owner, BLOCK) for f in range(4)]
 
     def plane(k):
         return 2.0 * now_ref[k] - prev_ref[k], phase_ref[k].astype(F32)
@@ -149,74 +164,90 @@
         upper = flux(liquid, roll(liquid, -1, 0), field, roll(field, -1, 0))
         upper = jnp.where(row == LY - 1, 0.0, upper)
         total = total + (upper - roll(upper, 1, 0))
-        ends = jnp.where(edge_lane, field, 0.0)
-        wet_ends = jnp.where(edge_lane, liquid, 0.0)
-        first = ends[:HALF] + roll(wet_ends[:HALF], -2, 1)
-        second = roll(ends[HALF:], -4, 1) + roll(wet_ends[HALF:], -6, 1)
-        lines = jnp.broadcast_to(liquid[LY - 1 : LY], (BLOCKS, LX))
+        faces = jnp.zeros((TEAMS, LX), F32)
+        for q, column in enumerate(
+            (field[:, 0:1], liquid[:, 0:1], field[:, LX - 1 : LX], liquid[:, LX - 1 : LX])
+        ):
+            column = jnp.broadcast_to(column, (LY, LX))
+            edge = roll(column[LY - BLOCKS :], 1, 0)
+            for t, part in enumerate(
+                (column[:BLOCKS], edge, column[BLOCKS:HALF], column[HALF : HALF + WIDE])
+            ):
+                faces = jnp.where(x_lanes[q][t], part, faces)
+        faces = pltpu.roll(faces, 0, 1, stride=BLOCK, stride_axis=0)
+        lines = jnp.broadcast_to(liquid[LY - 1 : LY], (8, LX))
         for f, line in ((2, field[LY - 1 : LY]), (1, liquid[0:1]), (0, field[0:1])):
-            lines = jnp.where(sub < 2 * f + 2, jnp.broadcast_to(line, (BLOCKS, LX)), lines)
-        lines = roll(lines, 9, 1)
-        for bit, by in ((1, 8), (2, 32), (4, 64)):
-            lines = jnp.where((sub & bit) != 0, roll(lines, by, 1), lines)
-        lines = turn(jnp.where(in_half, lines, 0.0), line_block, 1, 0)
-
-        start = k * PER_PLANE * 3
-        out[pl.ds(start, BLOCKS, stride=3), :] = turn(total[:BLOCKS], block, 1, 0)
-        out[pl.ds(start + 1, BLOCKS, stride=3), :] = turn(total[LY - BLOCKS :], block, 1, 7)
-        out[pl.ds(start + 2, BLOCKS, stride=3), :] = (
-            first[:BLOCKS] + roll(second[WIDE:], 1, 0) + lines
-        )
-        start += BLOCKS * 3
-        out[pl.ds(start, WIDE, stride=3), :] = total[BLOCKS:HALF]
-        out[pl.ds(start + 1, WIDE, stride=3), :] = total[HALF : HALF + WIDE]
-        out[pl.ds(start + 2, WIDE, stride=3), :] = first[BLOCKS:] + second[:WIDE]
+            lines = jnp.where(sub <= f, jnp.broadcast_to(line, (8, LX)), lines)
+        lines = roll(lines, BLOCK // 2, 1)
+        for bit in (1, 2):
+            lines = jnp.where((sub & bit) != 0, roll(lines, QUARTER * bit, 1), lines)
+        for f in range(4):
+            faces = jnp.where(y_lanes[f], jnp.broadcast_to(lines[f : f + 1], (TEAMS, LX)), faces)
+
+        start = k * TEAMS * ROWS
+        for r, value in enumerate(
+            (
+                turn(total[:BLOCKS], block, -1, 0),
+                turn(total[LY - BLOCKS :], block, -1, 15),
+                total[BLOCKS:HALF],
+                total[HALF : HALF + WIDE],
+                faces,
+            )
+        ):
+            out[pl.ds(start + r, TEAMS, stride=ROWS), :] = value
         field, liquid, flux_z = field_after, liquid_after, flux_z_upper
         if k % GROUP == GROUP - 1:
             g = k // GROUP
-            rows = pl.ds(g * GROUP * PER_PLANE * 3, GROUP * PER_PLANE * 3)
+            rows = pl.ds(g * GROUP * TEAMS * ROWS, GROUP * TEAMS * ROWS)
             sent.append(pltpu.make_async_copy(out.at[rows], out_hbm.at[rows], out_sems.at[g]))
             sent[-1].start()
     for copy in sent:
         copy.wait()
 
 
-def device_kernel(x_ref, high_ref, low_ref, out, cells):
-    last_lane = lanes_of(N_GY) == LX - 1
-    own = (BLOCKS - lax.axis_index("gy") % BLOCKS) % BLOCKS
-    line_block, in_half = face_block(N_GY)
-    first_half = in_half & (line_block == own)
-    second_half = in_half & (line_block == (own + 1) % BLOCKS)
-
-    def group(g, r):
-        return x_ref[pl.ds((g % N_GX) * N_GY * 3 + r, N_GY, stride=3), :]
-
-    def x_flux(here, there, t):
-        through = flux(
-            roll(here, 2 + 4 * t, 1),
-            roll(there, 1 + 4 * t, 1),
-            roll(here, 4 * t, 1),
-            roll(there, 4 * t - 1, 1),
-        )
-        return jnp.where(last_lane, through, 0.0)
-
-    last = group(N_GX - 1, 2)
-    here = group(0, 2)
-    entering = [x_flux(last, here, t) for t in range(2)]
-    for g in range(N_GX):
-        there = group(g + 1, 2)
-        first, second = group(g, 0), group(g, 1)
-        leaving = [x_flux(here, there, t) for t in range(2)]
-        first = first + (leaving[0] - roll(entering[0], 1, 1))
-        second = second + (leaving[1] - roll(entering[1], 1, 1))
-        after = roll(here, -1, 0)
-        through = flux(roll(here, -96, 1), roll(after, -32, 1), roll(here, -64, 1), after)
-        through = roll(jnp.where(first_half, through, 0.0), -9, 1) + roll(
-            jnp.where(second_half, through, 0.0), -17, 1
-        )
-        cells[pl.ds(g * N_GY, N_GY), :LX] = first - roll(through, 1, 0)
-        cells[pl.ds(g * N_GY, N_GY), LX:] = second + through
-        here, entering = there, leaving
+def device_kernel(own_ref, other_ref, high_ref, low_ref, out, cells):
+    lane = lanes_of(N_GY)
+    core = lax.axis_index("c")
+    team = (lax.axis_index("zl") * 4 + lax.axis_index("y")) % TEAMS * BLOCK
+    in_y = (lane & 15) < BLOCK
+    own_y = (lane < BLOCK) & (core == 0)
+    at_last, at_first = lane == LX - 1, lane == 0
+    groups = N_GX // 2
+
+    def rows(c, g, r):
+        place = pl.ds((g % groups) * N_GY * ROWS + r, N_GY, stride=ROWS)
+        return jnp.where(core == c, own_ref[place, :], other_ref[place, :])
+
+    def aligned(c, g):
+        return roll(rows(c, g, 4), 2 * LX - team - 4 * core, 1)
+
+    def through(here, there):
+        lower = jnp.where(in_y, roll(here, -1, 0), there)
+        upper = roll(here, -2 * QUARTER, 1)
+        return weighted(roll(upper + lower, -QUARTER, 1), lower - upper)
+
+    def x_parts(value):
+        return [roll(value, LX - 1 - (8 + 2 * t), 1) for t in range(2)]
+
+    faces = [aligned(c, 0) for c in range(2)]
+    entering = x_parts(through(aligned(1, groups - 1), faces[0]))
+    for g in range(groups):
+        after = [aligned(c, g + 1) for c in range(2)]
+        for c in range(2):
+            value = through(faces[c], after[0] if c else faces[1])
+            leaving = x_parts(value)
+            along_y = roll(jnp.where(own_y, value, 0.0), team + (LX - BLOCK // 2), 1)
+            part = [
+                rows(c, g, 2 * core + t)
+                + jnp.where(at_last, leaving[t], 0.0)
+                - jnp.where(at_first, entering[t], 0.0)
+                for t in range(2)
+            ]
+            place = pl.ds(c * N_CHIP + g * N_GY, N_GY)
+            cells[place, :LX] = part[0] - roll(along_y, 1, 0)
+            cells[place, LX:] = part[1] + along_y
+            entering = leaving
+        faces = after
 
     right_high, right_low = split(cells[...])
     result = dot3((high_ref[...], low_ref[...]), (right_high, right_low))
@@ -242,12 +273,12 @@
     for g in range(PLANES // GROUP):
         group = []
         for k in range(GROUP * g, GROUP * (g + 1)):
-            start = k * 2 * LY
+            start = (k // 2) * 4 * LY + (k % 2) * LY
             lines = [
-                turn(x_ref[pl.ds(start + kind, BLOCKS, stride=4), :], block, -1, kind & 1)
+                turn(x_ref[pl.ds(start + kind, BLOCKS, stride=4), :], block, 1, kind & 1)
                 for kind in range(4)
             ]
-            lines.append(x_ref[pl.ds(start + 4 * BLOCKS, 4 * WIDE), :])
+            lines.append(x_ref[pl.ds(start + 2 * LY, LY), :])
             group.append(jnp.concatenate(lines, axis=0))
         lines = dot3(y_matrix, split(jnp.concatenate(group, axis=1)))
         lines = jnp.concatenate(
@@ -273,13 +304,15 @@
 
 
 def device_tables():
-    source = np.arange(N_ALL)
+    dest = np.arange(N_ALL)
     rev_p = np.array([reversal(i, 4) for i in range(N_GX)])
     rev_q = np.array([reversal(i, 5) for i in range(N_GY)])
-    kx = rev_p[source // N_GY][:, None]
-    ky = rev_q[source % N_GY][:, None]
-    turns = (2 * kx * (source // N_GY)[None] + ky * (source % N_GY)[None]) % N_GY
-    angle = turns * (2.0 * math.pi / N_GY)
+    kx = rev_p[dest // N_GY][:, None]
+    ky = rev_q[dest % N_GY][:, None]
+    source = np.arange(N_ALL)
+    gx = (2 * (source % N_CHIP // N_GY) + source // N_CHIP)[None]
+    gy = (source % N_GY)[None]
+    angle = (2 * kx * gx + ky * gy) % N_GY * (2.0 * math.pi / N_GY)
     table = np.concatenate([np.cos(angle), -np.sin(angle)])
     high = table.astype(ml_dtypes.bfloat16)
     return high, (table - high.astype(np.float64)).astype(ml_dtypes.bfloat16)
@@ -295,10 +328,10 @@
     col = lax.broadcasted_iota(jnp.int32, (2 * LY, 2 * LY), 1)
     rest = col - 4 * BLOCKS
     in_block = rest < 0
-    part_in = jnp.where(in_block, col >> 4, rest >> 1) & 1
+    part_in = jnp.where(in_block, col // (2 * BLOCKS), rest >> 1) & 1
     place = jnp.where(
         in_block,
-        (col & 7) + (LY - BLOCKS) * ((col >> 3) & 1),
+        col % BLOCKS + (LY - BLOCKS) * (col // BLOCKS & 1),
         BLOCKS + (rest >> 2) + WIDE * (rest & 1),
     )
     cosine, sine = cos_sin(place, 32 * (line % LY) + rq, NY)
@@ -332,7 +365,7 @@
     padded = (PLANES + 2, LY, LX)
     chunks = call(
         stencil_kernel,
-        shape(3 * N_ALL, LX),
+        shape(ROWS * N_CHIP, LX),
         p_now,
         p_prev,
         phase,
@@ -342,7 +375,7 @@
             pltpu.VMEM(padded, F32),
             pltpu.VMEM(padded, jnp.int32),
             pltpu.VMEM((PLANES, LY, LX), F32),
-            pltpu.VMEM((3 * N_ALL, LX), F32),
+            pltpu.VMEM((ROWS * N_CHIP, LX), F32),
             pltpu.SemaphoreType.DMA((PLANES // GROUP, 4)),
             pltpu.SemaphoreType.DMA((PLANES // GROUP,)),
         ],
@@ -350,23 +383,29 @@
         out_hbm=True,
         mib=60,
     )
-    everywhere = ("gx", "gy")
     chunks, rp, rq = lax.optimization_barrier(
-        (chunks, reversal(lax.axis_index("gx"), 4), reversal(lax.axis_index("gy"), 5))
+        (
+            chunks,
+            reversal(lax.axis_index(("zh", "x", "c")), 4),
+            reversal(lax.axis_index(("zl", "y")), 5),
+        )
     )
     tables = local_tables(rp, rq)
-    chunks = lax.all_to_all(chunks.reshape(N_ALL, 1, 3 * LX), everywhere, 0, 0, tiled=True)
+    chunks = lax.all_to_all(chunks.reshape(N_CHIP, 1, ROWS * LX), CHIPS, 0, 0, tiled=True)
     chunks, tables = lax.optimization_barrier((chunks, tables))
+    chunks = chunks.reshape(ROWS * N_CHIP, LX)
+    other = lax.ppermute(chunks, "c", [(0, 1), (1, 0)])
     high, low = device_tables()
     modes = call(
         device_kernel,
         shape(4 * N_ALL, LX),
-        chunks.reshape(3 * N_ALL, LX),
+        chunks,
+        other,
         jnp.asarray(high),
         jnp.asarray(low),
         scratch=[pltpu.VMEM((N_ALL, 2 * LX), F32)],
     )
-    back = lax.all_to_all(modes.reshape(N_ALL, 4, LX), everywhere, 0, 0, tiled=True)
+    back = lax.all_to_all(modes.reshape(N_ALL, 4, LX), EVERYWHERE, 0, 0, tiled=True)
     result = call(
         local_kernel,
         shape(2, PLANES, LY, LX),
@@ -382,11 +421,12 @@
 
 
 def solution(mesh):
-    spec = P(None, "gy", "gx")
+    fine = Mesh(mesh.devices.reshape(2, 4, 2, 8, 4), EVERYWHERE)
+    spec = P(None, ("zl", "y"), ("zh", "x", "c"))
     return jax.shard_map(
         body,
-        mesh=mesh,
+        mesh=fine,
         in_specs=(spec, spec, spec, spec),
-        out_specs=P(None, None, "gy", None, "gx", None),
+        out_specs=P(None, None, ("zl", "y"), None, ("zh", "x", "c"), None),
         check_vma=False,
     )

time: 146 us -> 146 us (level)
  waiting for transfers between devices: 45.8 us -> 39.6 us
  blocking collectives: 67.8 us -> 70.7 us
  starting transfers between devices: 23.3 us -> 25.7 us
  Pallas kernels: 7.67 us -> 9.23 us
    all_to_all x1, waiting for transfers between devices: 45.8 us -> 37.5 us  [body(): lax.all_to_all(chunks.reshape(N_CHIP, 1, ROWS * LX), CHIPS, 0, 0, tiled=T...]
    all_to_all x1, blocking collectives: 67.8 us -> 70.7 us  [body(): lax.all_to_all(modes.reshape(N_ALL, 4, LX), EVERYWHERE, 0, 0, tiled=True)]
    ppermute x0 -> x1, waiting for transfers between devices: none -> 2.06 us  [body(): other = lax.ppermute(chunks, 'c', [(0, 1), (1, 0)])]
    ppermute x0 -> x1, starting transfers between devices: none -> 1.91 us  [body(): other = lax.ppermute(chunks, 'c', [(0, 1), (1, 0)])]
    pallas_call x3, Pallas kernels: 7.67 us -> 9.23 us  [call(): pl.pallas_call(kernel, out_shape=outs, in_specs=[spec(in_hbm)] * len(args...]
  transfers between devices with their start and end apart: 1 -> 2, of which waited for: 1 -> 2; matrix products, arithmetic and copies ran while one was open for 0% -> 0% of each run, Pallas kernels for 0% -> 0%
where the time goes in v6:
time: 146 us
  blocking collectives  70.7 us (48%)
  waiting for transfers between devices  39.6 us (27%)
  starting transfers between devices  25.7 us (18%)
  Pallas kernels  9.23 us (6%)
    all_to_all x1, blocking collectives, body(): lax.all_to_all(modes.reshape(N_ALL, 4, LX), EVERYWHERE, 0, 0, tiled=True)  70.7 us
    all_to_all x1, waiting for transfers between devices, body(): lax.all_to_all(chunks.reshape(N_CHIP, 1, ROWS * LX), CHIPS, 0, 0, tiled=T...  37.5 us
    all_to_all x1, starting transfers between devices, body(): lax.all_to_all(chunks.reshape(N_CHIP, 1, ROWS * LX), CHIPS, 0, 0, tiled=T...  23.8 us
    pallas_call x3, Pallas kernels, call(): pl.pallas_call(kernel, out_shape=outs, in_specs=[spec(in_hbm)] * len(args...  9.23 us
  transfers between devices with their start and end apart: 2, of which 2 were waited for; matrix products, arithmetic and copies ran while one was open for 0% of the time, Pallas kernels for 0%

profile of v6, /device:TPU:2, one launch (start us, length us, event | category | flops | bytes accessed | tf_op | source)
XLA Modules:
  0.0 146.1 jit_solution(8582471109619129916)
XLA Ops:
  0.0 0.0 copy-start.1
  0.0 5.6 %shard_map.64 = f32[1280,128]{1,0:T(8,128)} custom-call(f32[18,64,128]{2,1,0:T(8,128)} %now_hbm.1, f32[18,64,128]{2,1,0:T(8,128)} %prev_hbm.1, s32[18,64,128]{2,1,0:T(8,128)} %phase_hbm.1, f32[16,64,128]{2,1,0:T(8,128)} %div_hbm.1), custom_call_target="tpu_custom_call" | custom-call | tf_op jit(solution)/shard_map/pallas_call | solution.py:350
  5.6 0.0 copy-start
  5.6 23.8 %all-to-all-start = ((f32[256,1,640]{2,1,0:T(1,128)}), f32[256,1,640]{2,1,0:T(1,128)S(1)}, u32[]{:S(2)}, u32[]{:S(2)}) async-start(f32[256,1,640]{2,1,0:T(1,128)} %bitcast.11), calls=%async_computation | async-start | bytes 1310720 | tf_op jit(solution)/shard_map/all_to_all | solution.py:394
  29.6 0.4 select_multiply_fusion.y_matrix_ref
  30.0 0.3 fusion.9
  30.2 37.5 %all-to-all-done = f32[256,1,640]{2,1,0:T(1,128)S(1)} async-done(((f32[256,1,640]{2,1,0:T(1,128)}), f32[256,1,640]{2,1,0:T(1,128)S(1)}, u32[]{:S(2)}, u32[]{:S(2)}) %all-to-all-start) | async-done | bytes 655392 | tf_op jit(solution)/shard_map/all_to_all | solution.py:394
  67.8 1.9 %collective-permute-start = (f32[1280,128]{1,0:T(8,128)S(1)}, f32[1280,128]{1,0:T(8,128)S(1)}, u32[]{:S(2)}, u32[]{:S(2)}) collective-permute-start(f32[1280,128]{1,0:T(8,128)S(1)} %bitcast.9), channel_id=1, source_target_pairs={{0,32},{32,0},{1,33},{33,1},{2,34},{34,2},{3,35},{35,3},{4,36},{36... | collective-permute-start | bytes 1966088 | tf_op jit(solution)/shard_map/ppermute | solution.py:397
  69.7 2.1 %collective-permute-done.other_ref = f32[1280,128]{1,0:T(8,128)S(1)} collective-permute-done((f32[1280,128]{1,0:T(8,128)S(1)}, f32[1280,128]{1,0:T(8,128)S(1)}, u32[]{:S(2)}, u32[]{:S(2)}) %collective-permute-start) | collective-permute-done | bytes 655392 | tf_op jit(solution)/shard_map/ppermute | solution.py:397
  71.8 0.0 copy-done.1
  71.8 0.0 copy-done
  71.8 1.5 %shard_map.65 = f32[2048,128]{1,0:T(8,128)S(1)} custom-call(f32[1280,128]{1,0:T(8,128)S(1)} %bitcast.10, f32[1280,128]{1,0:T(8,128)S(1)} %collective-permute-done.other_ref, bf16[1024,512]{1,0:T(8,128)(2,1)S(1)} %copy-done.1, bf16[1024,512]{1,0:T(8,128)(2,1)S(1)} %copy-done), custom_call_target="tpu_custom_call" | custom-call | tf_op jit(solution)/shard_map/pallas_call | solution.py:350
  73.3 70.7 %all_to_all.10 = f32[512,4,128]{2,1,0:T(4,128)S(1)} all-to-all(f32[512,4,128]{2,1,0:T(4,128)S(1)} %bitcast.7), channel_id=1, replica_groups=mesh['zh'=2,'x'=4,'c'=2,'zl'=8,'y'=4] {'zh','x','c','zl','y'}, dimensions={0} | all-to-all | bytes 2097152 | tf_op jit(solution)/shard_map/all_to_all | solution.py:408
  143.9 2.2 %shard_map.66 = f32[2,16,64,128]{3,2,1,0:T(8,128)} custom-call(f32[2048,128]{1,0:T(8,128)S(1)} %bitcast.8, f32[128,128]{1,0:T(8,128)S(1)} %select_multiply_fusion.y_matrix_ref, f32[128,128]{1,0:T(8,128)S(1)} %get-tuple-element.17.cos_ref, f32[128,128]{1,0:T(8,128)S(1)} %get-tuple-element.18.sin_ref), custom_call_target="tpu_custom_call" | custom-call | tf_op jit(solution)/shard_map/pallas_call | solution.py:350
  (10 shorter events, 0.1 us)
Async XLA Ops:
  0.0 71.8 %copy-start.1 = (bf16[1024,512]{1,0:T(8,128)(2,1)S(1)}, bf16[1024,512]{1,0:T(8,128)(2,1)}, u32[]{:S(2)}) copy-start(bf16[1024,512]{1,0:T(8,128)(2,1)} %constant.140.clone.high_ref) | copy-start | bytes 3145732
  5.6 66.2 %copy-start = (bf16[1024,512]{1,0:T(8,128)(2,1)S(1)}, bf16[1024,512]{1,0:T(8,128)(2,1)}, u32[]{:S(2)}) copy-start(bf16[1024,512]{1,0:T(8,128)(2,1)} %constant.141.clone.low_ref) | copy-start | bytes 3145732
  5.6 62.2 %all-to-all-start = ((f32[256,1,640]{2,1,0:T(1,128)}), f32[256,1,640]{2,1,0:T(1,128)S(1)}, u32[]{:S(2)}, u32[]{:S(2)}) async-start(f32[256,1,640]{2,1,0:T(1,128)} %bitcast.11), calls=%async_computation | async-start | bytes 1310720 | tf_op jit(solution)/shard_map/all_to_all | solution.py:394
  67.8 4.0 %collective-permute-start = (f32[1280,128]{1,0:T(8,128)S(1)}, f32[1280,128]{1,0:T(8,128)S(1)}, u32[]{:S(2)}, u32[]{:S(2)}) collective-permute-start(f32[1280,128]{1,0:T(8,128)S(1)} %bitcast.9), channel_id=1, source_target_pairs={{0,32},{32,0},{1,33},{33,1},{2,34},{34,2},{3,35},{35,3},{4,36},{36... | collective-permute-start | bytes 1966088 | tf_op jit(solution)/shard_map/ppermute | solution.py:397

commit v7 on v6

--- a/solution.py
+++ b/solution.py
@@ -139,9 +139,8 @@
     block = cell_block()
     lane_in = lanes_of(TEAMS)
     owner = rows_of(TEAMS) * BLOCK
-    x_lanes = [
-        [within(lane_in, QUARTER * q + 8 + 2 * t, 2) for t in range(4)] for q in range(4)
-    ]
+    moved = rows_of(TEAMS) % 4 == 0
+    edge_lane = (lane == 0) | (lane == LX - 1)
     y_lanes = [within(lane_in, QUARTER * f + owner, BLOCK) for f in range(4)]
 
     def plane(k):
@@ -164,17 +163,14 @@
         upper = flux(liquid, roll(liquid, -1, 0), field, roll(field, -1, 0))
         upper = jnp.where(row == LY - 1, 0.0, upper)
         total = total + (upper - roll(upper, 1, 0))
-        faces = jnp.zeros((TEAMS, LX), F32)
-        for q, column in enumerate(
-            (field[:, 0:1], liquid[:, 0:1], field[:, LX - 1 : LX], liquid[:, LX - 1 : LX])
-        ):
-            column = jnp.broadcast_to(column, (LY, LX))
-            edge = roll(column[LY - BLOCKS :], 1, 0)
-            for t, part in enumerate(
-                (column[:BLOCKS], edge, column[BLOCKS:HALF], column[HALF : HALF + WIDE])
-            ):
-                faces = jnp.where(x_lanes[q][t], part, faces)
-        faces = pltpu.roll(faces, 0, 1, stride=BLOCK, stride_axis=0)
+        ends = jnp.where(edge_lane, field, 0.0) + roll(
+            jnp.where(edge_lane, liquid, 0.0), QUARTER, 1
+        )
+        faces = roll(ends[:BLOCKS], 1, 1)
+        faces = faces + roll(roll(ends[LY - BLOCKS :], 1, 0), 3, 1)
+        faces = faces + roll(ends[BLOCKS:HALF], 5, 1)
+        faces = faces + roll(ends[HALF : HALF + WIDE], 7, 1)
+        faces = jnp.where(moved, roll(faces, BLOCK, 1), faces)
         lines = jnp.broadcast_to(liquid[LY - 1 : LY], (8, LX))
         for f, line in ((2, field[LY - 1 : LY]), (1, liquid[0:1]), (0, field[0:1])):
             lines = jnp.where(sub <= f, jnp.broadcast_to(line, (8, LX)), lines)
@@ -209,7 +205,6 @@
     lane = lanes_of(N_GY)
     core = lax.axis_index("c")
     team = (lax.axis_index("zl") * 4 + lax.axis_index("y")) % TEAMS * BLOCK
-    in_y = (lane & 15) < BLOCK
     own_y = (lane < BLOCK) & (core == 0)
     at_last, at_first = lane == LX - 1, lane == 0
     groups = N_GX // 2
@@ -218,36 +213,41 @@
         place = pl.ds((g % groups) * N_GY * ROWS + r, N_GY, stride=ROWS)
         return jnp.where(core == c, own_ref[place, :], other_ref[place, :])
 
-    def aligned(c, g):
-        return roll(rows(c, g, 4), 2 * LX - team - 4 * core, 1)
-
-    def through(here, there):
-        lower = jnp.where(in_y, roll(here, -1, 0), there)
+    def x_aligned(value):
+        return roll(value, 2 * LX - 1 - 4 * core - BLOCK * (team % (4 * BLOCK) == 0), 1)
+
+    def x_parts(here, there):
+        lower = roll(there, -1, 1)
+        value = weighted(roll(here + lower, -QUARTER, 1), lower - here)
+        return [(value, roll(value, 1, 1)), (roll(value, -2, 1), roll(value, -1, 1))]
+
+    def y_part(here):
+        here = roll(here, LX - team, 1)
+        lower = roll(here, -1, 0)
         upper = roll(here, -2 * QUARTER, 1)
-        return weighted(roll(upper + lower, -QUARTER, 1), lower - upper)
-
-    def x_parts(value):
-        return [roll(value, LX - 1 - (8 + 2 * t), 1) for t in range(2)]
-
-    faces = [aligned(c, 0) for c in range(2)]
-    entering = x_parts(through(aligned(1, groups - 1), faces[0]))
+        value = weighted(roll(upper + lower, -QUARTER, 1), lower - upper)
+        return roll(jnp.where(own_y, value, 0.0), team + (LX - BLOCK // 2), 1)
+
+    raw = [rows(c, 0, 4) for c in range(2)]
+    faces = [x_aligned(value) for value in raw]
+    entering = x_parts(x_aligned(rows(1, groups - 1, 4)), faces[0])
     for g in range(groups):
-        after = [aligned(c, g + 1) for c in range(2)]
+        next_raw = [rows(c, g + 1, 4) for c in range(2)]
+        after = [x_aligned(value) for value in next_raw]
         for c in range(2):
-            value = through(faces[c], after[0] if c else faces[1])
-            leaving = x_parts(value)
-            along_y = roll(jnp.where(own_y, value, 0.0), team + (LX - BLOCK // 2), 1)
+            leaving = x_parts(faces[c], after[0] if c else faces[1])
+            along_y = y_part(raw[c])
             part = [
                 rows(c, g, 2 * core + t)
-                + jnp.where(at_last, leaving[t], 0.0)
-                - jnp.where(at_first, entering[t], 0.0)
+                + jnp.where(at_last, leaving[t][0], 0.0)
+                - jnp.where(at_first, entering[t][1], 0.0)
                 for t in range(2)
             ]
             place = pl.ds(c * N_CHIP + g * N_GY, N_GY)
             cells[place, :LX] = part[0] - roll(along_y, 1, 0)
             cells[place, LX:] = part[1] + along_y
             entering = leaving
-        faces = after
+        raw, faces = next_raw, after
 
     right_high, right_low = split(cells[...])
     result = dot3((high_ref[...], low_ref[...]), (right_high, right_low))

time: 146 us -> 145 us (level)
  Pallas kernels: 9.23 us -> 7.47 us
    pallas_call x3, Pallas kernels: 9.23 us -> 7.47 us  [call(): pl.pallas_call(kernel, out_shape=outs, in_specs=[spec(in_hbm)] * len(args...]
  transfers between devices with their start and end apart: 2 -> 2, of which waited for: 2 -> 2; matrix products, arithmetic and copies ran while one was open for 0% -> 1% of each run, Pallas kernels for 0% -> 0%
where the time goes in v7:
time: 145 us; the launch traced here: 144 us
  blocking collectives  70.7 us (49%)
  waiting for transfers between devices  39.6 us (27%)
  starting transfers between devices  25.7 us (18%)
  Pallas kernels  7.47 us (5%)
    all_to_all x1, blocking collectives, body(): lax.all_to_all(modes.reshape(N_ALL, 4, LX), EVERYWHERE, 0, 0, tiled=True)  70.7 us
    all_to_all x1, waiting for transfers between devices, body(): lax.all_to_all(chunks.reshape(N_CHIP, 1, ROWS * LX), CHIPS, 0, 0, tiled=T...  37.5 us
    all_to_all x1, starting transfers between devices, body(): lax.all_to_all(chunks.reshape(N_CHIP, 1, ROWS * LX), CHIPS, 0, 0, tiled=T...  23.8 us
    pallas_call x3, Pallas kernels, call(): pl.pallas_call(kernel, out_shape=outs, in_specs=[spec(in_hbm)] * len(args...  7.47 us
  transfers between devices with their start and end apart: 2, of which 2 were waited for; matrix products, arithmetic and copies ran while one was open for 1% of the time, Pallas kernels for 0%

profile of v7, /device:TPU:2, one launch (start us, length us, event | category | flops | bytes accessed | tf_op | source)
XLA Modules:
  0.0 144.3 jit_solution(4756783290773060805)
XLA Ops:
  0.0 0.0 copy-start.1
  0.0 3.6 %shard_map.64 = f32[1280,128]{1,0:T(8,128)} custom-call(f32[18,64,128]{2,1,0:T(8,128)} %now_hbm.1, f32[18,64,128]{2,1,0:T(8,128)} %prev_hbm.1, s32[18,64,128]{2,1,0:T(8,128)} %phase_hbm.1, f32[16,64,128]{2,1,0:T(8,128)} %div_hbm.1), custom_call_target="tpu_custom_call" | custom-call | tf_op jit(solution)/shard_map/pallas_call | solution.py:350
  3.6 0.0 copy-start
  3.6 23.8 %all-to-all-start = ((f32[256,1,640]{2,1,0:T(1,128)}), f32[256,1,640]{2,1,0:T(1,128)S(1)}, u32[]{:S(2)}, u32[]{:S(2)}) async-start(f32[256,1,640]{2,1,0:T(1,128)} %bitcast.11), calls=%async_computation | async-start | bytes 1310720 | tf_op jit(solution)/shard_map/all_to_all | solution.py:394
  27.6 0.4 select_multiply_fusion.y_matrix_ref
  28.0 0.3 fusion.9
  28.2 37.5 %all-to-all-done = f32[256,1,640]{2,1,0:T(1,128)S(1)} async-done(((f32[256,1,640]{2,1,0:T(1,128)}), f32[256,1,640]{2,1,0:T(1,128)S(1)}, u32[]{:S(2)}, u32[]{:S(2)}) %all-to-all-start) | async-done | bytes 655392 | tf_op jit(solution)/shard_map/all_to_all | solution.py:394
  65.8 1.9 %collective-permute-start = (f32[1280,128]{1,0:T(8,128)S(1)}, f32[1280,128]{1,0:T(8,128)S(1)}, u32[]{:S(2)}, u32[]{:S(2)}) collective-permute-start(f32[1280,128]{1,0:T(8,128)S(1)} %bitcast.9), channel_id=1, source_target_pairs={{0,32},{32,0},{1,33},{33,1},{2,34},{34,2},{3,35},{35,3},{4,36},{36... | collective-permute-start | bytes 1966088 | tf_op jit(solution)/shard_map/ppermute | solution.py:397
  67.7 2.1 %collective-permute-done.other_ref = f32[1280,128]{1,0:T(8,128)S(1)} collective-permute-done((f32[1280,128]{1,0:T(8,128)S(1)}, f32[1280,128]{1,0:T(8,128)S(1)}, u32[]{:S(2)}, u32[]{:S(2)}) %collective-permute-start) | collective-permute-done | bytes 655392 | tf_op jit(solution)/shard_map/ppermute | solution.py:397
  69.8 0.0 copy-done.1
  69.8 0.0 copy-done
  69.8 1.7 %shard_map.65 = f32[2048,128]{1,0:T(8,128)S(1)} custom-call(f32[1280,128]{1,0:T(8,128)S(1)} %bitcast.10, f32[1280,128]{1,0:T(8,128)S(1)} %collective-permute-done.other_ref, bf16[1024,512]{1,0:T(8,128)(2,1)S(1)} %copy-done.1, bf16[1024,512]{1,0:T(8,128)(2,1)S(1)} %copy-done), custom_call_target="tpu_custom_call" | custom-call | tf_op jit(solution)/shard_map/pallas_call | solution.py:350
  71.5 70.7 %all_to_all.10 = f32[512,4,128]{2,1,0:T(4,128)S(1)} all-to-all(f32[512,4,128]{2,1,0:T(4,128)S(1)} %bitcast.7), channel_id=1, replica_groups=mesh['zh'=2,'x'=4,'c'=2,'zl'=8,'y'=4] {'zh','x','c','zl','y'}, dimensions={0} | all-to-all | bytes 2097152 | tf_op jit(solution)/shard_map/all_to_all | solution.py:408
  142.2 2.2 %shard_map.66 = f32[2,16,64,128]{3,2,1,0:T(8,128)} custom-call(f32[2048,128]{1,0:T(8,128)S(1)} %bitcast.8, f32[128,128]{1,0:T(8,128)S(1)} %select_multiply_fusion.y_matrix_ref, f32[128,128]{1,0:T(8,128)S(1)} %get-tuple-element.17.cos_ref, f32[128,128]{1,0:T(8,128)S(1)} %get-tuple-element.18.sin_ref), custom_call_target="tpu_custom_call" | custom-call | tf_op jit(solution)/shard_map/pallas_call | solution.py:350
  (10 shorter events, 0.1 us)
Async XLA Ops:
  0.0 69.8 %copy-start.1 = (bf16[1024,512]{1,0:T(8,128)(2,1)S(1)}, bf16[1024,512]{1,0:T(8,128)(2,1)}, u32[]{:S(2)}) copy-start(bf16[1024,512]{1,0:T(8,128)(2,1)} %constant.140.clone.high_ref) | copy-start | bytes 3145732
  3.6 66.2 %copy-start = (bf16[1024,512]{1,0:T(8,128)(2,1)S(1)}, bf16[1024,512]{1,0:T(8,128)(2,1)}, u32[]{:S(2)}) copy-start(bf16[1024,512]{1,0:T(8,128)(2,1)} %constant.141.clone.low_ref) | copy-start | bytes 3145732
  3.6 62.2 %all-to-all-start = ((f32[256,1,640]{2,1,0:T(1,128)}), f32[256,1,640]{2,1,0:T(1,128)S(1)}, u32[]{:S(2)}, u32[]{:S(2)}) async-start(f32[256,1,640]{2,1,0:T(1,128)} %bitcast.11), calls=%async_computation | async-start | bytes 1310720 | tf_op jit(solution)/shard_map/all_to_all | solution.py:394
  65.8 4.0 %collective-permute-start = (f32[1280,128]{1,0:T(8,128)S(1)}, f32[1280,128]{1,0:T(8,128)S(1)}, u32[]{:S(2)}, u32[]{:S(2)}) collective-permute-start(f32[1280,128]{1,0:T(8,128)S(1)} %bitcast.9), channel_id=1, source_target_pairs={{0,32},{32,0},{1,33},{33,1},{2,34},{34,2},{3,35},{35,3},{4,36},{36... | collective-permute-start | bytes 1966088 | tf_op jit(solution)/shard_map/ppermute | solution.py:397

commit v8 on v7

--- a/solution.py
+++ b/solution.py
@@ -25,8 +25,10 @@
 CHIPS = ("zh", "x", "zl", "y")
 EVERYWHERE = ("zh", "x", "c", "zl", "y")
 
-QUAD = 7.0 / 16.0 - 7.0 / 9.0
-LIN = 7.0 / 9.0 - QUAD
+LIQUID = 7.0 / 8.0
+MIXED = 7.0 / 9.0
+QUAD = -4.0 / 9.0
+LIN = 11.5 / 9.0
 
 BLOCKS = 16
 BLOCK = LX // BLOCKS
@@ -35,6 +37,7 @@
 TEAMS = PLANES
 ROWS = 5
 GROUP = 4
+PAIR = 2
 QUARTER = LX // 4
 
 
@@ -65,7 +68,7 @@
 
 
 def flux(liquid_a, liquid_b, field_a, field_b):
-    return weighted(liquid_a + liquid_b, field_b - field_a)
+    return jnp.where(liquid_a == liquid_b, liquid_a, MIXED) * (field_b - field_a)
 
 
 def roll(value, by, axis):
@@ -144,7 +147,7 @@
     y_lanes = [within(lane_in, QUARTER * f + owner, BLOCK) for f in range(4)]
 
     def plane(k):
-        return 2.0 * now_ref[k] - prev_ref[k], phase_ref[k].astype(F32)
+        return 2.0 * now_ref[k] - prev_ref[k], jnp.where(phase_ref[k] == 1, LIQUID, 0.0)
 
     for k in range(PLANES):
         if k % GROUP == 0:
@@ -209,9 +212,16 @@
     at_last, at_first = lane == LX - 1, lane == 0
     groups = N_GX // 2
 
-    def rows(c, g, r):
-        place = pl.ds((g % groups) * N_GY * ROWS + r, N_GY, stride=ROWS)
-        return jnp.where(core == c, own_ref[place, :], other_ref[place, :])
+    def row(ref, g, r):
+        return ref[pl.ds((g % groups) * N_GY * ROWS + r, N_GY, stride=ROWS), :]
+
+    def mine(c, g, t):
+        refs = (own_ref, other_ref) if c == 0 else (other_ref, own_ref)
+        return jnp.where(core == 0, row(refs[0], g, t), row(refs[1], g, 2 + t))
+
+    def face_row(c, g):
+        refs = (own_ref, other_ref) if c == 0 else (other_ref, own_ref)
+        return jnp.where(core == 0, row(refs[0], g, 4), row(refs[1], g, 4))
 
     def x_aligned(value):
         return roll(value, 2 * LX - 1 - 4 * core - BLOCK * (team % (4 * BLOCK) == 0), 1)
@@ -228,17 +238,17 @@
         value = weighted(roll(upper + lower, -QUARTER, 1), lower - upper)
         return roll(jnp.where(own_y, value, 0.0), team + (LX - BLOCK // 2), 1)
 
-    raw = [rows(c, 0, 4) for c in range(2)]
+    raw = [face_row(c, 0) for c in range(2)]
     faces = [x_aligned(value) for value in raw]
-    entering = x_parts(x_aligned(rows(1, groups - 1, 4)), faces[0])
+    entering = x_parts(x_aligned(face_row(1, groups - 1)), faces[0])
     for g in range(groups):
-        next_raw = [rows(c, g + 1, 4) for c in range(2)]
+        next_raw = [face_row(c, g + 1) for c in range(2)]
         after = [x_aligned(value) for value in next_raw]
         for c in range(2):
             leaving = x_parts(faces[c], after[0] if c else faces[1])
             along_y = y_part(raw[c])
             part = [
-                rows(c, g, 2 * core + t)
+                mine(c, g, t)
                 + jnp.where(at_last, leaving[t][0], 0.0)
                 - jnp.where(at_first, entering[t][1], 0.0)
                 for t in range(2)
@@ -270,9 +280,9 @@
     )
     block = cell_block()
     copies = []
-    for g in range(PLANES // GROUP):
+    for g in range(PLANES // PAIR):
         group = []
-        for k in range(GROUP * g, GROUP * (g + 1)):
+        for k in range(PAIR * g, PAIR * (g + 1)):
             start = (k // 2) * 4 * LY + (k % 2) * LY
             lines = [
                 turn(x_ref[pl.ds(start + kind, BLOCKS, stride=4), :], block, 1, kind & 1)
@@ -286,15 +296,15 @@
                 jnp.concatenate(
                     [lines[:LY, k * LX : (k + 1) * LX], lines[LY:, k * LX : (k + 1) * LX]], axis=1
                 )
-                for k in range(GROUP)
+                for k in range(PAIR)
             ],
             axis=0,
         )
         modes = dot3(split(lines), x_matrix)
         for part in range(2):
-            for k in range(GROUP):
-                out[part, GROUP * g + k] = modes[k * LY : (k + 1) * LY, part * LX : (part + 1) * LX]
-            planes = (part, pl.ds(g * GROUP, GROUP))
+            for k in range(PAIR):
+                out[part, PAIR * g + k] = modes[k * LY : (k + 1) * LY, part * LX : (part + 1) * LX]
+            planes = (part, pl.ds(g * PAIR, PAIR))
             copies.append(
                 pltpu.make_async_copy(out.at[planes], out_hbm.at[planes], sems.at[g, part])
             )
@@ -413,7 +423,7 @@
         *tables,
         scratch=[
             pltpu.VMEM((2, PLANES, LY, LX), F32),
-            pltpu.SemaphoreType.DMA((PLANES // GROUP, 2)),
+            pltpu.SemaphoreType.DMA((PLANES // PAIR, 2)),
         ],
         out_hbm=True,
     )

time: 145 us -> 144 us (level)
  no operation moved by 1% of the time
where the time goes in v8:
time: 144 us
  blocking collectives  70.7 us (49%)
  waiting for transfers between devices  39.6 us (28%)
  starting transfers between devices  25.7 us (18%)
  Pallas kernels  7.06 us (5%)
    all_to_all x1, blocking collectives, body(): lax.all_to_all(modes.reshape(N_ALL, 4, LX), EVERYWHERE, 0, 0, tiled=True)  70.7 us
    all_to_all x1, waiting for transfers between devices, body(): lax.all_to_all(chunks.reshape(N_CHIP, 1, ROWS * LX), CHIPS, 0, 0, tiled=T...  37.5 us
    all_to_all x1, starting transfers between devices, body(): lax.all_to_all(chunks.reshape(N_CHIP, 1, ROWS * LX), CHIPS, 0, 0, tiled=T...  23.8 us
    pallas_call x3, Pallas kernels, call(): pl.pallas_call(kernel, out_shape=outs, in_specs=[spec(in_hbm)] * len(args...  7.06 us
  transfers between devices with their start and end apart: 2, of which 2 were waited for; matrix products, arithmetic and copies ran while one was open for 1% of the time, Pallas kernels for 0%

profile of v8, /device:TPU:2, one launch (start us, length us, event | category | flops | bytes accessed | tf_op | source)
XLA Modules:
  0.0 143.9 jit_solution(17545890473284826381)
XLA Ops:
  0.0 0.0 copy-start.1
  0.0 3.4 %shard_map.64 = f32[1280,128]{1,0:T(8,128)} custom-call(f32[18,64,128]{2,1,0:T(8,128)} %now_hbm.1, f32[18,64,128]{2,1,0:T(8,128)} %prev_hbm.1, s32[18,64,128]{2,1,0:T(8,128)} %phase_hbm.1, f32[16,64,128]{2,1,0:T(8,128)} %div_hbm.1), custom_call_target="tpu_custom_call" | custom-call | tf_op jit(solution)/shard_map/pallas_call | solution.py:360
  3.4 0.0 copy-start
  3.4 23.8 %all-to-all-start = ((f32[256,1,640]{2,1,0:T(1,128)}), f32[256,1,640]{2,1,0:T(1,128)S(1)}, u32[]{:S(2)}, u32[]{:S(2)}) async-start(f32[256,1,640]{2,1,0:T(1,128)} %bitcast.11), calls=%async_computation | async-start | bytes 1310720 | tf_op jit(solution)/shard_map/all_to_all | solution.py:404
  27.3 0.4 select_multiply_fusion.y_matrix_ref
  27.7 0.3 fusion.9
  28.0 37.5 %all-to-all-done = f32[256,1,640]{2,1,0:T(1,128)S(1)} async-done(((f32[256,1,640]{2,1,0:T(1,128)}), f32[256,1,640]{2,1,0:T(1,128)S(1)}, u32[]{:S(2)}, u32[]{:S(2)}) %all-to-all-start) | async-done | bytes 655392 | tf_op jit(solution)/shard_map/all_to_all | solution.py:404
  65.6 1.9 %collective-permute-start = (f32[1280,128]{1,0:T(8,128)S(1)}, f32[1280,128]{1,0:T(8,128)S(1)}, u32[]{:S(2)}, u32[]{:S(2)}) collective-permute-start(f32[1280,128]{1,0:T(8,128)S(1)} %bitcast.9), channel_id=1, source_target_pairs={{0,32},{32,0},{1,33},{33,1},{2,34},{34,2},{3,35},{35,3},{4,36},{36... | collective-permute-start | bytes 1966088 | tf_op jit(solution)/shard_map/ppermute | solution.py:407
  67.5 2.1 %collective-permute-done.other_ref = f32[1280,128]{1,0:T(8,128)S(1)} collective-permute-done((f32[1280,128]{1,0:T(8,128)S(1)}, f32[1280,128]{1,0:T(8,128)S(1)}, u32[]{:S(2)}, u32[]{:S(2)}) %collective-permute-start) | collective-permute-done | bytes 655392 | tf_op jit(solution)/shard_map/ppermute | solution.py:407
  69.5 0.0 copy-done.1
  69.5 0.0 copy-done
  69.5 1.7 %shard_map.65 = f32[2048,128]{1,0:T(8,128)S(1)} custom-call(f32[1280,128]{1,0:T(8,128)S(1)} %bitcast.10, f32[1280,128]{1,0:T(8,128)S(1)} %collective-permute-done.other_ref, bf16[1024,512]{1,0:T(8,128)(2,1)S(1)} %copy-done.1, bf16[1024,512]{1,0:T(8,128)(2,1)S(1)} %copy-done), custom_call_target="tpu_custom_call" | custom-call | tf_op jit(solution)/shard_map/pallas_call | solution.py:360
  71.3 70.7 %all_to_all.10 = f32[512,4,128]{2,1,0:T(4,128)S(1)} all-to-all(f32[512,4,128]{2,1,0:T(4,128)S(1)} %bitcast.7), channel_id=1, replica_groups=mesh['zh'=2,'x'=4,'c'=2,'zl'=8,'y'=4] {'zh','x','c','zl','y'}, dimensions={0} | all-to-all | bytes 2097152 | tf_op jit(solution)/shard_map/all_to_all | solution.py:418
  142.0 2.0 %shard_map.66 = f32[2,16,64,128]{3,2,1,0:T(8,128)} custom-call(f32[2048,128]{1,0:T(8,128)S(1)} %bitcast.8, f32[128,128]{1,0:T(8,128)S(1)} %select_multiply_fusion.y_matrix_ref, f32[128,128]{1,0:T(8,128)S(1)} %get-tuple-element.17.cos_ref, f32[128,128]{1,0:T(8,128)S(1)} %get-tuple-element.18.sin_ref), custom_call_target="tpu_custom_call" | custom-call | tf_op jit(solution)/shard_map/pallas_call | solution.py:360
  (10 shorter events, 0.1 us)
Async XLA Ops:
  0.0 69.5 %copy-start.1 = (bf16[1024,512]{1,0:T(8,128)(2,1)S(1)}, bf16[1024,512]{1,0:T(8,128)(2,1)}, u32[]{:S(2)}) copy-start(bf16[1024,512]{1,0:T(8,128)(2,1)} %constant.140.clone.high_ref) | copy-start | bytes 3145732
  3.4 66.2 %copy-start = (bf16[1024,512]{1,0:T(8,128)(2,1)S(1)}, bf16[1024,512]{1,0:T(8,128)(2,1)}, u32[]{:S(2)}) copy-start(bf16[1024,512]{1,0:T(8,128)(2,1)} %constant.141.clone.low_ref) | copy-start | bytes 3145732
  3.4 62.2 %all-to-all-start = ((f32[256,1,640]{2,1,0:T(1,128)}), f32[256,1,640]{2,1,0:T(1,128)S(1)}, u32[]{:S(2)}, u32[]{:S(2)}) async-start(f32[256,1,640]{2,1,0:T(1,128)} %bitcast.11), calls=%async_computation | async-start | bytes 1310720 | tf_op jit(solution)/shard_map/all_to_all | solution.py:404
  65.6 4.0 %collective-permute-start = (f32[1280,128]{1,0:T(8,128)S(1)}, f32[1280,128]{1,0:T(8,128)S(1)}, u32[]{:S(2)}, u32[]{:S(2)}) collective-permute-start(f32[1280,128]{1,0:T(8,128)S(1)} %bitcast.9), channel_id=1, source_target_pairs={{0,32},{32,0},{1,33},{33,1},{2,34},{34,2},{3,35},{35,3},{4,36},{36... | collective-permute-start | bytes 1966088 | tf_op jit(solution)/shard_map/ppermute | solution.py:407

commit v9 on v8

--- a/solution.py
+++ b/solution.py
@@ -393,18 +393,16 @@
         out_hbm=True,
         mib=60,
     )
+    chunks = lax.all_to_all(chunks.reshape(N_CHIP, 1, ROWS * LX), CHIPS, 0, 0, tiled=True)
     chunks, rp, rq = lax.optimization_barrier(
         (
-            chunks,
+            chunks.reshape(ROWS * N_CHIP, LX),
             reversal(lax.axis_index(("zh", "x", "c")), 4),
             reversal(lax.axis_index(("zl", "y")), 5),
         )
     )
-    tables = local_tables(rp, rq)
-    chunks = lax.all_to_all(chunks.reshape(N_CHIP, 1, ROWS * LX), CHIPS, 0, 0, tiled=True)
-    chunks, tables = lax.optimization_barrier((chunks, tables))
-    chunks = chunks.reshape(ROWS * N_CHIP, LX)
     other = lax.ppermute(chunks, "c", [(0, 1), (1, 0)])
+    other, tables = lax.optimization_barrier((other, local_tables(rp, rq)))
     high, low = device_tables()
     modes = call(
         device_kernel,

time: 144 us -> 144 us (level)
  no operation moved by 1% of the time
where the time goes in v9:
time: 144 us
  blocking collectives  70.7 us (49%)
  waiting for transfers between devices  39.6 us (28%)
  starting transfers between devices  25.7 us (18%)
  Pallas kernels  7.06 us (5%)
    all_to_all x1, blocking collectives, body(): lax.all_to_all(modes.reshape(N_ALL, 4, LX), EVERYWHERE, 0, 0, tiled=True)  70.7 us
    all_to_all x1, waiting for transfers between devices, body(): lax.all_to_all(chunks.reshape(N_CHIP, 1, ROWS * LX), CHIPS, 0, 0, tiled=T...  38.2 us
    all_to_all x1, starting transfers between devices, body(): lax.all_to_all(chunks.reshape(N_CHIP, 1, ROWS * LX), CHIPS, 0, 0, tiled=T...  23.8 us
    pallas_call x3, Pallas kernels, call(): pl.pallas_call(kernel, out_shape=outs, in_specs=[spec(in_hbm)] * len(args...  7.06 us
  transfers between devices with their start and end apart: 2, of which 2 were waited for; matrix products, arithmetic and copies ran while one was open for 1% of the time, Pallas kernels for 0%

profile of v9, /device:TPU:2, one launch (start us, length us, event | category | flops | bytes accessed | tf_op | source)
XLA Modules:
  0.0 143.9 jit_solution(15001350500170266452)
XLA Ops:
  0.0 0.0 copy-start.1
  0.0 3.4 %shard_map.64 = f32[1280,128]{1,0:T(8,128)} custom-call(f32[18,64,128]{2,1,0:T(8,128)} %now_hbm.1, f32[18,64,128]{2,1,0:T(8,128)} %prev_hbm.1, s32[18,64,128]{2,1,0:T(8,128)} %phase_hbm.1, f32[16,64,128]{2,1,0:T(8,128)} %div_hbm.1), custom_call_target="tpu_custom_call" | custom-call | tf_op jit(solution)/shard_map/pallas_call | solution.py:360
  3.4 0.0 copy-start
  3.4 23.8 %all-to-all-start = ((f32[256,1,640]{2,1,0:T(1,128)}), f32[256,1,640]{2,1,0:T(1,128)S(1)}, u32[]{:S(2)}, u32[]{:S(2)}) async-start(f32[256,1,640]{2,1,0:T(1,128)} %bitcast.11), calls=%async_computation | async-start | bytes 1310720 | tf_op jit(solution)/shard_map/all_to_all | solution.py:396
  27.3 38.2 %all-to-all-done = f32[256,1,640]{2,1,0:T(1,128)S(1)} async-done(((f32[256,1,640]{2,1,0:T(1,128)}), f32[256,1,640]{2,1,0:T(1,128)S(1)}, u32[]{:S(2)}, u32[]{:S(2)}) %all-to-all-start) | async-done | bytes 655392 | tf_op jit(solution)/shard_map/all_to_all | solution.py:396
  65.6 1.9 %collective-permute-start = (f32[1280,128]{1,0:T(8,128)S(1)}, f32[1280,128]{1,0:T(8,128)S(1)}, u32[]{:S(2)}, u32[]{:S(2)}) collective-permute-start(f32[1280,128]{1,0:T(8,128)S(1)} %bitcast.9), channel_id=1, source_target_pairs={{0,32},{32,0},{1,33},{33,1},{2,34},{34,2},{3,35},{35,3},{4,36},{36... | collective-permute-start | bytes 1966088 | tf_op jit(solution)/shard_map/ppermute | solution.py:404
  67.5 0.4 select_multiply_fusion.y_matrix_ref
  67.9 0.3 fusion.9
  68.2 1.4 collective-permute-done.other_ref
  69.5 0.0 copy-done.1
  69.5 0.0 copy-done
  69.5 1.7 %shard_map.65 = f32[2048,128]{1,0:T(8,128)S(1)} custom-call(f32[1280,128]{1,0:T(8,128)S(1)} %bitcast.10, f32[1280,128]{1,0:T(8,128)S(1)} %collective-permute-done.other_ref, bf16[1024,512]{1,0:T(8,128)(2,1)S(1)} %copy-done.1, bf16[1024,512]{1,0:T(8,128)(2,1)S(1)} %copy-done), custom_call_target="tpu_custom_call" | custom-call | tf_op jit(solution)/shard_map/pallas_call | solution.py:360
  71.3 70.7 %all_to_all.10 = f32[512,4,128]{2,1,0:T(4,128)S(1)} all-to-all(f32[512,4,128]{2,1,0:T(4,128)S(1)} %bitcast.7), channel_id=1, replica_groups=mesh['zh'=2,'x'=4,'c'=2,'zl'=8,'y'=4] {'zh','x','c','zl','y'}, dimensions={0} | all-to-all | bytes 2097152 | tf_op jit(solution)/shard_map/all_to_all | solution.py:416
  142.0 2.0 %shard_map.66 = f32[2,16,64,128]{3,2,1,0:T(8,128)} custom-call(f32[2048,128]{1,0:T(8,128)S(1)} %bitcast.8, f32[128,128]{1,0:T(8,128)S(1)} %select_multiply_fusion.y_matrix_ref, f32[128,128]{1,0:T(8,128)S(1)} %get-tuple-element.17.cos_ref, f32[128,128]{1,0:T(8,128)S(1)} %get-tuple-element.18.sin_ref), custom_call_target="tpu_custom_call" | custom-call | tf_op jit(solution)/shard_map/pallas_call | solution.py:360
  (10 shorter events, 0.1 us)
Async XLA Ops:
  0.0 69.5 %copy-start.1 = (bf16[1024,512]{1,0:T(8,128)(2,1)S(1)}, bf16[1024,512]{1,0:T(8,128)(2,1)}, u32[]{:S(2)}) copy-start(bf16[1024,512]{1,0:T(8,128)(2,1)} %constant.140.clone.high_ref) | copy-start | bytes 3145732
  3.4 66.2 %copy-start = (bf16[1024,512]{1,0:T(8,128)(2,1)S(1)}, bf16[1024,512]{1,0:T(8,128)(2,1)}, u32[]{:S(2)}) copy-start(bf16[1024,512]{1,0:T(8,128)(2,1)} %constant.141.clone.low_ref) | copy-start | bytes 3145732
  3.4 62.2 %all-to-all-start = ((f32[256,1,640]{2,1,0:T(1,128)}), f32[256,1,640]{2,1,0:T(1,128)S(1)}, u32[]{:S(2)}, u32[]{:S(2)}) async-start(f32[256,1,640]{2,1,0:T(1,128)} %bitcast.11), calls=%async_computation | async-start | bytes 1310720 | tf_op jit(solution)/shard_map/all_to_all | solution.py:396
  65.6 4.0 %collective-permute-start = (f32[1280,128]{1,0:T(8,128)S(1)}, f32[1280,128]{1,0:T(8,128)S(1)}, u32[]{:S(2)}, u32[]{:S(2)}) collective-permute-start(f32[1280,128]{1,0:T(8,128)S(1)} %bitcast.9), channel_id=1, source_target_pairs={{0,32},{32,0},{1,33},{33,1},{2,34},{34,2},{3,35},{35,3},{4,36},{36... | collective-permute-start | bytes 1966088 | tf_op jit(solution)/shard_map/ppermute | solution.py:404

commit v10 on v9

--- a/solution.py
+++ b/solution.py
@@ -22,7 +22,6 @@
 F32 = jnp.float32
 BF16 = jnp.bfloat16
 
-CHIPS = ("zh", "x", "zl", "y")
 EVERYWHERE = ("zh", "x", "c", "zl", "y")
 
 LIQUID = 7.0 / 8.0
@@ -314,13 +313,13 @@
 
 
 def device_tables():
-    dest = np.arange(N_ALL)
+    dest = np.arange(N_ALL) ^ N_ALL // 2
     rev_p = np.array([reversal(i, 4) for i in range(N_GX)])
     rev_q = np.array([reversal(i, 5) for i in range(N_GY)])
     kx = rev_p[dest // N_GY][:, None]
     ky = rev_q[dest % N_GY][:, None]
     source = np.arange(N_ALL)
-    gx = (2 * (source % N_CHIP // N_GY) + source // N_CHIP)[None]
+    gx = (2 * (source % N_CHIP // N_GY) + source // N_CHIP ^ N_GX // 2)[None]
     gy = (source % N_GY)[None]
     angle = (2 * kx * gx + ky * gy) % N_GY * (2.0 * math.pi / N_GY)
     table = np.concatenate([np.cos(angle), -np.sin(angle)])
@@ -365,6 +364,19 @@
         scratch_shapes=scratch,
         compiler_params=pltpu.CompilerParams(vmem_limit_bytes=mib * 1024 * 1024),
     )(*args)
+
+
+def exchange(chunks, per_core):
+    order = np.arange(N_ALL).reshape(2, 4, 2, 8, 4)[::-1]
+    groups = [order[:, :, c].ravel() for c in range(2)] if per_core else [order.ravel()]
+    return lax.all_to_all(
+        chunks,
+        EVERYWHERE,
+        0,
+        0,
+        axis_index_groups=[[int(device) for device in group] for group in groups],
+        tiled=True,
+    )
 
 
 def shape(*dims):
@@ -393,7 +405,7 @@
         out_hbm=True,
         mib=60,
     )
-    chunks = lax.all_to_all(chunks.reshape(N_CHIP, 1, ROWS * LX), CHIPS, 0, 0, tiled=True)
+    chunks = exchange(chunks.reshape(N_CHIP, 1, ROWS * LX), per_core=True)
     chunks, rp, rq = lax.optimization_barrier(
         (
             chunks.reshape(ROWS * N_CHIP, LX),
@@ -413,7 +425,7 @@
         jnp.asarray(low),
         scratch=[pltpu.VMEM((N_ALL, 2 * LX), F32)],
     )
-    back = lax.all_to_all(modes.reshape(N_ALL, 4, LX), EVERYWHERE, 0, 0, tiled=True)
+    back = exchange(modes.reshape(N_ALL, 4, LX), per_core=False)
     result = call(
         local_kernel,
         shape(2, PLANES, LY, LX),

time: 144 us -> 144 us (level)
  waiting for transfers between devices: 39.6 us -> 31.4 us
  starting transfers between devices: 25.7 us -> 29.8 us
  blocking collectives: 70.7 us -> 74.2 us
    all_to_all x1, waiting for transfers between devices: 38.2 us -> 30 us  [exchange(): lax.all_to_all(chunks, EVERYWHERE, 0, 0, axis_index_groups=[[int(device)...]
    all_to_all x1, starting transfers between devices: 23.8 us -> 27.9 us  [exchange(): lax.all_to_all(chunks, EVERYWHERE, 0, 0, axis_index_groups=[[int(device)...]
    all_to_all x1, blocking collectives: 70.7 us -> 74.2 us  [exchange(): lax.all_to_all(chunks, EVERYWHERE, 0, 0, axis_index_groups=[[int(device)...]
where the time goes in v10:
time: 144 us; the launch traced here: 143 us
  blocking collectives  74.2 us (52%)
  waiting for transfers between devices  31.4 us (22%)
  starting transfers between devices  29.8 us (21%)
  Pallas kernels  7.06 us (5%)
    all_to_all x1, blocking collectives, exchange(): lax.all_to_all(chunks, EVERYWHERE, 0, 0, axis_index_groups=[[int(device)...  74.2 us
    all_to_all x1, waiting for transfers between devices, exchange(): lax.all_to_all(chunks, EVERYWHERE, 0, 0, axis_index_groups=[[int(device)...  30 us
    all_to_all x1, starting transfers between devices, exchange(): lax.all_to_all(chunks, EVERYWHERE, 0, 0, axis_index_groups=[[int(device)...  27.9 us
    pallas_call x3, Pallas kernels, call(): pl.pallas_call(kernel, out_shape=outs, in_specs=[spec(in_hbm)] * len(args...  7.06 us
  transfers between devices with their start and end apart: 2, of which 2 were waited for; matrix products, arithmetic and copies ran while one was open for 1% of the time, Pallas kernels for 0%

profile of v10, /device:TPU:2, one launch (start us, length us, event | category | flops | bytes accessed | tf_op | source)
XLA Modules:
  0.0 143.3 jit_solution(410165252420833261)
XLA Ops:
  0.0 0.0 copy-start.1
  0.0 3.4 %shard_map.64 = f32[1280,128]{1,0:T(8,128)} custom-call(f32[18,64,128]{2,1,0:T(8,128)} %now_hbm.1, f32[18,64,128]{2,1,0:T(8,128)} %prev_hbm.1, s32[18,64,128]{2,1,0:T(8,128)} %phase_hbm.1, f32[16,64,128]{2,1,0:T(8,128)} %div_hbm.1), custom_call_target="tpu_custom_call" | custom-call | tf_op jit(solution)/shard_map/pallas_call | solution.py:359
  3.4 0.0 copy-start
  3.4 27.9 %all-to-all-start = ((f32[256,1,640]{2,1,0:T(1,128)}), f32[256,1,640]{2,1,0:T(1,128)S(1)}, u32[]{:S(2)}, u32[]{:S(2)}) async-start(f32[256,1,640]{2,1,0:T(1,128)} %bitcast.11), calls=%async_computation | async-start | bytes 1310720 | tf_op jit(solution)/shard_map/all_to_all | solution.py:372
  31.4 30.0 %all-to-all-done = f32[256,1,640]{2,1,0:T(1,128)S(1)} async-done(((f32[256,1,640]{2,1,0:T(1,128)}), f32[256,1,640]{2,1,0:T(1,128)S(1)}, u32[]{:S(2)}, u32[]{:S(2)}) %all-to-all-start) | async-done | bytes 655392 | tf_op jit(solution)/shard_map/all_to_all | solution.py:372
  61.4 1.9 %collective-permute-start = (f32[1280,128]{1,0:T(8,128)S(1)}, f32[1280,128]{1,0:T(8,128)S(1)}, u32[]{:S(2)}, u32[]{:S(2)}) collective-permute-start(f32[1280,128]{1,0:T(8,128)S(1)} %bitcast.9), channel_id=1, source_target_pairs={{0,32},{32,0},{1,33},{33,1},{2,34},{34,2},{3,35},{35,3},{4,36},{36... | collective-permute-start | bytes 1966088 | tf_op jit(solution)/shard_map/ppermute | solution.py:416
  63.4 0.4 select_multiply_fusion.y_matrix_ref
  63.8 0.3 fusion.9
  64.1 1.4 collective-permute-done.other_ref
  65.4 0.0 copy-done.1
  65.4 0.0 copy-done
  65.4 1.7 %shard_map.65 = f32[2048,128]{1,0:T(8,128)S(1)} custom-call(f32[1280,128]{1,0:T(8,128)S(1)} %bitcast.10, f32[1280,128]{1,0:T(8,128)S(1)} %collective-permute-done.other_ref, bf16[1024,512]{1,0:T(8,128)(2,1)S(1)} %copy-done.1, bf16[1024,512]{1,0:T(8,128)(2,1)S(1)} %copy-done), custom_call_target="tpu_custom_call" | custom-call | tf_op jit(solution)/shard_map/pallas_call | solution.py:359
  67.1 74.2 %all_to_all.10 = f32[512,4,128]{2,1,0:T(4,128)S(1)} all-to-all(f32[512,4,128]{2,1,0:T(4,128)S(1)} %bitcast.7), channel_id=1, replica_groups={{256,257,258,259,260,261,262,263,264,265,266,267,268,269,270,271,272,27..., dimensions={0} | all-to-all | bytes 2097152 | tf_op jit(solution)/shard_map/all_to_all | solution.py:372
  141.3 2.0 %shard_map.66 = f32[2,16,64,128]{3,2,1,0:T(8,128)} custom-call(f32[2048,128]{1,0:T(8,128)S(1)} %bitcast.8, f32[128,128]{1,0:T(8,128)S(1)} %select_multiply_fusion.y_matrix_ref, f32[128,128]{1,0:T(8,128)S(1)} %get-tuple-element.17.cos_ref, f32[128,128]{1,0:T(8,128)S(1)} %get-tuple-element.18.sin_ref), custom_call_target="tpu_custom_call" | custom-call | tf_op jit(solution)/shard_map/pallas_call | solution.py:359
  (10 shorter events, 0.1 us)
Async XLA Ops:
  0.0 65.4 %copy-start.1 = (bf16[1024,512]{1,0:T(8,128)(2,1)S(1)}, bf16[1024,512]{1,0:T(8,128)(2,1)}, u32[]{:S(2)}) copy-start(bf16[1024,512]{1,0:T(8,128)(2,1)} %constant.140.clone.high_ref) | copy-start | bytes 3145732
  3.4 62.0 %copy-start = (bf16[1024,512]{1,0:T(8,128)(2,1)S(1)}, bf16[1024,512]{1,0:T(8,128)(2,1)}, u32[]{:S(2)}) copy-start(bf16[1024,512]{1,0:T(8,128)(2,1)} %constant.141.clone.low_ref) | copy-start | bytes 3145732
  3.4 58.0 %all-to-all-start = ((f32[256,1,640]{2,1,0:T(1,128)}), f32[256,1,640]{2,1,0:T(1,128)S(1)}, u32[]{:S(2)}, u32[]{:S(2)}) async-start(f32[256,1,640]{2,1,0:T(1,128)} %bitcast.11), calls=%async_computation | async-start | bytes 1310720 | tf_op jit(solution)/shard_map/all_to_all | solution.py:372
  61.4 4.0 %collective-permute-start = (f32[1280,128]{1,0:T(8,128)S(1)}, f32[1280,128]{1,0:T(8,128)S(1)}, u32[]{:S(2)}, u32[]{:S(2)}) collective-permute-start(f32[1280,128]{1,0:T(8,128)S(1)} %bitcast.9), channel_id=1, source_target_pairs={{0,32},{32,0},{1,33},{33,1},{2,34},{34,2},{3,35},{35,3},{4,36},{36... | collective-permute-start | bytes 1966088 | tf_op jit(solution)/shard_map/ppermute | solution.py:416

commit v11 on v9

--- a/solution.py
+++ b/solution.py
@@ -22,7 +22,6 @@
 F32 = jnp.float32
 BF16 = jnp.bfloat16
 
-CHIPS = ("zh", "x", "zl", "y")
 EVERYWHERE = ("zh", "x", "c", "zl", "y")
 
 LIQUID = 7.0 / 8.0
@@ -283,7 +282,7 @@
     for g in range(PLANES // PAIR):
         group = []
         for k in range(PAIR * g, PAIR * (g + 1)):
-            start = (k // 2) * 4 * LY + (k % 2) * LY
+            start = (k // 2 ^ TEAMS // 4) * 4 * LY + (k % 2) * LY
             lines = [
                 turn(x_ref[pl.ds(start + kind, BLOCKS, stride=4), :], block, 1, kind & 1)
                 for kind in range(4)
@@ -320,7 +319,7 @@
     kx = rev_p[dest // N_GY][:, None]
     ky = rev_q[dest % N_GY][:, None]
     source = np.arange(N_ALL)
-    gx = (2 * (source % N_CHIP // N_GY) + source // N_CHIP)[None]
+    gx = (2 * (source % N_CHIP // N_GY) + source // N_CHIP ^ N_GX // 2)[None]
     gy = (source % N_GY)[None]
     angle = (2 * kx * gx + ky * gy) % N_GY * (2.0 * math.pi / N_GY)
     table = np.concatenate([np.cos(angle), -np.sin(angle)])
@@ -365,6 +364,12 @@
         scratch_shapes=scratch,
         compiler_params=pltpu.CompilerParams(vmem_limit_bytes=mib * 1024 * 1024),
     )(*args)
+
+
+def first_exchange(chunks):
+    order = np.arange(N_ALL).reshape(2, 4, 2, 8, 4)[::-1]
+    groups = [[int(device) for device in order[:, :, c].ravel()] for c in range(2)]
+    return lax.all_to_all(chunks, EVERYWHERE, 0, 0, axis_index_groups=groups, tiled=True)
 
 
 def shape(*dims):
@@ -393,7 +398,7 @@
         out_hbm=True,
         mib=60,
     )
-    chunks = lax.all_to_all(chunks.reshape(N_CHIP, 1, ROWS * LX), CHIPS, 0, 0, tiled=True)
+    chunks = first_exchange(chunks.reshape(N_CHIP, 1, ROWS * LX))
     chunks, rp, rq = lax.optimization_barrier(
         (
             chunks.reshape(ROWS * N_CHIP, LX),

time: 144 us -> 144 us (level)
  waiting for transfers between devices: 39.6 us -> 31.4 us
  starting transfers between devices: 25.7 us -> 29.8 us
  blocking collectives: 70.7 us -> 74.2 us
    all_to_all x1, waiting for transfers between devices: 38.2 us -> 30 us  [first_exchange(): lax.all_to_all(chunks, EVERYWHERE, 0, 0, axis_index_groups=groups, tiled=...]
    all_to_all x1, starting transfers between devices: 23.8 us -> 27.9 us  [first_exchange(): lax.all_to_all(chunks, EVERYWHERE, 0, 0, axis_index_groups=groups, tiled=...]
    all_to_all x1, blocking collectives: 70.7 us -> 74.2 us  [body(): lax.all_to_all(modes.reshape(N_ALL, 4, LX), EVERYWHERE, 0, 0, tiled=True)]
where the time goes in v11:
time: 144 us; the launch traced here: 143 us
  blocking collectives  74.2 us (52%)
  waiting for transfers between devices  31.4 us (22%)
  starting transfers between devices  29.8 us (21%)
  Pallas kernels  7.06 us (5%)
    all_to_all x1, blocking collectives, body(): lax.all_to_all(modes.reshape(N_ALL, 4, LX), EVERYWHERE, 0, 0, tiled=True)  74.2 us
    all_to_all x1, waiting for transfers between devices, first_exchange(): lax.all_to_all(chunks, EVERYWHERE, 0, 0, axis_index_groups=groups, tiled=...  30 us
    all_to_all x1, starting transfers between devices, first_exchange(): lax.all_to_all(chunks, EVERYWHERE, 0, 0, axis_index_groups=groups, tiled=...  27.9 us
    pallas_call x3, Pallas kernels, call(): pl.pallas_call(kernel, out_shape=outs, in_specs=[spec(in_hbm)] * len(args...  7.06 us
  transfers between devices with their start and end apart: 2, of which 2 were waited for; matrix products, arithmetic and copies ran while one was open for 1% of the time, Pallas kernels for 0%

profile of v11, /device:TPU:2, one launch (start us, length us, event | category | flops | bytes accessed | tf_op | source)
XLA Modules:
  0.0 143.3 jit_solution(7608077531269155424)
XLA Ops:
  0.0 0.0 copy-start.1
  0.0 3.4 %shard_map.64 = f32[1280,128]{1,0:T(8,128)} custom-call(f32[18,64,128]{2,1,0:T(8,128)} %now_hbm.1, f32[18,64,128]{2,1,0:T(8,128)} %prev_hbm.1, s32[18,64,128]{2,1,0:T(8,128)} %phase_hbm.1, f32[16,64,128]{2,1,0:T(8,128)} %div_hbm.1), custom_call_target="tpu_custom_call" | custom-call | tf_op jit(solution)/shard_map/pallas_call | solution.py:359
  3.4 0.0 copy-start
  3.4 27.9 %all-to-all-start = ((f32[256,1,640]{2,1,0:T(1,128)}), f32[256,1,640]{2,1,0:T(1,128)S(1)}, u32[]{:S(2)}, u32[]{:S(2)}) async-start(f32[256,1,640]{2,1,0:T(1,128)} %bitcast.11), calls=%async_computation | async-start | bytes 1310720 | tf_op jit(solution)/shard_map/all_to_all | solution.py:372
  31.4 30.0 %all-to-all-done = f32[256,1,640]{2,1,0:T(1,128)S(1)} async-done(((f32[256,1,640]{2,1,0:T(1,128)}), f32[256,1,640]{2,1,0:T(1,128)S(1)}, u32[]{:S(2)}, u32[]{:S(2)}) %all-to-all-start) | async-done | bytes 655392 | tf_op jit(solution)/shard_map/all_to_all | solution.py:372
  61.4 1.9 %collective-permute-start = (f32[1280,128]{1,0:T(8,128)S(1)}, f32[1280,128]{1,0:T(8,128)S(1)}, u32[]{:S(2)}, u32[]{:S(2)}) collective-permute-start(f32[1280,128]{1,0:T(8,128)S(1)} %bitcast.9), channel_id=1, source_target_pairs={{0,32},{32,0},{1,33},{33,1},{2,34},{34,2},{3,35},{35,3},{4,36},{36... | collective-permute-start | bytes 1966088 | tf_op jit(solution)/shard_map/ppermute | solution.py:409
  63.4 0.4 select_multiply_fusion.y_matrix_ref
  63.8 0.3 fusion.9
  64.1 1.4 collective-permute-done.other_ref
  65.4 0.0 copy-done.1
  65.4 0.0 copy-done
  65.4 1.7 %shard_map.65 = f32[2048,128]{1,0:T(8,128)S(1)} custom-call(f32[1280,128]{1,0:T(8,128)S(1)} %bitcast.10, f32[1280,128]{1,0:T(8,128)S(1)} %collective-permute-done.other_ref, bf16[1024,512]{1,0:T(8,128)(2,1)S(1)} %copy-done.1, bf16[1024,512]{1,0:T(8,128)(2,1)S(1)} %copy-done), custom_call_target="tpu_custom_call" | custom-call | tf_op jit(solution)/shard_map/pallas_call | solution.py:359
  67.1 74.2 %all_to_all.10 = f32[512,4,128]{2,1,0:T(4,128)S(1)} all-to-all(f32[512,4,128]{2,1,0:T(4,128)S(1)} %bitcast.7), channel_id=1, replica_groups=mesh['zh'=2,'x'=4,'c'=2,'zl'=8,'y'=4] {'zh','x','c','zl','y'}, dimensions={0} | all-to-all | bytes 2097152 | tf_op jit(solution)/shard_map/all_to_all | solution.py:421
  141.3 2.0 %shard_map.66 = f32[2,16,64,128]{3,2,1,0:T(8,128)} custom-call(f32[2048,128]{1,0:T(8,128)S(1)} %bitcast.8, f32[128,128]{1,0:T(8,128)S(1)} %select_multiply_fusion.y_matrix_ref, f32[128,128]{1,0:T(8,128)S(1)} %get-tuple-element.17.cos_ref, f32[128,128]{1,0:T(8,128)S(1)} %get-tuple-element.18.sin_ref), custom_call_target="tpu_custom_call" | custom-call | tf_op jit(solution)/shard_map/pallas_call | solution.py:359
  (10 shorter events, 0.1 us)
Async XLA Ops:
  0.0 65.4 %copy-start.1 = (bf16[1024,512]{1,0:T(8,128)(2,1)S(1)}, bf16[1024,512]{1,0:T(8,128)(2,1)}, u32[]{:S(2)}) copy-start(bf16[1024,512]{1,0:T(8,128)(2,1)} %constant.140.clone.high_ref) | copy-start | bytes 3145732
  3.4 62.0 %copy-start = (bf16[1024,512]{1,0:T(8,128)(2,1)S(1)}, bf16[1024,512]{1,0:T(8,128)(2,1)}, u32[]{:S(2)}) copy-start(bf16[1024,512]{1,0:T(8,128)(2,1)} %constant.141.clone.low_ref) | copy-start | bytes 3145732
  3.4 58.0 %all-to-all-start = ((f32[256,1,640]{2,1,0:T(1,128)}), f32[256,1,640]{2,1,0:T(1,128)S(1)}, u32[]{:S(2)}, u32[]{:S(2)}) async-start(f32[256,1,640]{2,1,0:T(1,128)} %bitcast.11), calls=%async_computation | async-start | bytes 1310720 | tf_op jit(solution)/shard_map/all_to_all | solution.py:372
  61.4 4.0 %collective-permute-start = (f32[1280,128]{1,0:T(8,128)S(1)}, f32[1280,128]{1,0:T(8,128)S(1)}, u32[]{:S(2)}, u32[]{:S(2)}) collective-permute-start(f32[1280,128]{1,0:T(8,128)S(1)} %bitcast.9), channel_id=1, source_target_pairs={{0,32},{32,0},{1,33},{33,1},{2,34},{34,2},{3,35},{35,3},{4,36},{36... | collective-permute-start | bytes 1966088 | tf_op jit(solution)/shard_map/ppermute | solution.py:409

commit v12 on v11

--- a/solution.py
+++ b/solution.py
@@ -282,7 +282,7 @@
     for g in range(PLANES // PAIR):
         group = []
         for k in range(PAIR * g, PAIR * (g + 1)):
-            start = (k // 2 ^ TEAMS // 4) * 4 * LY + (k % 2) * LY
+            start = (k // 2 ^ TEAMS // 4) * 4 * LY + (k % 2 ^ 1) * LY
             lines = [
                 turn(x_ref[pl.ds(start + kind, BLOCKS, stride=4), :], block, 1, kind & 1)
                 for kind in range(4)
@@ -320,7 +320,7 @@
     ky = rev_q[dest % N_GY][:, None]
     source = np.arange(N_ALL)
     gx = (2 * (source % N_CHIP // N_GY) + source // N_CHIP ^ N_GX // 2)[None]
-    gy = (source % N_GY)[None]
+    gy = (source % N_GY ^ N_GY // 2)[None]
     angle = (2 * kx * gx + ky * gy) % N_GY * (2.0 * math.pi / N_GY)
     table = np.concatenate([np.cos(angle), -np.sin(angle)])
     high = table.astype(ml_dtypes.bfloat16)
@@ -367,7 +367,7 @@
 
 
 def first_exchange(chunks):
-    order = np.arange(N_ALL).reshape(2, 4, 2, 8, 4)[::-1]
+    order = np.roll(np.arange(N_ALL).reshape(2, 4, 2, 8, 4)[::-1], 4, axis=3)
     groups = [[int(device) for device in order[:, :, c].ravel()] for c in range(2)]
     return lax.all_to_all(chunks, EVERYWHERE, 0, 0, axis_index_groups=groups, tiled=True)
 

time: 144 us -> 141 us (0.979)
  waiting for transfers between devices: 31.4 us -> 37.1 us
  blocking collectives: 74.2 us -> 69.1 us
  starting transfers between devices: 29.8 us -> 26.7 us
    all_to_all x1, waiting for transfers between devices: 30 us -> 35.7 us  [first_exchange(): lax.all_to_all(chunks, EVERYWHERE, 0, 0, axis_index_groups=groups, tiled=...]
    all_to_all x1, blocking collectives: 74.2 us -> 69.1 us  [body(): lax.all_to_all(modes.reshape(N_ALL, 4, LX), EVERYWHERE, 0, 0, tiled=True)]
    all_to_all x1, starting transfers between devices: 27.9 us -> 24.8 us  [first_exchange(): lax.all_to_all(chunks, EVERYWHERE, 0, 0, axis_index_groups=groups, tiled=...]
where the time goes in v12:
time: 141 us
  blocking collectives  69.1 us (49%)
  waiting for transfers between devices  37.1 us (26%)
  starting transfers between devices  26.7 us (19%)
  Pallas kernels  7.06 us (5%)
    all_to_all x1, blocking collectives, body(): lax.all_to_all(modes.reshape(N_ALL, 4, LX), EVERYWHERE, 0, 0, tiled=True)  69.1 us
    all_to_all x1, waiting for transfers between devices, first_exchange(): lax.all_to_all(chunks, EVERYWHERE, 0, 0, axis_index_groups=groups, tiled=...  35.7 us
    all_to_all x1, starting transfers between devices, first_exchange(): lax.all_to_all(chunks, EVERYWHERE, 0, 0, axis_index_groups=groups, tiled=...  24.8 us
    pallas_call x3, Pallas kernels, call(): pl.pallas_call(kernel, out_shape=outs, in_specs=[spec(in_hbm)] * len(args...  7.06 us
  transfers between devices with their start and end apart: 2, of which 2 were waited for; matrix products, arithmetic and copies ran while one was open for 1% of the time, Pallas kernels for 0%

profile of v12, /device:TPU:2, one launch (start us, length us, event | category | flops | bytes accessed | tf_op | source)
XLA Modules:
  0.0 140.9 jit_solution(16898070684008055464)
XLA Ops:
  0.0 0.0 copy-start.1
  0.0 3.4 %shard_map.64 = f32[1280,128]{1,0:T(8,128)} custom-call(f32[18,64,128]{2,1,0:T(8,128)} %now_hbm.1, f32[18,64,128]{2,1,0:T(8,128)} %prev_hbm.1, s32[18,64,128]{2,1,0:T(8,128)} %phase_hbm.1, f32[16,64,128]{2,1,0:T(8,128)} %div_hbm.1), custom_call_target="tpu_custom_call" | custom-call | tf_op jit(solution)/shard_map/pallas_call | solution.py:359
  3.4 0.0 copy-start
  3.4 24.8 %all-to-all-start = ((f32[256,1,640]{2,1,0:T(1,128)}), f32[256,1,640]{2,1,0:T(1,128)S(1)}, u32[]{:S(2)}, u32[]{:S(2)}) async-start(f32[256,1,640]{2,1,0:T(1,128)} %bitcast.11), calls=%async_computation | async-start | bytes 1310720 | tf_op jit(solution)/shard_map/all_to_all | solution.py:372
  28.3 35.7 %all-to-all-done = f32[256,1,640]{2,1,0:T(1,128)S(1)} async-done(((f32[256,1,640]{2,1,0:T(1,128)}), f32[256,1,640]{2,1,0:T(1,128)S(1)}, u32[]{:S(2)}, u32[]{:S(2)}) %all-to-all-start) | async-done | bytes 655392 | tf_op jit(solution)/shard_map/all_to_all | solution.py:372
  64.1 1.9 %collective-permute-start = (f32[1280,128]{1,0:T(8,128)S(1)}, f32[1280,128]{1,0:T(8,128)S(1)}, u32[]{:S(2)}, u32[]{:S(2)}) collective-permute-start(f32[1280,128]{1,0:T(8,128)S(1)} %bitcast.9), channel_id=1, source_target_pairs={{0,32},{32,0},{1,33},{33,1},{2,34},{34,2},{3,35},{35,3},{4,36},{36... | collective-permute-start | bytes 1966088 | tf_op jit(solution)/shard_map/ppermute | solution.py:409
  66.0 0.4 select_multiply_fusion.y_matrix_ref
  66.4 0.3 fusion.9
  66.7 1.4 collective-permute-done.other_ref
  68.0 0.0 copy-done.1
  68.0 0.0 copy-done
  68.0 1.7 %shard_map.65 = f32[2048,128]{1,0:T(8,128)S(1)} custom-call(f32[1280,128]{1,0:T(8,128)S(1)} %bitcast.10, f32[1280,128]{1,0:T(8,128)S(1)} %collective-permute-done.other_ref, bf16[1024,512]{1,0:T(8,128)(2,1)S(1)} %copy-done.1, bf16[1024,512]{1,0:T(8,128)(2,1)S(1)} %copy-done), custom_call_target="tpu_custom_call" | custom-call | tf_op jit(solution)/shard_map/pallas_call | solution.py:359
  69.8 69.1 %all_to_all.10 = f32[512,4,128]{2,1,0:T(4,128)S(1)} all-to-all(f32[512,4,128]{2,1,0:T(4,128)S(1)} %bitcast.7), channel_id=1, replica_groups=mesh['zh'=2,'x'=4,'c'=2,'zl'=8,'y'=4] {'zh','x','c','zl','y'}, dimensions={0} | all-to-all | bytes 2097152 | tf_op jit(solution)/shard_map/all_to_all | solution.py:421
  138.9 2.0 %shard_map.66 = f32[2,16,64,128]{3,2,1,0:T(8,128)} custom-call(f32[2048,128]{1,0:T(8,128)S(1)} %bitcast.8, f32[128,128]{1,0:T(8,128)S(1)} %select_multiply_fusion.y_matrix_ref, f32[128,128]{1,0:T(8,128)S(1)} %get-tuple-element.17.cos_ref, f32[128,128]{1,0:T(8,128)S(1)} %get-tuple-element.18.sin_ref), custom_call_target="tpu_custom_call" | custom-call | tf_op jit(solution)/shard_map/pallas_call | solution.py:359
  (10 shorter events, 0.1 us)
Async XLA Ops:
  0.0 68.0 %copy-start.1 = (bf16[1024,512]{1,0:T(8,128)(2,1)S(1)}, bf16[1024,512]{1,0:T(8,128)(2,1)}, u32[]{:S(2)}) copy-start(bf16[1024,512]{1,0:T(8,128)(2,1)} %constant.140.clone.high_ref) | copy-start | bytes 3145732
  3.4 64.7 %copy-start = (bf16[1024,512]{1,0:T(8,128)(2,1)S(1)}, bf16[1024,512]{1,0:T(8,128)(2,1)}, u32[]{:S(2)}) copy-start(bf16[1024,512]{1,0:T(8,128)(2,1)} %constant.141.clone.low_ref) | copy-start | bytes 3145732
  3.4 60.7 %all-to-all-start = ((f32[256,1,640]{2,1,0:T(1,128)}), f32[256,1,640]{2,1,0:T(1,128)S(1)}, u32[]{:S(2)}, u32[]{:S(2)}) async-start(f32[256,1,640]{2,1,0:T(1,128)} %bitcast.11), calls=%async_computation | async-start | bytes 1310720 | tf_op jit(solution)/shard_map/all_to_all | solution.py:372
  64.1 4.0 %collective-permute-start = (f32[1280,128]{1,0:T(8,128)S(1)}, f32[1280,128]{1,0:T(8,128)S(1)}, u32[]{:S(2)}, u32[]{:S(2)}) collective-permute-start(f32[1280,128]{1,0:T(8,128)S(1)} %bitcast.9), channel_id=1, source_target_pairs={{0,32},{32,0},{1,33},{33,1},{2,34},{34,2},{3,35},{35,3},{4,36},{36... | collective-permute-start | bytes 1966088 | tf_op jit(solution)/shard_map/ppermute | solution.py:409

commit v13 on v9

--- a/solution.py
+++ b/solution.py
@@ -22,7 +22,6 @@
 F32 = jnp.float32
 BF16 = jnp.bfloat16
 
-CHIPS = ("zh", "x", "zl", "y")
 EVERYWHERE = ("zh", "x", "c", "zl", "y")
 
 LIQUID = 7.0 / 8.0
@@ -37,6 +36,8 @@
 TEAMS = PLANES
 ROWS = 5
 GROUP = 4
+FIRST_CHIP = 6
+FIRST_Y = 18
 PAIR = 2
 QUARTER = LX // 4
 
@@ -207,7 +208,8 @@
 def device_kernel(own_ref, other_ref, high_ref, low_ref, out, cells):
     lane = lanes_of(N_GY)
     core = lax.axis_index("c")
-    team = (lax.axis_index("zl") * 4 + lax.axis_index("y")) % TEAMS * BLOCK
+    own_place = lax.axis_index("zl") * 4 + lax.axis_index("y") + (N_GY - FIRST_Y)
+    team = own_place % TEAMS * BLOCK
     own_y = (lane < BLOCK) & (core == 0)
     at_last, at_first = lane == LX - 1, lane == 0
     groups = N_GX // 2
@@ -313,15 +315,19 @@
         copy.wait()
 
 
+def listed():
+    devices = np.arange(N_ALL).reshape(N_GX // 2, 2, N_GY)
+    return np.roll(devices, (-FIRST_CHIP, -FIRST_Y), axis=(0, 2))
+
+
 def device_tables():
-    dest = np.arange(N_ALL)
+    dest = listed().ravel()
     rev_p = np.array([reversal(i, 4) for i in range(N_GX)])
     rev_q = np.array([reversal(i, 5) for i in range(N_GY)])
     kx = rev_p[dest // N_GY][:, None]
     ky = rev_q[dest % N_GY][:, None]
-    source = np.arange(N_ALL)
-    gx = (2 * (source % N_CHIP // N_GY) + source // N_CHIP)[None]
-    gy = (source % N_GY)[None]
+    source = listed().transpose(1, 0, 2).ravel()[None]
+    gx, gy = source // N_GY, source % N_GY
     angle = (2 * kx * gx + ky * gy) % N_GY * (2.0 * math.pi / N_GY)
     table = np.concatenate([np.cos(angle), -np.sin(angle)])
     high = table.astype(ml_dtypes.bfloat16)
@@ -365,6 +371,13 @@
         scratch_shapes=scratch,
         compiler_params=pltpu.CompilerParams(vmem_limit_bytes=mib * 1024 * 1024),
     )(*args)
+
+
+def exchange(chunks, per_core):
+    order = listed()
+    groups = [order[:, c].ravel() for c in range(2)] if per_core else [order.ravel()]
+    groups = [[int(device) for device in group] for group in groups]
+    return lax.all_to_all(chunks, EVERYWHERE, 0, 0, axis_index_groups=groups, tiled=True)
 
 
 def shape(*dims):
@@ -393,7 +406,7 @@
         out_hbm=True,
         mib=60,
     )
-    chunks = lax.all_to_all(chunks.reshape(N_CHIP, 1, ROWS * LX), CHIPS, 0, 0, tiled=True)
+    chunks = exchange(chunks.reshape(N_CHIP, 1, ROWS * LX), per_core=True)
     chunks, rp, rq = lax.optimization_barrier(
         (
             chunks.reshape(ROWS * N_CHIP, LX),
@@ -413,7 +426,7 @@
         jnp.asarray(low),
         scratch=[pltpu.VMEM((N_ALL, 2 * LX), F32)],
     )
-    back = lax.all_to_all(modes.reshape(N_ALL, 4, LX), EVERYWHERE, 0, 0, tiled=True)
+    back = exchange(modes.reshape(N_ALL, 4, LX), per_core=False)
     result = call(
         local_kernel,
         shape(2, PLANES, LY, LX),

time: 144 us -> 141 us (0.979)
  waiting for transfers between devices: 39.6 us -> 34.1 us
    all_to_all x1, waiting for transfers between devices: 38.2 us -> 32.7 us  [exchange(): lax.all_to_all(chunks, EVERYWHERE, 0, 0, axis_index_groups=groups, tiled=...]
where the time goes in v13:
time: 141 us; the launch traced here: 140 us
  blocking collectives  72 us (51%)
  waiting for transfers between devices  34.1 us (24%)
  starting transfers between devices  26.1 us (19%)
  Pallas kernels  7.07 us (5%)
    all_to_all x1, blocking collectives, exchange(): lax.all_to_all(chunks, EVERYWHERE, 0, 0, axis_index_groups=groups, tiled=...  72 us
    all_to_all x1, waiting for transfers between devices, exchange(): lax.all_to_all(chunks, EVERYWHERE, 0, 0, axis_index_groups=groups, tiled=...  32.7 us
    all_to_all x1, starting transfers between devices, exchange(): lax.all_to_all(chunks, EVERYWHERE, 0, 0, axis_index_groups=groups, tiled=...  24.2 us
    pallas_call x3, Pallas kernels, call(): pl.pallas_call(kernel, out_shape=outs, in_specs=[spec(in_hbm)] * len(args...  7.07 us
  transfers between devices with their start and end apart: 2, of which 2 were waited for; matrix products, arithmetic and copies ran while one was open for 1% of the time, Pallas kernels for 0%

profile of v13, /device:TPU:2, one launch (start us, length us, event | category | flops | bytes accessed | tf_op | source)
XLA Modules:
  0.0 140.1 jit_solution(11101089693166452166)
XLA Ops:
  0.0 0.0 copy-start.1
  0.0 3.4 %shard_map.64 = f32[1280,128]{1,0:T(8,128)} custom-call(f32[18,64,128]{2,1,0:T(8,128)} %now_hbm.1, f32[18,64,128]{2,1,0:T(8,128)} %prev_hbm.1, s32[18,64,128]{2,1,0:T(8,128)} %phase_hbm.1, f32[16,64,128]{2,1,0:T(8,128)} %div_hbm.1), custom_call_target="tpu_custom_call" | custom-call | tf_op jit(solution)/shard_map/pallas_call | solution.py:366
  3.4 0.0 copy-start
  3.4 24.2 %all-to-all-start = ((f32[256,1,640]{2,1,0:T(1,128)}), f32[256,1,640]{2,1,0:T(1,128)S(1)}, u32[]{:S(2)}, u32[]{:S(2)}) async-start(f32[256,1,640]{2,1,0:T(1,128)} %bitcast.11), calls=%async_computation | async-start | bytes 1310720 | tf_op jit(solution)/shard_map/all_to_all | solution.py:380
  27.7 32.7 %all-to-all-done = f32[256,1,640]{2,1,0:T(1,128)S(1)} async-done(((f32[256,1,640]{2,1,0:T(1,128)}), f32[256,1,640]{2,1,0:T(1,128)S(1)}, u32[]{:S(2)}, u32[]{:S(2)}) %all-to-all-start) | async-done | bytes 655392 | tf_op jit(solution)/shard_map/all_to_all | solution.py:380
  60.4 1.9 %collective-permute-start = (f32[1280,128]{1,0:T(8,128)S(1)}, f32[1280,128]{1,0:T(8,128)S(1)}, u32[]{:S(2)}, u32[]{:S(2)}) collective-permute-start(f32[1280,128]{1,0:T(8,128)S(1)} %bitcast.9), channel_id=1, source_target_pairs={{0,32},{32,0},{1,33},{33,1},{2,34},{34,2},{3,35},{35,3},{4,36},{36... | collective-permute-start | bytes 1966088 | tf_op jit(solution)/shard_map/ppermute | solution.py:417
  62.4 0.4 select_multiply_fusion.y_matrix_ref
  62.8 0.3 fusion.9
  63.1 1.4 collective-permute-done.other_ref
  64.4 0.0 copy-done.1
  64.4 0.0 copy-done
  64.4 1.7 %shard_map.65 = f32[2048,128]{1,0:T(8,128)S(1)} custom-call(f32[1280,128]{1,0:T(8,128)S(1)} %bitcast.10, f32[1280,128]{1,0:T(8,128)S(1)} %collective-permute-done.other_ref, bf16[1024,512]{1,0:T(8,128)(2,1)S(1)} %copy-done.1, bf16[1024,512]{1,0:T(8,128)(2,1)S(1)} %copy-done), custom_call_target="tpu_custom_call" | custom-call | tf_op jit(solution)/shard_map/pallas_call | solution.py:366
  66.1 72.0 %all_to_all.10 = f32[512,4,128]{2,1,0:T(4,128)S(1)} all-to-all(f32[512,4,128]{2,1,0:T(4,128)S(1)} %bitcast.7), channel_id=1, replica_groups={{402,403,404,405,406,407,408,409,410,411,412,413,414,415,384,385,386,38..., dimensions={0} | all-to-all | bytes 2097152 | tf_op jit(solution)/shard_map/all_to_all | solution.py:380
  138.2 2.0 %shard_map.66 = f32[2,16,64,128]{3,2,1,0:T(8,128)} custom-call(f32[2048,128]{1,0:T(8,128)S(1)} %bitcast.8, f32[128,128]{1,0:T(8,128)S(1)} %select_multiply_fusion.y_matrix_ref, f32[128,128]{1,0:T(8,128)S(1)} %get-tuple-element.17.cos_ref, f32[128,128]{1,0:T(8,128)S(1)} %get-tuple-element.18.sin_ref), custom_call_target="tpu_custom_call" | custom-call | tf_op jit(solution)/shard_map/pallas_call | solution.py:366
  (10 shorter events, 0.1 us)
Async XLA Ops:
  0.0 64.4 %copy-start.1 = (bf16[1024,512]{1,0:T(8,128)(2,1)S(1)}, bf16[1024,512]{1,0:T(8,128)(2,1)}, u32[]{:S(2)}) copy-start(bf16[1024,512]{1,0:T(8,128)(2,1)} %constant.140.clone.high_ref) | copy-start | bytes 3145732
  3.4 61.0 %copy-start = (bf16[1024,512]{1,0:T(8,128)(2,1)S(1)}, bf16[1024,512]{1,0:T(8,128)(2,1)}, u32[]{:S(2)}) copy-start(bf16[1024,512]{1,0:T(8,128)(2,1)} %constant.141.clone.low_ref) | copy-start | bytes 3145732
  3.4 57.0 %all-to-all-start = ((f32[256,1,640]{2,1,0:T(1,128)}), f32[256,1,640]{2,1,0:T(1,128)S(1)}, u32[]{:S(2)}, u32[]{:S(2)}) async-start(f32[256,1,640]{2,1,0:T(1,128)} %bitcast.11), calls=%async_computation | async-start | bytes 1310720 | tf_op jit(solution)/shard_map/all_to_all | solution.py:380
  60.4 4.0 %collective-permute-start = (f32[1280,128]{1,0:T(8,128)S(1)}, f32[1280,128]{1,0:T(8,128)S(1)}, u32[]{:S(2)}, u32[]{:S(2)}) collective-permute-start(f32[1280,128]{1,0:T(8,128)S(1)} %bitcast.9), channel_id=1, source_target_pairs={{0,32},{32,0},{1,33},{33,1},{2,34},{34,2},{3,35},{35,3},{4,36},{36... | collective-permute-start | bytes 1966088 | tf_op jit(solution)/shard_map/ppermute | solution.py:417

commit v14 on v13

--- a/solution.py
+++ b/solution.py
@@ -37,7 +37,7 @@
 ROWS = 5
 GROUP = 4
 FIRST_CHIP = 6
-FIRST_Y = 18
+FIRST_Y = 16
 PAIR = 2
 QUARTER = LX // 4
 
@@ -285,7 +285,9 @@
     for g in range(PLANES // PAIR):
         group = []
         for k in range(PAIR * g, PAIR * (g + 1)):
-            start = (k // 2) * 4 * LY + (k % 2) * LY
+            chip = (k // 2 + FIRST_CHIP) % (N_GX // 2)
+            half = (k % 2 + FIRST_Y // TEAMS) % 2
+            start = chip * 4 * LY + half * LY
             lines = [
                 turn(x_ref[pl.ds(start + kind, BLOCKS, stride=4), :], block, 1, kind & 1)
                 for kind in range(4)
@@ -321,7 +323,7 @@
 
 
 def device_tables():
-    dest = listed().ravel()
+    dest = np.arange(N_ALL)
     rev_p = np.array([reversal(i, 4) for i in range(N_GX)])
     rev_q = np.array([reversal(i, 5) for i in range(N_GY)])
     kx = rev_p[dest // N_GY][:, None]
@@ -373,10 +375,8 @@
     )(*args)
 
 
-def exchange(chunks, per_core):
-    order = listed()
-    groups = [order[:, c].ravel() for c in range(2)] if per_core else [order.ravel()]
-    groups = [[int(device) for device in group] for group in groups]
+def first_exchange(chunks):
+    groups = [[int(device) for device in listed()[:, c].ravel()] for c in range(2)]
     return lax.all_to_all(chunks, EVERYWHERE, 0, 0, axis_index_groups=groups, tiled=True)
 
 
@@ -406,7 +406,7 @@
         out_hbm=True,
         mib=60,
     )
-    chunks = exchange(chunks.reshape(N_CHIP, 1, ROWS * LX), per_core=True)
+    chunks = first_exchange(chunks.reshape(N_CHIP, 1, ROWS * LX))
     chunks, rp, rq = lax.optimization_barrier(
         (
             chunks.reshape(ROWS * N_CHIP, LX),
@@ -426,7 +426,7 @@
         jnp.asarray(low),
         scratch=[pltpu.VMEM((N_ALL, 2 * LX), F32)],
     )
-    back = exchange(modes.reshape(N_ALL, 4, LX), per_core=False)
+    back = lax.all_to_all(modes.reshape(N_ALL, 4, LX), EVERYWHERE, 0, 0, tiled=True)
     result = call(
         local_kernel,
         shape(2, PLANES, LY, LX),

time: 141 us -> 140 us (level)
  waiting for transfers between devices: 34.1 us -> 36.5 us
  blocking collectives: 72 us -> 70 us
    all_to_all x1, waiting for transfers between devices: 32.7 us -> 35.1 us  [first_exchange(): lax.all_to_all(chunks, EVERYWHERE, 0, 0, axis_index_groups=groups, tiled=...]
    all_to_all x1, blocking collectives: 72 us -> 70 us  [body(): lax.all_to_all(modes.reshape(N_ALL, 4, LX), EVERYWHERE, 0, 0, tiled=True)]
where the time goes in v14:
time: 140 us
  blocking collectives  70 us (50%)
  waiting for transfers between devices  36.5 us (26%)
  starting transfers between devices  25.4 us (18%)
  Pallas kernels  7.07 us (5%)
    all_to_all x1, blocking collectives, body(): lax.all_to_all(modes.reshape(N_ALL, 4, LX), EVERYWHERE, 0, 0, tiled=True)  70 us
    all_to_all x1, waiting for transfers between devices, first_exchange(): lax.all_to_all(chunks, EVERYWHERE, 0, 0, axis_index_groups=groups, tiled=...  35.1 us
    all_to_all x1, starting transfers between devices, first_exchange(): lax.all_to_all(chunks, EVERYWHERE, 0, 0, axis_index_groups=groups, tiled=...  23.5 us
    pallas_call x3, Pallas kernels, call(): pl.pallas_call(kernel, out_shape=outs, in_specs=[spec(in_hbm)] * len(args...  7.07 us
  transfers between devices with their start and end apart: 2, of which 2 were waited for; matrix products, arithmetic and copies ran while one was open for 1% of the time, Pallas kernels for 0%

profile of v14, /device:TPU:2, one launch (start us, length us, event | category | flops | bytes accessed | tf_op | source)
XLA Modules:
  0.0 139.9 jit_solution(16103353891728409820)
XLA Ops:
  0.0 0.0 copy-start.1
  0.0 3.4 %shard_map.64 = f32[1280,128]{1,0:T(8,128)} custom-call(f32[18,64,128]{2,1,0:T(8,128)} %now_hbm.1, f32[18,64,128]{2,1,0:T(8,128)} %prev_hbm.1, s32[18,64,128]{2,1,0:T(8,128)} %phase_hbm.1, f32[16,64,128]{2,1,0:T(8,128)} %div_hbm.1), custom_call_target="tpu_custom_call" | custom-call | tf_op jit(solution)/shard_map/pallas_call | solution.py:368
  3.4 0.0 copy-start
  3.4 23.5 %all-to-all-start = ((f32[256,1,640]{2,1,0:T(1,128)}), f32[256,1,640]{2,1,0:T(1,128)S(1)}, u32[]{:S(2)}, u32[]{:S(2)}) async-start(f32[256,1,640]{2,1,0:T(1,128)} %bitcast.11), calls=%async_computation | async-start | bytes 1310720 | tf_op jit(solution)/shard_map/all_to_all | solution.py:380
  27.0 35.1 %all-to-all-done = f32[256,1,640]{2,1,0:T(1,128)S(1)} async-done(((f32[256,1,640]{2,1,0:T(1,128)}), f32[256,1,640]{2,1,0:T(1,128)S(1)}, u32[]{:S(2)}, u32[]{:S(2)}) %all-to-all-start) | async-done | bytes 655392 | tf_op jit(solution)/shard_map/all_to_all | solution.py:380
  62.1 1.9 %collective-permute-start = (f32[1280,128]{1,0:T(8,128)S(1)}, f32[1280,128]{1,0:T(8,128)S(1)}, u32[]{:S(2)}, u32[]{:S(2)}) collective-permute-start(f32[1280,128]{1,0:T(8,128)S(1)} %bitcast.9), channel_id=1, source_target_pairs={{0,32},{32,0},{1,33},{33,1},{2,34},{34,2},{3,35},{35,3},{4,36},{36... | collective-permute-start | bytes 1966088 | tf_op jit(solution)/shard_map/ppermute | solution.py:417
  64.1 0.4 select_multiply_fusion.y_matrix_ref
  64.5 0.3 fusion.9
  64.8 1.4 collective-permute-done.other_ref
  66.1 0.0 copy-done.1
  66.1 0.0 copy-done
  66.1 1.7 %shard_map.65 = f32[2048,128]{1,0:T(8,128)S(1)} custom-call(f32[1280,128]{1,0:T(8,128)S(1)} %bitcast.10, f32[1280,128]{1,0:T(8,128)S(1)} %collective-permute-done.other_ref, bf16[1024,512]{1,0:T(8,128)(2,1)S(1)} %copy-done.1, bf16[1024,512]{1,0:T(8,128)(2,1)S(1)} %copy-done), custom_call_target="tpu_custom_call" | custom-call | tf_op jit(solution)/shard_map/pallas_call | solution.py:368
  67.8 70.0 %all_to_all.10 = f32[512,4,128]{2,1,0:T(4,128)S(1)} all-to-all(f32[512,4,128]{2,1,0:T(4,128)S(1)} %bitcast.7), channel_id=1, replica_groups=mesh['zh'=2,'x'=4,'c'=2,'zl'=8,'y'=4] {'zh','x','c','zl','y'}, dimensions={0} | all-to-all | bytes 2097152 | tf_op jit(solution)/shard_map/all_to_all | solution.py:429
  137.9 2.0 %shard_map.66 = f32[2,16,64,128]{3,2,1,0:T(8,128)} custom-call(f32[2048,128]{1,0:T(8,128)S(1)} %bitcast.8, f32[128,128]{1,0:T(8,128)S(1)} %select_multiply_fusion.y_matrix_ref, f32[128,128]{1,0:T(8,128)S(1)} %get-tuple-element.17.cos_ref, f32[128,128]{1,0:T(8,128)S(1)} %get-tuple-element.18.sin_ref), custom_call_target="tpu_custom_call" | custom-call | tf_op jit(solution)/shard_map/pallas_call | solution.py:368
  (10 shorter events, 0.1 us)
Async XLA Ops:
  0.0 66.1 %copy-start.1 = (bf16[1024,512]{1,0:T(8,128)(2,1)S(1)}, bf16[1024,512]{1,0:T(8,128)(2,1)}, u32[]{:S(2)}) copy-start(bf16[1024,512]{1,0:T(8,128)(2,1)} %constant.140.clone.high_ref) | copy-start | bytes 3145732
  3.4 62.7 %copy-start = (bf16[1024,512]{1,0:T(8,128)(2,1)S(1)}, bf16[1024,512]{1,0:T(8,128)(2,1)}, u32[]{:S(2)}) copy-start(bf16[1024,512]{1,0:T(8,128)(2,1)} %constant.141.clone.low_ref) | copy-start | bytes 3145732
  3.4 58.7 %all-to-all-start = ((f32[256,1,640]{2,1,0:T(1,128)}), f32[256,1,640]{2,1,0:T(1,128)S(1)}, u32[]{:S(2)}, u32[]{:S(2)}) async-start(f32[256,1,640]{2,1,0:T(1,128)} %bitcast.11), calls=%async_computation | async-start | bytes 1310720 | tf_op jit(solution)/shard_map/all_to_all | solution.py:380
  62.1 4.0 %collective-permute-start = (f32[1280,128]{1,0:T(8,128)S(1)}, f32[1280,128]{1,0:T(8,128)S(1)}, u32[]{:S(2)}, u32[]{:S(2)}) collective-permute-start(f32[1280,128]{1,0:T(8,128)S(1)} %bitcast.9), channel_id=1, source_target_pairs={{0,32},{32,0},{1,33},{33,1},{2,34},{34,2},{3,35},{35,3},{4,36},{36... | collective-permute-start | bytes 1966088 | tf_op jit(solution)/shard_map/ppermute | solution.py:417

commit v15 on v14

--- a/solution.py
+++ b/solution.py
@@ -36,7 +36,7 @@
 TEAMS = PLANES
 ROWS = 5
 GROUP = 4
-FIRST_CHIP = 6
+FIRST_CHIP = 7
 FIRST_Y = 16
 PAIR = 2
 QUARTER = LX // 4

time: 140 us -> 140 us (level)
  no operation moved by 1% of the time
where the time goes in v15:
time: 140 us
  blocking collectives  70 us (50%)
  waiting for transfers between devices  35.6 us (25%)
  starting transfers between devices  26 us (19%)
  Pallas kernels  7.06 us (5%)
    all_to_all x1, blocking collectives, body(): lax.all_to_all(modes.reshape(N_ALL, 4, LX), EVERYWHERE, 0, 0, tiled=True)  70 us
    all_to_all x1, waiting for transfers between devices, first_exchange(): lax.all_to_all(chunks, EVERYWHERE, 0, 0, axis_index_groups=groups, tiled=...  34.2 us
    all_to_all x1, starting transfers between devices, first_exchange(): lax.all_to_all(chunks, EVERYWHERE, 0, 0, axis_index_groups=groups, tiled=...  24.1 us
    pallas_call x3, Pallas kernels, call(): pl.pallas_call(kernel, out_shape=outs, in_specs=[spec(in_hbm)] * len(args...  7.06 us
  transfers between devices with their start and end apart: 2, of which 2 were waited for; matrix products, arithmetic and copies ran while one was open for 1% of the time, Pallas kernels for 0%

profile of v15, /device:TPU:2, one launch (start us, length us, event | category | flops | bytes accessed | tf_op | source)
XLA Modules:
  0.0 139.6 jit_solution(13094972277168456890)
XLA Ops:
  0.0 0.0 copy-start.1
  0.0 3.4 %shard_map.64 = f32[1280,128]{1,0:T(8,128)} custom-call(f32[18,64,128]{2,1,0:T(8,128)} %now_hbm.1, f32[18,64,128]{2,1,0:T(8,128)} %prev_hbm.1, s32[18,64,128]{2,1,0:T(8,128)} %phase_hbm.1, f32[16,64,128]{2,1,0:T(8,128)} %div_hbm.1), custom_call_target="tpu_custom_call" | custom-call | tf_op jit(solution)/shard_map/pallas_call | solution.py:368
  3.4 0.0 copy-start
  3.4 24.1 %all-to-all-start = ((f32[256,1,640]{2,1,0:T(1,128)}), f32[256,1,640]{2,1,0:T(1,128)S(1)}, u32[]{:S(2)}, u32[]{:S(2)}) async-start(f32[256,1,640]{2,1,0:T(1,128)} %bitcast.11), calls=%async_computation | async-start | bytes 1310720 | tf_op jit(solution)/shard_map/all_to_all | solution.py:380
  27.6 34.2 %all-to-all-done = f32[256,1,640]{2,1,0:T(1,128)S(1)} async-done(((f32[256,1,640]{2,1,0:T(1,128)}), f32[256,1,640]{2,1,0:T(1,128)S(1)}, u32[]{:S(2)}, u32[]{:S(2)}) %all-to-all-start) | async-done | bytes 655392 | tf_op jit(solution)/shard_map/all_to_all | solution.py:380
  61.9 1.9 %collective-permute-start = (f32[1280,128]{1,0:T(8,128)S(1)}, f32[1280,128]{1,0:T(8,128)S(1)}, u32[]{:S(2)}, u32[]{:S(2)}) collective-permute-start(f32[1280,128]{1,0:T(8,128)S(1)} %bitcast.9), channel_id=1, source_target_pairs={{0,32},{32,0},{1,33},{33,1},{2,34},{34,2},{3,35},{35,3},{4,36},{36... | collective-permute-start | bytes 1966088 | tf_op jit(solution)/shard_map/ppermute | solution.py:417
  63.8 0.4 select_multiply_fusion.y_matrix_ref
  64.2 0.3 fusion.9
  64.5 1.4 collective-permute-done.other_ref
  65.8 0.0 copy-done.1
  65.8 0.0 copy-done
  65.8 1.7 %shard_map.65 = f32[2048,128]{1,0:T(8,128)S(1)} custom-call(f32[1280,128]{1,0:T(8,128)S(1)} %bitcast.10, f32[1280,128]{1,0:T(8,128)S(1)} %collective-permute-done.other_ref, bf16[1024,512]{1,0:T(8,128)(2,1)S(1)} %copy-done.1, bf16[1024,512]{1,0:T(8,128)(2,1)S(1)} %copy-done), custom_call_target="tpu_custom_call" | custom-call | tf_op jit(solution)/shard_map/pallas_call | solution.py:368
  67.6 70.0 %all_to_all.10 = f32[512,4,128]{2,1,0:T(4,128)S(1)} all-to-all(f32[512,4,128]{2,1,0:T(4,128)S(1)} %bitcast.7), channel_id=1, replica_groups=mesh['zh'=2,'x'=4,'c'=2,'zl'=8,'y'=4] {'zh','x','c','zl','y'}, dimensions={0} | all-to-all | bytes 2097152 | tf_op jit(solution)/shard_map/all_to_all | solution.py:429
  137.6 2.0 %shard_map.66 = f32[2,16,64,128]{3,2,1,0:T(8,128)} custom-call(f32[2048,128]{1,0:T(8,128)S(1)} %bitcast.8, f32[128,128]{1,0:T(8,128)S(1)} %select_multiply_fusion.y_matrix_ref, f32[128,128]{1,0:T(8,128)S(1)} %get-tuple-element.17.cos_ref, f32[128,128]{1,0:T(8,128)S(1)} %get-tuple-element.18.sin_ref), custom_call_target="tpu_custom_call" | custom-call | tf_op jit(solution)/shard_map/pallas_call | solution.py:368
  (10 shorter events, 0.1 us)
Async XLA Ops:
  0.0 65.8 %copy-start.1 = (bf16[1024,512]{1,0:T(8,128)(2,1)S(1)}, bf16[1024,512]{1,0:T(8,128)(2,1)}, u32[]{:S(2)}) copy-start(bf16[1024,512]{1,0:T(8,128)(2,1)} %constant.140.clone.high_ref) | copy-start | bytes 3145732
  3.4 62.5 %copy-start = (bf16[1024,512]{1,0:T(8,128)(2,1)S(1)}, bf16[1024,512]{1,0:T(8,128)(2,1)}, u32[]{:S(2)}) copy-start(bf16[1024,512]{1,0:T(8,128)(2,1)} %constant.141.clone.low_ref) | copy-start | bytes 3145732
  3.4 58.5 %all-to-all-start = ((f32[256,1,640]{2,1,0:T(1,128)}), f32[256,1,640]{2,1,0:T(1,128)S(1)}, u32[]{:S(2)}, u32[]{:S(2)}) async-start(f32[256,1,640]{2,1,0:T(1,128)} %bitcast.11), calls=%async_computation | async-start | bytes 1310720 | tf_op jit(solution)/shard_map/all_to_all | solution.py:380
  61.9 4.0 %collective-permute-start = (f32[1280,128]{1,0:T(8,128)S(1)}, f32[1280,128]{1,0:T(8,128)S(1)}, u32[]{:S(2)}, u32[]{:S(2)}) collective-permute-start(f32[1280,128]{1,0:T(8,128)S(1)} %bitcast.9), channel_id=1, source_target_pairs={{0,32},{32,0},{1,33},{33,1},{2,34},{34,2},{3,35},{35,3},{4,36},{36... | collective-permute-start | bytes 1966088 | tf_op jit(solution)/shard_map/ppermute | solution.py:417
